TPU v7x, 32 devices: a whole 2x2x4 slice. The times are simulated.
32 devices in a mesh: layer: 4 (over y, x), feat: 8 (over z, core).
Axes of the slice: x: 2, y: 2, z: 4, core: 2. Of those that a mesh axis runs over, the one named last changes fastest.
Arguments:
- residuals: bfloat16 [256, 4096], P('feat', 'layer'), may hold values from -6 to 6
- errors: bfloat16 [256, 4096], P('feat', 'layer'), may hold values from -0.375 to 0.375
- enc_weight: bfloat16 [4096, 65536], P('layer', 'feat'), may hold values from -0.09375 to 0.09375
- dec_weight: bfloat16 [4096, 65536], P('layer', 'feat'), may hold values from -0.09375 to 0.09375
- enc_bias: float32 [65536], P('feat'), may hold values from -3 to 3
Outputs:
- enc_grad: bfloat16 [4096, 65536], P('layer', 'feat')
- dec_grad: bfloat16 [4096, 65536], P('layer', 'feat')
- bias_grad: float32 [65536], P('feat')
All inputs are finite; a program needn't handle non-finite values.
Results may differ from a plain program's by a relative error of at most 0.0055.
Values may be sent and summed in bfloat16 or wider, within the bound.
No kernel may reach another device: no remote copies, remote signals or barrier semaphores. Data moves between devices by JAX's collectives and lax.ppermute only.
A program may use at most 128 MiB of HBM per device.

v0:
```python
import jax
import jax.numpy as jnp
from jax import lax
from jax.sharding import PartitionSpec as P


def transposed(left, right):
    return lax.dot_general(
        left, right, (((0,), (0,)), ((), ())), preferred_element_type=jnp.float32
    )


def gate_values(preact, code_grad):
    code = (jax.nn.softplus(4.0 * preact) / 4.0).astype(jnp.bfloat16)
    masked = (code_grad * jax.nn.sigmoid(4.0 * preact)).astype(jnp.bfloat16)
    return (code, masked)


def per_device(residuals, errors, enc_weight, dec_weight, enc_bias):
    all_resid, all_errors = (
        lax.all_gather(residuals, "feat", axis=0, tiled=True),
        lax.all_gather(errors, "feat", axis=0, tiled=True),
    )
    resid_block = all_resid
    error_block = all_errors
    first = jnp.dot(resid_block, enc_weight, preferred_element_type=jnp.float32)
    second = jnp.dot(error_block, dec_weight, preferred_element_type=jnp.float32)
    summed = lax.psum_scatter(
        jnp.stack([first, second], axis=1), "layer", scatter_dimension=0, tiled=True
    )
    code, masked = gate_values(summed[:, 0] + enc_bias, summed[:, 1])
    bias_grad = lax.psum(jnp.sum(masked.astype(jnp.float32), axis=0), "layer")
    code_piece = lax.all_gather(code, "layer", axis=0, tiled=True)
    masked_piece = lax.all_gather(masked, "layer", axis=0, tiled=True)
    resid_block = all_resid
    error_block = all_errors
    enc_grad = transposed(resid_block, masked_piece)
    dec_grad = transposed(error_block, code_piece)
    return (enc_grad.astype(jnp.bfloat16), dec_grad.astype(jnp.bfloat16), bias_grad)


def solution(mesh):
    placed = (
        P("feat", "layer"),
        P("feat", "layer"),
        P("layer", "feat"),
        P("layer", "feat"),
        P("feat"),
    )
    return jax.shard_map(
        per_device,
        mesh=mesh,
        in_specs=placed,
        out_specs=(P("layer", "feat"), P("layer", "feat"), P("feat")),
        check_vma=False,
    )
```

profile of v0, /device:TPU:0, one launch (start us, length us, event | category | flops | bytes accessed | tf_op | source)
XLA Modules:
  0.0 368.3 jit_solution(15539636367751443985)
XLA Ops:
  7.2 0.0 reduce-scatter.2.cloned.1.call-start
  7.2 16.8 %all_gather.12 = bf16[256,1024]{1,0:T(8,128)(2,1)S(1)} all-gather(bf16[32,1024]{1,0:T(8,128)(2,1)} %param.5), channel_id=1, replica_groups=mesh['layer'=4,'feat'=8] {'feat'}, dimensions={0}, use_global_device_ids=true | all-gather | bytes 589824 | tf_op jit(solution)/shard_map/all_gather | solution.py:21
  24.0 14.9 %all_gather.13 = bf16[256,1024]{1,0:T(8,128)(2,1)S(1)} all-gather(bf16[32,1024]{1,0:T(8,128)(2,1)} %param.6), channel_id=1, replica_groups=mesh['layer'=4,'feat'=8] {'feat'}, dimensions={0}, use_global_device_ids=true | all-gather | bytes 589824 | tf_op jit(solution)/shard_map/all_gather | solution.py:22
  38.9 8.1 %convolution_bitcast_fusion = f32[256,1,8192]{2,0,1:T(8,128)S(1)} fusion(bf16[256,1024]{1,0:T(8,128)(2,1)S(1)} %all_gather.13, bf16[1024,8192]{1,0:T(8,128)(2,1)} %param.8), kind=kOutput, calls=%fused_computation.3 | convolution fusion | flops 4294967296 | bytes 25690112 | tf_op jit(solution)/shard_map/dot_general | solution.py:27
  47.1 8.1 %convolution_bitcast_fusion.1 = f32[256,1,8192]{2,0,1:T(8,128)S(1)} fusion(bf16[256,1024]{1,0:T(8,128)(2,1)S(1)} %all_gather.12, bf16[1024,8192]{1,0:T(8,128)(2,1)} %param.7), kind=kOutput, calls=%fused_computation.4 | convolution fusion | flops 4294967296 | bytes 25690112 | tf_op jit(solution)/shard_map/dot_general | solution.py:26
  55.2 6.3 %pad_maximum_fusion = f32[256,2,8192]{2,0,1:T(8,128)} fusion(f32[256,1,8192]{2,0,1:T(8,128)S(1)} %convolution_bitcast_fusion, f32[256,1,8192]{2,0,1:T(8,128)S(1)} %convolution_bitcast_fusion.1), kind=kLoop, calls=%fused_computation | loop fusion | flops 4194304 | bytes 33554432 | tf_op jit(solution)/shard_map/stack | solution.py:29
  61.5 0.0 copy-start
  61.5 0.0 reduce-scatter.2.cloned.1.call-update
  61.6 0.0 all-gather.5.cloned.1.call-start
  61.6 155.4 %reduce-scatter.2.cloned.1.call-done = f32[64,2,8192]{2,0,1:T(8,128)} async-done(((f32[256,2,8192]{2,0,1:T(8,128)}), f32[64,2,8192]{2,0,1:T(8,128)}) %reduce-scatter.2.cloned.1.call-update) | async-done | bytes 4194320 | tf_op jit(solution)/shard_map/reduce_scatter | solution.py:28
  217.0 0.0 copy-done
  217.0 5.4 %convert_reduce_fusion = (f32[8192]{0:T(1024)S(1)}, bf16[64,8192]{1,0:T(8,128)(2,1)}, bf16[64,8192]{1,0:T(8,128)(2,1)}) fusion(f32[8192]{0:T(1024)S(1)} %copy-done, f32[64,2,8192]{2,0,1:T(8,128)} %reduce-scatter.2.cloned.1.call-done), kind=kLoop, calls=%fused_computation.14 | loop fusion | flops 8904704 | bytes 6356992 | tf_op jit(solution)/shard_map/reduce_sum | solution.py:32
  222.4 0.0 all-gather.5.cloned.1.call-update
  222.4 0.0 all-gather.3.cloned.1.call-start
  222.5 0.7 all-gather.3.cloned.1.call-update
  223.2 16.3 %psum.7 = f32[8192]{0:T(1024)} all-reduce(f32[8192]{0:T(1024)S(1)} %get-tuple-element.6), channel_id=1, replica_groups=mesh['layer'=4,'feat'=8] {'layer'}, use_global_device_ids=true, to_apply=%region_2.3 | all-reduce | flops 8192 | bytes 65536 | tf_op jit(solution)/shard_map/psum | solution.py:32
  239.5 35.9 %all-gather.5.cloned.1.call-done = bf16[256,8192]{1,0:T(8,128)(2,1)} async-done(((bf16[64,8192]{1,0:T(8,128)(2,1)}), bf16[256,8192]{1,0:T(8,128)(2,1)}) %all-gather.5.cloned.1.call-update) | async-done | bytes 4194320 | tf_op jit(solution)/shard_map/all_gather | solution.py:33
  275.5 10.8 %convert_bitcast_fusion = bf16[1024,8192]{0,1:T(8,128)(2,1)} fusion(bf16[256,8192]{1,0:T(8,128)(2,1)} %all-gather.5.cloned.1.call-done, bf16[256,1024]{1,0:T(8,128)(2,1)S(1)} %all_gather.13), kind=kOutput, calls=%fused_computation.1 | convolution fusion | flops 4303355904 | bytes 21495808 | tf_op jit(solution)/shard_map/dot_general | solution.py:8
  286.3 21.5 %copy.9 = bf16[1024,8192]{1,0:T(8,128)(2,1)} copy(bf16[1024,8192]{0,1:T(8,128)(2,1)} %convert_bitcast_fusion) | data formatting | bytes 33554432
  307.8 22.2 %all-gather.3.cloned.1.call-done = bf16[256,8192]{1,0:T(8,128)(2,1)} async-done(((bf16[64,8192]{1,0:T(8,128)(2,1)}), bf16[256,8192]{1,0:T(8,128)(2,1)}) %all-gather.3.cloned.1.call-update) | async-done | bytes 4194320 | tf_op jit(solution)/shard_map/all_gather | solution.py:34
  330.1 10.5 %convert_bitcast_fusion.1 = bf16[1024,8192]{0,1:T(8,128)(2,1)} fusion(bf16[256,8192]{1,0:T(8,128)(2,1)} %all-gather.3.cloned.1.call-done, bf16[256,1024]{1,0:T(8,128)(2,1)S(1)} %all_gather.12), kind=kOutput, calls=%fused_computation.2 | convolution fusion | flops 4303355904 | bytes 21495808 | tf_op jit(solution)/shard_map/dot_general | solution.py:8
  340.5 21.2 %copy.8 = bf16[1024,8192]{1,0:T(8,128)(2,1)} copy(bf16[1024,8192]{0,1:T(8,128)(2,1)} %convert_bitcast_fusion.1) | data formatting | bytes 33554432
Async XLA Ops:
  7.2 209.8 %reduce-scatter.2.cloned.1.call-start = ((), (), s32[]{:S(2)}) async-start(), calls=%async_computation.1 | async-start | bytes 20971520 | tf_op jit(solution)/shard_map/reduce_scatter | solution.py:28
  61.5 155.4 %copy-start = (f32[8192]{0:T(1024)S(1)}, f32[8192]{0:T(1024)}, u32[]{:S(2)}) copy-start(f32[8192]{0:T(1024)} %param.9) | copy-start | bytes 98308
  61.6 213.9 %all-gather.5.cloned.1.call-start = ((), (), s32[]{:S(2)}) async-start(), calls=%async_computation.3 | async-start | bytes 5242880 | tf_op jit(solution)/shard_map/all_gather | solution.py:33
  222.4 107.6 %all-gather.3.cloned.1.call-start = ((), (), s32[]{:S(2)}) async-start(), calls=%async_computation.2 | async-start | bytes 5242880 | tf_op jit(solution)/shard_map/all_gather | solution.py:34
Sparse Core Ops, SparseCore 0:
  61.7 155.2 reduce-scatter.1
  222.6 52.8 all-gather.4
  277.3 52.6 all-gather.2
where the time goes:
time: 370 us; the launch traced here: 368 us
  waiting for transfers between devices  214 us (58%)
  blocking collectives  48.1 us (13%)
  local copies, waits for them, and re-layouts  42.7 us (12%)
  matrix products  37.6 us (10%)
  between operations  13.8 us (4%)
  other arithmetic  11.8 us (3%)
    reduce_scatter x1, waiting for transfers between devices, per_device(): lax.psum_scatter(jnp.stack([first, second], axis=1), 'layer', scatter_dim...  155 us
    unnamed x4, local copies, waits for them, and re-layouts  42.7 us
    all_gather x1, waiting for transfers between devices, per_device(): code_piece = lax.all_gather(code, 'layer', axis=0, tiled=True)  35.9 us
    all_gather x1, waiting for transfers between devices, per_device(): masked_piece = lax.all_gather(masked, 'layer', axis=0, tiled=True)  22.2 us
    dot_general x2, matrix products, transposed(): lax.dot_general(left, right, (((0,), (0,)), ((), ())), preferred_element_...  21.3 us
    all_gather x1, blocking collectives, per_device(): lax.all_gather(residuals, 'feat', axis=0, tiled=True)  16.8 us
    psum x1, blocking collectives, per_device(): bias_grad = lax.psum(jnp.sum(masked.astype(jnp.float32), axis=0), 'layer')  16.3 us
    all_gather x1, blocking collectives, per_device(): lax.all_gather(errors, 'feat', axis=0, tiled=True)  14.9 us
  transfers between devices with their start and end apart: 3, of which 3 were waited for; matrix products, arithmetic and copies ran while one was open for 9% of the time, Pallas kernels for 0%

commit v1 on v0

v1 whole, which is shorter than its diff:
```python
import functools

import jax
import jax.numpy as jnp
from jax import lax
from jax.experimental import pallas as pl
from jax.experimental.pallas import tpu as pltpu
from jax.sharding import PartitionSpec as P

BF16 = jnp.bfloat16
F32 = jnp.float32
VMEM_LIMIT = 48 * 2**20


def params():
    return pltpu.CompilerParams(vmem_limit_bytes=VMEM_LIMIT)


def tree_sum(parts):
    while len(parts) > 1:
        parts = [parts[i] + parts[i + 1] for i in range(0, len(parts), 2)]
    return parts[0]


def divisor(extent, most):
    size = min(extent, most)
    while extent % size:
        size -= 128
    return size


class Plan:
    def __init__(self, layers, peers, rows, stack, feats):
        self.layers, self.peers, self.rows = layers, peers, rows
        self.stack, self.feats = stack, feats
        self.bits = layers.bit_length() - 1
        self.blocks = 1 << max(self.bits - 1, 0)
        order = list(range(self.bits))
        self.orders = (order[::-1], order)
        near = 2
        while near < peers and (near * rows) % (32 * self.blocks):
            near *= 2
        self.near = min(near, peers)

    def keys(self):
        me = lax.axis_index("layer")
        out = []
        for order in self.orders:
            key = 0
            for level, bit in enumerate(order[:-1]):
                key = key + (((me >> bit) & 1) << (self.bits - 2 - level))
            out.append(key)
        return out

    def swap(self, array, bit):
        pairs = [(i, i ^ (1 << bit)) for i in range(self.layers)]
        return lax.ppermute(array, "layer", pairs)

    def peer(self, array, distance):
        pairs = [(i, i ^ distance) for i in range(self.peers)]
        return lax.ppermute(array, "feat", pairs)


def place_rows(plan, raws, store):
    keys = plan.keys()
    tokens = len(raws) * plan.rows
    half = tokens // 2
    block = half // plan.blocks
    step = 16
    for start in range(0, tokens, step):
        stream, within = divmod(start, half)
        index, off = divmod(within, block)
        row = stream * half + (index ^ keys[stream]) * block + off
        row = pl.multiple_of(row, step)
        piece, at = divmod(start, plan.rows)
        for q in range(2):
            store(q, row, raws[piece][q, at : at + step, :])


def partial_kernel(plan, count, *refs):
    raws, (enc_ref, dec_ref), outs, (tokens_ref,) = (
        refs[:count],
        refs[count : count + 2],
        refs[count + 2 : -1],
        refs[-1:],
    )

    @pl.when(pl.program_id(0) == 0)
    def _():
        def store(q, row, values):
            tokens_ref[q, pl.ds(row, 16), :] = values

        place_rows(plan, raws, store)

    rows = outs[0].shape[1]
    for q, weight in enumerate((enc_ref, dec_ref)):
        part = jnp.dot(tokens_ref[q], weight[...], preferred_element_type=F32)
        for i, out in enumerate(outs):
            out[q] = part[i * rows : (i + 1) * rows].astype(BF16)


def partials(plan, raws, enc_weight, dec_weight, first, width):
    tokens = len(raws) * plan.rows
    outs = 4 if plan.blocks > 1 else 2
    block = divisor(width, 512)
    base = first // block
    weight = pl.BlockSpec((plan.stack, block), lambda i: (0, base + i))
    raw = pl.BlockSpec((2, plan.rows, plan.stack), lambda i: (0, 0, 0))
    out = pl.BlockSpec((2, tokens // outs, block), lambda i: (0, 0, i))
    return pl.pallas_call(
        functools.partial(partial_kernel, plan, len(raws)),
        grid=(width // block,),
        in_specs=[raw] * len(raws) + [weight] * 2,
        out_specs=[out] * outs,
        out_shape=[jax.ShapeDtypeStruct((2, tokens // outs, width), BF16)] * outs,
        scratch_shapes=[pltpu.VMEM((2, tokens, plan.stack), BF16)],
        compiler_params=params(),
        name="partials",
    )(*raws, enc_weight, dec_weight)


def add_kernel(pieces, *refs):
    outs = refs[4:]
    for stream in range(2):
        total = refs[2 * stream][...].astype(F32) + refs[2 * stream + 1][...].astype(F32)
        rows = total.shape[1] // pieces
        for i in range(pieces):
            outs[stream * pieces + i][...] = total[:, i * rows : (i + 1) * rows].astype(BF16)


def add(plan, kept, got, pieces):
    _, rows, width = kept[0].shape
    block = divisor(width, 1024)
    whole = pl.BlockSpec((2, rows, block), lambda i: (0, 0, i))
    part = pl.BlockSpec((2, rows // pieces, block), lambda i: (0, 0, i))
    return pl.pallas_call(
        functools.partial(add_kernel, pieces),
        grid=(width // block,),
        in_specs=[whole] * 4,
        out_specs=[part] * (2 * pieces),
        out_shape=[jax.ShapeDtypeStruct((2, rows // pieces, width), BF16)] * (2 * pieces),
        compiler_params=params(),
        name="add",
    )(kept[0], got[0], kept[1], got[1])


def gate_kernel(*refs):
    bias = refs[4][...]
    for stream in range(2):
        mine, other = refs[2 * stream], refs[2 * stream + 1]
        scaled = 4.0 * (mine[0].astype(F32) + other[0].astype(F32) + bias)
        code_grad = mine[1].astype(F32) + other[1].astype(F32)
        small = jnp.exp(-jnp.abs(scaled))
        code = 0.25 * (jnp.maximum(scaled, 0.0) + jnp.log1p(small))
        gate = jnp.where(scaled >= 0.0, 1.0, small) / (1.0 + small)
        refs[5 + stream][0] = code.astype(BF16)
        refs[5 + stream][1] = (code_grad * gate).astype(BF16)


def gate(plan, mine, other, bias, first):
    _, rows, width = mine[0].shape
    block = divisor(width, 1024)
    base = first // block
    whole = pl.BlockSpec((2, rows, block), lambda i: (0, 0, i))
    return pl.pallas_call(
        gate_kernel,
        grid=(width // block,),
        in_specs=[whole] * 4 + [pl.BlockSpec((1, block), lambda i: (0, base + i))],
        out_specs=[whole] * 2,
        out_shape=[jax.ShapeDtypeStruct((2, rows, width), BF16)] * 2,
        compiler_params=params(),
        name="gate",
    )(mine[0], other[0], mine[1], other[1], bias)


def turn_kernel(plan, counts, *refs):
    raws, outs, scratch = refs[: sum(counts)], refs[sum(counts) : -1], refs[-1]
    done = 0
    for group, count in enumerate(counts):
        base = done * plan.rows

        def store(q, row, values):
            scratch[q, pl.ds(pl.multiple_of(base + row, 16), 16), :] = values

        place_rows(plan, raws[done : done + count], store)
        done += count
    for q in range(2):
        outs[q][...] = scratch[q].T


def turned(plan, groups):
    counts = [len(group) for group in groups]
    raws = [raw for group in groups for raw in group]
    tokens = len(raws) * plan.rows
    return pl.pallas_call(
        functools.partial(turn_kernel, plan, counts),
        out_shape=[jax.ShapeDtypeStruct((plan.stack, tokens), BF16)] * 2,
        scratch_shapes=[pltpu.VMEM((2, tokens, plan.stack), BF16)],
        compiler_params=params(),
        name="turned",
    )(*raws)


def grads_kernel(sizes, count, aliased, *refs):
    resid_ref, error_ref = refs[:2]
    parts = refs[2 : 2 + count]
    enc_ref, dec_ref, bias_ref, code_ref, masked_ref = refs[2 + count + aliased :]
    row = 0
    at = 0
    sums = []
    for size in sizes:
        blocks = []
        for part in parts[at : at + size]:
            rows = part.shape[1]
            code_ref[row : row + rows] = part[0]
            masked_ref[row : row + rows] = part[1]
            blocks.append(jnp.sum(part[1].astype(F32), axis=0, keepdims=True))
            row += rows
        at += size
        sums.append(tree_sum(blocks))
    total = sums[0]
    for value in sums[1:]:
        total = total + value
    bias_ref[...] = total
    enc_ref[...] = jnp.dot(resid_ref[...], masked_ref[...], preferred_element_type=F32).astype(BF16)
    dec_ref[...] = jnp.dot(error_ref[...], code_ref[...], preferred_element_type=F32).astype(BF16)


def grads(plan, turned_tokens, holdings, first, width, before):
    tokens = turned_tokens[0].shape[1]
    block = divisor(width, 512)
    base = first // block
    parts, specs, sizes = [], [], []
    for arrays, origin in holdings:
        sizes.append(len(arrays))
        skip = (first - origin) // block
        for array in arrays:
            parts.append(array)
            specs.append(
                pl.BlockSpec((2, array.shape[1], block), lambda i, skip=skip: (0, 0, skip + i))
            )
    whole = pl.BlockSpec((plan.stack, tokens), lambda i: (0, 0))
    aliased = [] if before is None else list(before)
    shapes = [
        jax.ShapeDtypeStruct((plan.stack, plan.feats), BF16),
        jax.ShapeDtypeStruct((plan.stack, plan.feats), BF16),
        jax.ShapeDtypeStruct((1, plan.feats), F32),
    ]
    return pl.pallas_call(
        functools.partial(grads_kernel, sizes, len(parts), len(aliased)),
        grid=(width // block,),
        in_specs=[whole] * 2 + specs + [pl.BlockSpec(memory_space=pl.ANY)] * len(aliased),
        out_specs=[
            pl.BlockSpec((plan.stack, block), lambda i: (0, base + i)),
            pl.BlockSpec((plan.stack, block), lambda i: (0, base + i)),
            pl.BlockSpec((1, block), lambda i: (0, base + i)),
        ],
        out_shape=shapes,
        scratch_shapes=[pltpu.VMEM((tokens, block), BF16)] * 2,
        input_output_aliases={2 + len(parts) + i: i for i in range(len(aliased))},
        compiler_params=params(),
        name="grads",
    )(*turned_tokens, *parts, *aliased)


def reduce_gate_gather(plan, outs, bias, first):
    if plan.blocks > 1:
        kept, sent = [outs[0], outs[2]], [outs[1], outs[3]]
    else:
        kept = list(outs)
    levels = plan.bits - 1
    for level in range(levels):
        got = [plan.swap(sent[s], plan.orders[s][level]) for s in range(2)]
        pieces = 2 if level < levels - 1 else 1
        cut = add(plan, kept, got, pieces)
        if pieces == 2:
            kept, sent = [cut[0], cut[2]], [cut[1], cut[3]]
        else:
            kept = list(cut)
    other = [plan.swap(kept[s], plan.orders[s][-1]) for s in range(2)]
    gated = gate(plan, kept, other, bias, first)
    held = [[gated[0]], [gated[1]]]
    for level in reversed(range(levels)):
        for s in range(2):
            held[s] = held[s] + [plan.swap(a, plan.orders[s][level]) for a in held[s]]
    return held


def per_device(plan, residuals, errors, enc_weight, dec_weight, enc_bias):
    feats = plan.feats
    bias = enc_bias.reshape(1, feats)
    own = jnp.stack([residuals, errors])
    near = [own] + [plan.peer(own, m) for m in range(1, plan.near)]
    far = []
    for m in range(plan.near, plan.peers, 2):
        came = plan.peer(own, m)
        far += [came, plan.peer(came, 1)]
    quarter = feats // 4
    near_cuts = [(0, quarter), (quarter, feats - quarter)]
    far_cuts = [(i * quarter, quarter) for i in range(4)]

    near_held = []
    for first, width in near_cuts:
        outs = partials(plan, near, enc_weight, dec_weight, first, width)
        near_held.append((first, width, reduce_gate_gather(plan, outs, bias, first)))
    flipped = turned(plan, [near, far] if far else [near])
    result = None
    for first, width in far_cuts:
        holdings = []
        for start, extent, held in near_held:
            if start <= first < start + extent:
                holdings += [(held[0], start), (held[1], start)]
        if far:
            outs = partials(plan, far, enc_weight, dec_weight, first, width)
            held = reduce_gate_gather(plan, outs, bias, first)
            holdings += [(held[0], first), (held[1], first)]
        result = grads(plan, flipped, holdings, first, width, result)
    enc_grad, dec_grad, bias_grad = result
    return enc_grad, dec_grad, bias_grad.reshape(feats)


def solution(mesh):
    placed = (
        P("feat", "layer"),
        P("feat", "layer"),
        P("layer", "feat"),
        P("layer", "feat"),
        P("feat"),
    )
    layers, peers = mesh.shape["layer"], mesh.shape["feat"]

    def body(residuals, errors, enc_weight, dec_weight, enc_bias):
        plan = Plan(layers, peers, residuals.shape[0], residuals.shape[1], enc_bias.shape[0])
        return per_device(plan, residuals, errors, enc_weight, dec_weight, enc_bias)

    return jax.shard_map(
        body,
        mesh=mesh,
        in_specs=placed,
        out_specs=(P("layer", "feat"), P("layer", "feat"), P("feat")),
        check_vma=False,
    )
```

time: 370 us -> 176 us (0.48)
  waiting for transfers between devices: 214 us -> 63.2 us
  Pallas kernels: 0 us -> 67.5 us
  blocking collectives: 48.1 us -> 0 us
  starting transfers between devices: 0.12 us -> 43.4 us
  local copies, waits for them, and re-layouts: 42.7 us -> 0.01 us
  matrix products: 37.6 us -> 0 us
  between operations: 13.8 us -> 0.87 us
  other arithmetic: 11.8 us -> 0.89 us
    reduce_scatter x1 -> x0, waiting for transfers between devices: 155 us -> none  [per_device(): lax.psum_scatter(jnp.stack([first, second], axis=1), 'layer', scatter_dim...]
    pallas_call x0 -> x23, Pallas kernels: none -> 67.5 us  [the longest x6 39.8 us: partials(): pl.pallas_call(functools.partial(partial_kernel, plan, len(raws)), grid=(...]
    ppermute x0 -> x43, waiting for transfers between devices: none -> 63.2 us  [the longest x36 62.2 us: swap(): return lax.ppermute(array, 'layer', pairs)]
    all_gather x2 -> x0, waiting for transfers between devices: 58.2 us -> none  [the longest x1 35.9 us: per_device(): code_piece = lax.all_gather(code, 'layer', axis=0, tiled=True)]
    ppermute x0 -> x43, starting transfers between devices: none -> 43.4 us  [the longest x36 37.9 us: swap(): return lax.ppermute(array, 'layer', pairs)]
    unnamed x4 -> x2, local copies, waits for them, and re-layouts: 42.7 us -> 0.01 us
    dot_general x4 -> x0, matrix products: 37.6 us -> none  [the longest x2 21.3 us: transposed(): lax.dot_general(left, right, (((0,), (0,)), ((), ())), preferred_element_...]
    all_gather x2 -> x0, blocking collectives: 31.7 us -> none  [the longest x1 16.8 us: per_device(): lax.all_gather(residuals, 'feat', axis=0, tiled=True)]
  transfers between devices with their start and end apart: 3 -> 43, of which waited for: 3 -> 11; matrix products, arithmetic and copies ran while one was open for 9% -> 0% of each run, Pallas kernels for 0% -> 33%
where the time goes in v1:
time: 176 us
  Pallas kernels  67.5 us (38%)
  waiting for transfers between devices  63.2 us (36%)
  starting transfers between devices  43.4 us (25%)
    ppermute x36, waiting for transfers between devices, swap(): return lax.ppermute(array, 'layer', pairs)  62.2 us
    pallas_call x6, Pallas kernels, partials(): pl.pallas_call(functools.partial(partial_kernel, plan, len(raws)), grid=(...  39.8 us
    ppermute x36, starting transfers between devices, swap(): return lax.ppermute(array, 'layer', pairs)  37.9 us
    pallas_call x4, Pallas kernels, grads(): pl.pallas_call(functools.partial(grads_kernel, sizes, len(parts), len(ali...  19.5 us
    pallas_call x6, Pallas kernels, gate(): pl.pallas_call(gate_kernel, grid=(width // block,), in_specs=[whole] * 4...  5.63 us
    ppermute x7, starting transfers between devices, peer(): return lax.ppermute(array, 'feat', pairs)  5.48 us
  transfers between devices with their start and end apart: 43, of which 11 were waited for; matrix products, arithmetic and copies ran while one was open for 0% of the time, Pallas kernels for 33%

profile of v1, /device:TPU:0, one launch (start us, length us, event | category | flops | bytes accessed | tf_op | source)
XLA Modules:
  0.0 175.9 jit_solution(6743934296076701203)
XLA Ops:
  3.0 4.9 %partials.10 = (bf16[2,16,2048]{2,1,0:T(8,128)(2,1)S(1)}, bf16[2,16,2048]{2,1,0:T(8,128)(2,1)S(1)}, bf16[2,16,2048]{2,1,0:T(8,128)(2,1)S(1)}, bf16[2,16,2048]{2,1,0:T(8,128)(2,1)S(1)}) custom-call(bf16[2,32,1024]{2,1,0:T(8,128)(2,1)S(1)} %pad_maximum_fusion.refs_0_, bf16[2,32,1024]{2,1,0:T(8,128)(2,1)S(1)} %collective-permute-done.refs_1_, ...), custom_call_target="tpu_custom_call" | custom-call | tf_op jit(solution)/shard_map/partials/pallas_call | solution.py:110
  8.0 2.9 %collective-permute-start.31 = (bf16[2,16,2048]{2,1,0:T(8,128)(2,1)S(1)}, bf16[2,16,2048]{2,1,0:T(8,128)(2,1)S(1)}, u32[]{:S(2)}, u32[]{:S(2)}) collective-permute-start(bf16[2,16,2048]{2,1,0:T(8,128)(2,1)S(1)} %get-tuple-element.100), channel_id=1, source_target_pairs={{0,16},{8,24},{16,0},{24,8},{1,17},{9,25},{17,1},{25,9},{2,18},{10... | collective-permute-start | bytes 393224 | tf_op jit(solution)/shard_map/ppermute | solution.py:57
  10.9 1.5 collective-permute-start.32
  12.4 1.6 collective-permute-start.1
  14.0 2.6 %collective-permute-start.3 = (bf16[2,32,1024]{2,1,0:T(8,128)(2,1)S(1)}, bf16[2,32,1024]{2,1,0:T(8,128)(2,1)S(1)}, u32[]{:S(2)}, u32[]{:S(2)}) collective-permute-start(bf16[2,32,1024]{2,1,0:T(8,128)(2,1)S(1)} %pad_maximum_fusion.refs_0_), channel_id=1, source_target_pairs={{0,4},{1,5},{2,6},{3,7},{4,0},{5,1},{6,2},{7,3},{8,12},{9,13},{10,... | collective-permute-start | bytes 393224 | tf_op jit(solution)/shard_map/ppermute | solution.py:61
  18.4 13.8 %partials.6 = (bf16[2,16,6144]{2,1,0:T(8,128)(2,1)S(1)}, bf16[2,16,6144]{2,1,0:T(8,128)(2,1)S(1)}, bf16[2,16,6144]{2,1,0:T(8,128)(2,1)S(1)}, bf16[2,16,6144]{2,1,0:T(8,128)(2,1)S(1)}) custom-call(bf16[2,32,1024]{2,1,0:T(8,128)(2,1)S(1)} %pad_maximum_fusion.refs_0_, bf16[2,32,1024]{2,1,0:T(8,128)(2,1)S(1)} %collective-permute-done.refs_1_, ...), custom_call_target="tpu_custom_call" | custom-call | tf_op jit(solution)/shard_map/partials/pallas_call | solution.py:110
  32.3 1.6 collective-permute-start.7
  36.6 5.3 %partials.11 = (bf16[2,48,2048]{2,1,0:T(8,128)(2,1)S(1)}, bf16[2,48,2048]{2,1,0:T(8,128)(2,1)S(1)}, bf16[2,48,2048]{2,1,0:T(8,128)(2,1)S(1)}, bf16[2,48,2048]{2,1,0:T(8,128)(2,1)S(1)}) custom-call(bf16[2,32,1024]{2,1,0:T(8,128)(2,1)S(1)} %collective-permute-done.1.refs_2_.refs_0_, bf16[2,32,1024]{2,1,0:T(8,128)(2,1)S(1)} %collective-permute-done.2.refs_3_.refs_1_, ...), custom_call_target="tpu_custom_call" | custom-call | tf_op jit(solution)/shard_map/partials/pallas_call | solution.py:110
  41.8 1.6 collective-permute-start.37
  44.3 5.2 %partials.9 = (bf16[2,48,2048]{2,1,0:T(8,128)(2,1)S(1)}, bf16[2,48,2048]{2,1,0:T(8,128)(2,1)S(1)}, bf16[2,48,2048]{2,1,0:T(8,128)(2,1)S(1)}, bf16[2,48,2048]{2,1,0:T(8,128)(2,1)S(1)}) custom-call(bf16[2,32,1024]{2,1,0:T(8,128)(2,1)S(1)} %collective-permute-done.1.refs_2_.refs_0_, bf16[2,32,1024]{2,1,0:T(8,128)(2,1)S(1)} %collective-permute-done.2.refs_3_.refs_1_, ...), custom_call_target="tpu_custom_call" | custom-call | tf_op jit(solution)/shard_map/partials/pallas_call | solution.py:110
  50.1 1.2 collective-permute-start.26
  51.3 5.2 %partials.8 = (bf16[2,48,2048]{2,1,0:T(8,128)(2,1)S(1)}, bf16[2,48,2048]{2,1,0:T(8,128)(2,1)S(1)}, bf16[2,48,2048]{2,1,0:T(8,128)(2,1)S(1)}, bf16[2,48,2048]{2,1,0:T(8,128)(2,1)S(1)}) custom-call(bf16[2,32,1024]{2,1,0:T(8,128)(2,1)S(1)} %collective-permute-done.1.refs_2_.refs_0_, bf16[2,32,1024]{2,1,0:T(8,128)(2,1)S(1)} %collective-permute-done.2.refs_3_.refs_1_, ...), custom_call_target="tpu_custom_call" | custom-call | tf_op jit(solution)/shard_map/partials/pallas_call | solution.py:110
  56.5 5.3 %partials.7 = (bf16[2,48,2048]{2,1,0:T(8,128)(2,1)S(1)}, bf16[2,48,2048]{2,1,0:T(8,128)(2,1)S(1)}, bf16[2,48,2048]{2,1,0:T(8,128)(2,1)S(1)}, bf16[2,48,2048]{2,1,0:T(8,128)(2,1)S(1)}) custom-call(bf16[2,32,1024]{2,1,0:T(8,128)(2,1)S(1)} %collective-permute-done.1.refs_2_.refs_0_, bf16[2,32,1024]{2,1,0:T(8,128)(2,1)S(1)} %collective-permute-done.2.refs_3_.refs_1_, ...), custom_call_target="tpu_custom_call" | custom-call | tf_op jit(solution)/shard_map/partials/pallas_call | solution.py:110
  61.8 1.6 collective-permute-start.19
  64.8 1.2 collective-permute-start.14
  66.5 1.6 collective-permute-start.10
  68.9 5.1 %collective-permute-done.19.refs_1_ = bf16[2,48,2048]{2,1,0:T(8,128)(2,1)S(1)} collective-permute-done((bf16[2,48,2048]{2,1,0:T(8,128)(2,1)S(1)}, bf16[2,48,2048]{2,1,0:T(8,128)(2,1)S(1)}, u32[]{:S(2)}, u32[]{:S(2)}) %collective-permute-start.19) | collective-permute-done | bytes 393248 | tf_op jit(solution)/shard_map/ppermute | solution.py:57
  76.3 6.0 %collective-permute-done.13.refs_1_ = bf16[2,48,2048]{2,1,0:T(8,128)(2,1)S(1)} collective-permute-done((bf16[2,48,2048]{2,1,0:T(8,128)(2,1)S(1)}, bf16[2,48,2048]{2,1,0:T(8,128)(2,1)S(1)}, u32[]{:S(2)}, u32[]{:S(2)}) %collective-permute-start.13) | collective-permute-done | bytes 393248 | tf_op jit(solution)/shard_map/ppermute | solution.py:57
  82.4 1.5 collective-permute-start.40
  84.8 6.0 %collective-permute-done.10.refs_3_ = bf16[2,16,6144]{2,1,0:T(8,128)(2,1)S(1)} collective-permute-done((bf16[2,16,6144]{2,1,0:T(8,128)(2,1)S(1)}, bf16[2,16,6144]{2,1,0:T(8,128)(2,1)S(1)}, u32[]{:S(2)}, u32[]{:S(2)}) %collective-permute-start.10) | collective-permute-done | bytes 393248 | tf_op jit(solution)/shard_map/ppermute | solution.py:57
  90.8 1.5 collective-permute-start.28
  94.1 6.6 %collective-permute-done.39.refs_1_ = bf16[2,48,2048]{2,1,0:T(8,128)(2,1)S(1)} collective-permute-done((bf16[2,48,2048]{2,1,0:T(8,128)(2,1)S(1)}, bf16[2,48,2048]{2,1,0:T(8,128)(2,1)S(1)}, u32[]{:S(2)}, u32[]{:S(2)}) %collective-permute-start.39) | collective-permute-done | bytes 393248 | tf_op jit(solution)/shard_map/ppermute | solution.py:57
  102.1 7.0 %collective-permute-done.27.refs_1_ = bf16[2,48,2048]{2,1,0:T(8,128)(2,1)S(1)} collective-permute-done((bf16[2,48,2048]{2,1,0:T(8,128)(2,1)S(1)}, bf16[2,48,2048]{2,1,0:T(8,128)(2,1)S(1)}, u32[]{:S(2)}, u32[]{:S(2)}) %collective-permute-start.27) | collective-permute-done | bytes 393248 | tf_op jit(solution)/shard_map/ppermute | solution.py:57
  113.8 12.5 %collective-permute-done.36.refs_5_ = bf16[2,16,2048]{2,1,0:T(8,128)(2,1)S(1)} collective-permute-done((bf16[2,16,2048]{2,1,0:T(8,128)(2,1)S(1)}, bf16[2,16,2048]{2,1,0:T(8,128)(2,1)S(1)}, u32[]{:S(2)}, u32[]{:S(2)}) %collective-permute-start.36) | collective-permute-done | bytes 131104 | tf_op jit(solution)/shard_map/ppermute | solution.py:57
  127.9 1.3 collective-permute-start.41
  132.9 5.4 %collective-permute-done.11.refs_3_ = bf16[2,16,6144]{2,1,0:T(8,128)(2,1)S(1)} collective-permute-done((bf16[2,16,6144]{2,1,0:T(8,128)(2,1)S(1)}, bf16[2,16,6144]{2,1,0:T(8,128)(2,1)S(1)}, u32[]{:S(2)}, u32[]{:S(2)}) %collective-permute-start.11) | collective-permute-done | bytes 393248 | tf_op jit(solution)/shard_map/ppermute | solution.py:57
  140.4 6.4 %collective-permute-done.41.refs_7_ = bf16[2,48,2048]{2,1,0:T(8,128)(2,1)S(1)} collective-permute-done((bf16[2,48,2048]{2,1,0:T(8,128)(2,1)S(1)}, bf16[2,48,2048]{2,1,0:T(8,128)(2,1)S(1)}, u32[]{:S(2)}, u32[]{:S(2)}) %collective-permute-start.41) | collective-permute-done | bytes 393248 | tf_op jit(solution)/shard_map/ppermute | solution.py:57
  148.8 6.4 %collective-permute-done.29.refs_7_ = bf16[2,48,2048]{2,1,0:T(8,128)(2,1)S(1)} collective-permute-done((bf16[2,48,2048]{2,1,0:T(8,128)(2,1)S(1)}, bf16[2,48,2048]{2,1,0:T(8,128)(2,1)S(1)}, u32[]{:S(2)}, u32[]{:S(2)}) %collective-permute-start.29) | collective-permute-done | bytes 393248 | tf_op jit(solution)/shard_map/ppermute | solution.py:57
  156.5 4.9 %grads.4 = (bf16[1024,8192]{1,0:T(8,128)(2,1)}, bf16[1024,8192]{1,0:T(8,128)(2,1)}, f32[1,8192]{1,0:T(1,128)}) custom-call(bf16[1024,256]{1,0:T(8,128)(2,1)S(1)} %get-tuple-element.65.refs_0_, bf16[1024,256]{1,0:T(8,128)(2,1)S(1)} %get-tuple-element.66.refs_1_, bf16[2,16,2048]{2,1,0:T(8,128)(2,1)S(1)} %get-tuple-element.105.refs_2_, ...), custom_call_target="tpu_custom_call" | custom-call | tf_op jit(solution)/shard_map/grads/pallas_call | solution.py:249
  161.3 4.9 %grads.5 = (bf16[1024,8192]{1,0:T(8,128)(2,1)}, bf16[1024,8192]{1,0:T(8,128)(2,1)}, f32[1,8192]{1,0:T(1,128)}) custom-call(bf16[1024,256]{1,0:T(8,128)(2,1)S(1)} %get-tuple-element.65.refs_0_, bf16[1024,256]{1,0:T(8,128)(2,1)S(1)} %get-tuple-element.66.refs_1_, ...), custom_call_target="tpu_custom_call", output_to_operand_aliasing={{0}: (10, {}), {1}: (11, {}), {2}: (12, {})} | custom-call | tf_op jit(solution)/shard_map/grads/pallas_call | solution.py:249
  166.2 4.9 %grads.6 = (bf16[1024,8192]{1,0:T(8,128)(2,1)}, bf16[1024,8192]{1,0:T(8,128)(2,1)}, f32[1,8192]{1,0:T(1,128)}) custom-call(bf16[1024,256]{1,0:T(8,128)(2,1)S(1)} %get-tuple-element.65.refs_0_, bf16[1024,256]{1,0:T(8,128)(2,1)S(1)} %get-tuple-element.66.refs_1_, ...), custom_call_target="tpu_custom_call", output_to_operand_aliasing={{0}: (10, {}), {1}: (11, {}), {2}: (12, {})} | custom-call | tf_op jit(solution)/shard_map/grads/pallas_call | solution.py:249
  171.1 4.9 %grads.7 = (bf16[1024,8192]{1,0:T(8,128)(2,1)}, bf16[1024,8192]{1,0:T(8,128)(2,1)}, f32[1,8192]{1,0:T(1,128)}) custom-call(bf16[1024,256]{1,0:T(8,128)(2,1)S(1)} %get-tuple-element.65.refs_0_, bf16[1024,256]{1,0:T(8,128)(2,1)S(1)} %get-tuple-element.66.refs_1_, ...), custom_call_target="tpu_custom_call", output_to_operand_aliasing={{0}: (10, {}), {1}: (11, {}), {2}: (12, {})} | custom-call | tf_op jit(solution)/shard_map/grads/pallas_call | solution.py:249
  (80 shorter events, 32.8 us)
Async XLA Ops:
  12.4 19.8 %collective-permute-start.1 = (bf16[2,32,1024]{2,1,0:T(8,128)(2,1)S(1)}, bf16[2,32,1024]{2,1,0:T(8,128)(2,1)S(1)}, u32[]{:S(2)}, u32[]{:S(2)}) collective-permute-start(bf16[2,32,1024]{2,1,0:T(8,128)(2,1)S(1)} %pad_maximum_fusion.refs_0_), channel_id=1, source_target_pairs={{0,2},{1,3},{2,0},{3,1},{4,6},{5,7},{6,4},{7,5},{8,10},{9,11},{10,... | collective-permute-start | bytes 393224 | tf_op jit(solution)/shard_map/ppermute | solution.py:61
  14.0 19.9 %collective-permute-start.3 = (bf16[2,32,1024]{2,1,0:T(8,128)(2,1)S(1)}, bf16[2,32,1024]{2,1,0:T(8,128)(2,1)S(1)}, u32[]{:S(2)}, u32[]{:S(2)}) collective-permute-start(bf16[2,32,1024]{2,1,0:T(8,128)(2,1)S(1)} %pad_maximum_fusion.refs_0_), channel_id=1, source_target_pairs={{0,4},{1,5},{2,6},{3,7},{4,0},{5,1},{6,2},{7,3},{8,12},{9,13},{10,... | collective-permute-start | bytes 393224 | tf_op jit(solution)/shard_map/ppermute | solution.py:61
  16.6 17.3 %collective-permute-start.5 = (bf16[2,32,1024]{2,1,0:T(8,128)(2,1)S(1)}, bf16[2,32,1024]{2,1,0:T(8,128)(2,1)S(1)}, u32[]{:S(2)}, u32[]{:S(2)}) collective-permute-start(bf16[2,32,1024]{2,1,0:T(8,128)(2,1)S(1)} %pad_maximum_fusion.refs_0_), channel_id=1, source_target_pairs={{0,6},{1,7},{2,4},{3,5},{4,2},{5,3},{6,0},{7,1},{8,14},{9,15},{10,... | collective-permute-start | bytes 393224 | tf_op jit(solution)/shard_map/ppermute | solution.py:61
  17.0 17.4 %collective-permute-start.33 = (bf16[2,16,2048]{2,1,0:T(8,128)(2,1)S(1)}, bf16[2,16,2048]{2,1,0:T(8,128)(2,1)S(1)}, u32[]{:S(2)}, u32[]{:S(2)}) collective-permute-start(bf16[2,16,2048]{2,1,0:T(8,128)(2,1)S(1)} %get-tuple-element.103.refs_0_), channel_id=1, source_target_pairs={{0,8},{8,0},{16,24},{24,16},{1,9},{9,1},{17,25},{25,17},{2,10},{10... | collective-permute-start | bytes 393224 | tf_op jit(solution)/shard_map/ppermute | solution.py:57
  17.9 16.5 %collective-permute-start.34 = (bf16[2,16,2048]{2,1,0:T(8,128)(2,1)S(1)}, bf16[2,16,2048]{2,1,0:T(8,128)(2,1)S(1)}, u32[]{:S(2)}, u32[]{:S(2)}) collective-permute-start(bf16[2,16,2048]{2,1,0:T(8,128)(2,1)S(1)} %get-tuple-element.104.refs_2_), channel_id=1, source_target_pairs={{0,16},{8,24},{16,0},{24,8},{1,17},{9,25},{17,1},{25,9},{2,18},{10... | collective-permute-start | bytes 393224 | tf_op jit(solution)/shard_map/ppermute | solution.py:57
  32.3 17.9 %collective-permute-start.7 = (bf16[2,16,6144]{2,1,0:T(8,128)(2,1)S(1)}, bf16[2,16,6144]{2,1,0:T(8,128)(2,1)S(1)}, u32[]{:S(2)}, u32[]{:S(2)}) collective-permute-start(bf16[2,16,6144]{2,1,0:T(8,128)(2,1)S(1)} %get-tuple-element.68), channel_id=1, source_target_pairs={{0,16},{8,24},{16,0},{24,8},{1,17},{9,25},{17,1},{25,9},{2,18},{10... | collective-permute-start | bytes 1179656 | tf_op jit(solution)/shard_map/ppermute | solution.py:57
  35.4 26.4 %collective-permute-start.8 = (bf16[2,16,6144]{2,1,0:T(8,128)(2,1)S(1)}, bf16[2,16,6144]{2,1,0:T(8,128)(2,1)S(1)}, u32[]{:S(2)}, u32[]{:S(2)}) collective-permute-start(bf16[2,16,6144]{2,1,0:T(8,128)(2,1)S(1)} %get-tuple-element.70), channel_id=1, source_target_pairs={{0,8},{8,0},{16,24},{24,16},{1,9},{9,1},{17,25},{25,17},{2,10},{10... | collective-permute-start | bytes 1179656 | tf_op jit(solution)/shard_map/ppermute | solution.py:57
  41.8 21.6 %collective-permute-start.37 = (bf16[2,48,2048]{2,1,0:T(8,128)(2,1)S(1)}, bf16[2,48,2048]{2,1,0:T(8,128)(2,1)S(1)}, u32[]{:S(2)}, u32[]{:S(2)}) collective-permute-start(bf16[2,48,2048]{2,1,0:T(8,128)(2,1)S(1)} %get-tuple-element.108), channel_id=1, source_target_pairs={{0,16},{8,24},{16,0},{24,8},{1,17},{9,25},{17,1},{25,9},{2,18},{10... | collective-permute-start | bytes 1179656 | tf_op jit(solution)/shard_map/ppermute | solution.py:57
  43.4 20.9 %collective-permute-start.38 = (bf16[2,48,2048]{2,1,0:T(8,128)(2,1)S(1)}, bf16[2,48,2048]{2,1,0:T(8,128)(2,1)S(1)}, u32[]{:S(2)}, u32[]{:S(2)}) collective-permute-start(bf16[2,48,2048]{2,1,0:T(8,128)(2,1)S(1)} %get-tuple-element.110), channel_id=1, source_target_pairs={{0,8},{8,0},{16,24},{24,16},{1,9},{9,1},{17,25},{25,17},{2,10},{10... | collective-permute-start | bytes 1179656 | tf_op jit(solution)/shard_map/ppermute | solution.py:57
  49.5 15.3 %collective-permute-start.25 = (bf16[2,48,2048]{2,1,0:T(8,128)(2,1)S(1)}, bf16[2,48,2048]{2,1,0:T(8,128)(2,1)S(1)}, u32[]{:S(2)}, u32[]{:S(2)}) collective-permute-start(bf16[2,48,2048]{2,1,0:T(8,128)(2,1)S(1)} %get-tuple-element.92), channel_id=1, source_target_pairs={{0,16},{8,24},{16,0},{24,8},{1,17},{9,25},{17,1},{25,9},{2,18},{10... | collective-permute-start | bytes 1179656 | tf_op jit(solution)/shard_map/ppermute | solution.py:57
  50.1 16.3 %collective-permute-start.26 = (bf16[2,48,2048]{2,1,0:T(8,128)(2,1)S(1)}, bf16[2,48,2048]{2,1,0:T(8,128)(2,1)S(1)}, u32[]{:S(2)}, u32[]{:S(2)}) collective-permute-start(bf16[2,48,2048]{2,1,0:T(8,128)(2,1)S(1)} %get-tuple-element.94), channel_id=1, source_target_pairs={{0,8},{8,0},{16,24},{24,16},{1,9},{9,1},{17,25},{25,17},{2,10},{10... | collective-permute-start | bytes 1179656 | tf_op jit(solution)/shard_map/ppermute | solution.py:57
  64.3 18.1 %collective-permute-start.13 = (bf16[2,48,2048]{2,1,0:T(8,128)(2,1)S(1)}, bf16[2,48,2048]{2,1,0:T(8,128)(2,1)S(1)}, u32[]{:S(2)}, u32[]{:S(2)}) collective-permute-start(bf16[2,48,2048]{2,1,0:T(8,128)(2,1)S(1)} %get-tuple-element.76), channel_id=1, source_target_pairs={{0,16},{8,24},{16,0},{24,8},{1,17},{9,25},{17,1},{25,9},{2,18},{10... | collective-permute-start | bytes 1179656 | tf_op jit(solution)/shard_map/ppermute | solution.py:57
  64.8 19.1 %collective-permute-start.14 = (bf16[2,48,2048]{2,1,0:T(8,128)(2,1)S(1)}, bf16[2,48,2048]{2,1,0:T(8,128)(2,1)S(1)}, u32[]{:S(2)}, u32[]{:S(2)}) collective-permute-start(bf16[2,48,2048]{2,1,0:T(8,128)(2,1)S(1)} %get-tuple-element.78), channel_id=1, source_target_pairs={{0,8},{8,0},{16,24},{24,16},{1,9},{9,1},{17,25},{25,17},{2,10},{10... | collective-permute-start | bytes 1179656 | tf_op jit(solution)/shard_map/ppermute | solution.py:57
  66.5 24.3 %collective-permute-start.10 = (bf16[2,16,6144]{2,1,0:T(8,128)(2,1)S(1)}, bf16[2,16,6144]{2,1,0:T(8,128)(2,1)S(1)}, u32[]{:S(2)}, u32[]{:S(2)}) collective-permute-start(bf16[2,16,6144]{2,1,0:T(8,128)(2,1)S(1)} %get-tuple-element.72.refs_2_), channel_id=1, source_target_pairs={{0,16},{8,24},{16,0},{24,8},{1,17},{9,25},{17,1},{25,9},{2,18},{10... | collective-permute-start | bytes 1179656 | tf_op jit(solution)/shard_map/ppermute | solution.py:57
  73.9 19.2 %collective-permute-start.9 = (bf16[2,16,6144]{2,1,0:T(8,128)(2,1)S(1)}, bf16[2,16,6144]{2,1,0:T(8,128)(2,1)S(1)}, u32[]{:S(2)}, u32[]{:S(2)}) collective-permute-start(bf16[2,16,6144]{2,1,0:T(8,128)(2,1)S(1)} %get-tuple-element.71.refs_0_), channel_id=1, source_target_pairs={{0,8},{8,0},{16,24},{24,16},{1,9},{9,1},{17,25},{25,17},{2,10},{10... | collective-permute-start | bytes 1179656 | tf_op jit(solution)/shard_map/ppermute | solution.py:57
  75.5 25.3 %collective-permute-start.39 = (bf16[2,48,2048]{2,1,0:T(8,128)(2,1)S(1)}, bf16[2,48,2048]{2,1,0:T(8,128)(2,1)S(1)}, u32[]{:S(2)}, u32[]{:S(2)}) collective-permute-start(bf16[2,48,2048]{2,1,0:T(8,128)(2,1)S(1)} %get-tuple-element.111.refs_0_), channel_id=1, source_target_pairs={{0,8},{8,0},{16,24},{24,16},{1,9},{9,1},{17,25},{25,17},{2,10},{10... | collective-permute-start | bytes 1179656 | tf_op jit(solution)/shard_map/ppermute | solution.py:57
  82.4 18.9 %collective-permute-start.40 = (bf16[2,48,2048]{2,1,0:T(8,128)(2,1)S(1)}, bf16[2,48,2048]{2,1,0:T(8,128)(2,1)S(1)}, u32[]{:S(2)}, u32[]{:S(2)}) collective-permute-start(bf16[2,48,2048]{2,1,0:T(8,128)(2,1)S(1)} %get-tuple-element.112.refs_2_), channel_id=1, source_target_pairs={{0,16},{8,24},{16,0},{24,8},{1,17},{9,25},{17,1},{25,9},{2,18},{10... | collective-permute-start | bytes 1179656 | tf_op jit(solution)/shard_map/ppermute | solution.py:57
  83.9 25.3 %collective-permute-start.27 = (bf16[2,48,2048]{2,1,0:T(8,128)(2,1)S(1)}, bf16[2,48,2048]{2,1,0:T(8,128)(2,1)S(1)}, u32[]{:S(2)}, u32[]{:S(2)}) collective-permute-start(bf16[2,48,2048]{2,1,0:T(8,128)(2,1)S(1)} %get-tuple-element.95.refs_0_), channel_id=1, source_target_pairs={{0,8},{8,0},{16,24},{24,16},{1,9},{9,1},{17,25},{25,17},{2,10},{10... | collective-permute-start | bytes 1179656 | tf_op jit(solution)/shard_map/ppermute | solution.py:57
  90.8 18.9 %collective-permute-start.28 = (bf16[2,48,2048]{2,1,0:T(8,128)(2,1)S(1)}, bf16[2,48,2048]{2,1,0:T(8,128)(2,1)S(1)}, u32[]{:S(2)}, u32[]{:S(2)}) collective-permute-start(bf16[2,48,2048]{2,1,0:T(8,128)(2,1)S(1)} %get-tuple-element.96.refs_2_), channel_id=1, source_target_pairs={{0,16},{8,24},{16,0},{24,8},{1,17},{9,25},{17,1},{25,9},{2,18},{10... | collective-permute-start | bytes 1179656 | tf_op jit(solution)/shard_map/ppermute | solution.py:57
  93.2 33.6 %collective-permute-start.21 = (bf16[2,48,2048]{2,1,0:T(8,128)(2,1)S(1)}, bf16[2,48,2048]{2,1,0:T(8,128)(2,1)S(1)}, u32[]{:S(2)}, u32[]{:S(2)}) collective-permute-start(bf16[2,48,2048]{2,1,0:T(8,128)(2,1)S(1)} %get-tuple-element.87.refs_0_), channel_id=1, source_target_pairs={{0,8},{8,0},{16,24},{24,16},{1,9},{9,1},{17,25},{25,17},{2,10},{10... | collective-permute-start | bytes 1179656 | tf_op jit(solution)/shard_map/ppermute | solution.py:57
  100.7 27.2 %collective-permute-start.22 = (bf16[2,48,2048]{2,1,0:T(8,128)(2,1)S(1)}, bf16[2,48,2048]{2,1,0:T(8,128)(2,1)S(1)}, u32[]{:S(2)}, u32[]{:S(2)}) collective-permute-start(bf16[2,48,2048]{2,1,0:T(8,128)(2,1)S(1)} %get-tuple-element.88.refs_2_), channel_id=1, source_target_pairs={{0,16},{8,24},{16,0},{24,8},{1,17},{9,25},{17,1},{25,9},{2,18},{10... | collective-permute-start | bytes 1179656 | tf_op jit(solution)/shard_map/ppermute | solution.py:57
  101.3 27.9 %collective-permute-start.15 = (bf16[2,48,2048]{2,1,0:T(8,128)(2,1)S(1)}, bf16[2,48,2048]{2,1,0:T(8,128)(2,1)S(1)}, u32[]{:S(2)}, u32[]{:S(2)}) collective-permute-start(bf16[2,48,2048]{2,1,0:T(8,128)(2,1)S(1)} %get-tuple-element.79.refs_0_), channel_id=1, source_target_pairs={{0,8},{8,0},{16,24},{24,16},{1,9},{9,1},{17,25},{25,17},{2,10},{10... | collective-permute-start | bytes 1179656 | tf_op jit(solution)/shard_map/ppermute | solution.py:57
  109.2 21.2 %collective-permute-start.16 = (bf16[2,48,2048]{2,1,0:T(8,128)(2,1)S(1)}, bf16[2,48,2048]{2,1,0:T(8,128)(2,1)S(1)}, u32[]{:S(2)}, u32[]{:S(2)}) collective-permute-start(bf16[2,48,2048]{2,1,0:T(8,128)(2,1)S(1)} %get-tuple-element.80.refs_2_), channel_id=1, source_target_pairs={{0,16},{8,24},{16,0},{24,8},{1,17},{9,25},{17,1},{25,9},{2,18},{10... | collective-permute-start | bytes 1179656 | tf_op jit(solution)/shard_map/ppermute | solution.py:57
  109.7 16.6 %collective-permute-start.36 = (bf16[2,16,2048]{2,1,0:T(8,128)(2,1)S(1)}, bf16[2,16,2048]{2,1,0:T(8,128)(2,1)S(1)}, u32[]{:S(2)}, u32[]{:S(2)}) collective-permute-start(bf16[2,16,2048]{2,1,0:T(8,128)(2,1)S(1)} %get-tuple-element.106.refs_4_), channel_id=1, source_target_pairs={{0,8},{8,0},{16,24},{24,16},{1,9},{9,1},{17,25},{25,17},{2,10},{10... | collective-permute-start | bytes 393224 | tf_op jit(solution)/shard_map/ppermute | solution.py:57
  127.9 18.8 %collective-permute-start.41 = (bf16[2,48,2048]{2,1,0:T(8,128)(2,1)S(1)}, bf16[2,48,2048]{2,1,0:T(8,128)(2,1)S(1)}, u32[]{:S(2)}, u32[]{:S(2)}) collective-permute-start(bf16[2,48,2048]{2,1,0:T(8,128)(2,1)S(1)} %get-tuple-element.113.refs_6_), channel_id=1, source_target_pairs={{0,16},{8,24},{16,0},{24,8},{1,17},{9,25},{17,1},{25,9},{2,18},{10... | collective-permute-start | bytes 1179656 | tf_op jit(solution)/shard_map/ppermute | solution.py:57
  129.2 18.4 %collective-permute-start.42 = (bf16[2,48,2048]{2,1,0:T(8,128)(2,1)S(1)}, bf16[2,48,2048]{2,1,0:T(8,128)(2,1)S(1)}, u32[]{:S(2)}, u32[]{:S(2)}) collective-permute-start(bf16[2,48,2048]{2,1,0:T(8,128)(2,1)S(1)} %get-tuple-element.114.refs_8_), channel_id=1, source_target_pairs={{0,8},{8,0},{16,24},{24,16},{1,9},{9,1},{17,25},{25,17},{2,10},{10... | collective-permute-start | bytes 1179656 | tf_op jit(solution)/shard_map/ppermute | solution.py:57
  130.3 24.8 %collective-permute-start.29 = (bf16[2,48,2048]{2,1,0:T(8,128)(2,1)S(1)}, bf16[2,48,2048]{2,1,0:T(8,128)(2,1)S(1)}, u32[]{:S(2)}, u32[]{:S(2)}) collective-permute-start(bf16[2,48,2048]{2,1,0:T(8,128)(2,1)S(1)} %get-tuple-element.97.refs_6_), channel_id=1, source_target_pairs={{0,16},{8,24},{16,0},{24,8},{1,17},{9,25},{17,1},{25,9},{2,18},{10... | collective-permute-start | bytes 1179656 | tf_op jit(solution)/shard_map/ppermute | solution.py:57
  138.3 23.0 %collective-permute-start.30 = (bf16[2,48,2048]{2,1,0:T(8,128)(2,1)S(1)}, bf16[2,48,2048]{2,1,0:T(8,128)(2,1)S(1)}, u32[]{:S(2)}, u32[]{:S(2)}) collective-permute-start(bf16[2,48,2048]{2,1,0:T(8,128)(2,1)S(1)} %get-tuple-element.98.refs_8_), channel_id=1, source_target_pairs={{0,8},{8,0},{16,24},{24,16},{1,9},{9,1},{17,25},{25,17},{2,10},{10... | collective-permute-start | bytes 1179656 | tf_op jit(solution)/shard_map/ppermute | solution.py:57
  139.2 27.0 %collective-permute-start.23 = (bf16[2,48,2048]{2,1,0:T(8,128)(2,1)S(1)}, bf16[2,48,2048]{2,1,0:T(8,128)(2,1)S(1)}, u32[]{:S(2)}, u32[]{:S(2)}) collective-permute-start(bf16[2,48,2048]{2,1,0:T(8,128)(2,1)S(1)} %get-tuple-element.89.refs_6_), channel_id=1, source_target_pairs={{0,16},{8,24},{16,0},{24,8},{1,17},{9,25},{17,1},{25,9},{2,18},{10... | collective-permute-start | bytes 1179656 | tf_op jit(solution)/shard_map/ppermute | solution.py:57
  146.8 19.4 %collective-permute-start.24 = (bf16[2,48,2048]{2,1,0:T(8,128)(2,1)S(1)}, bf16[2,48,2048]{2,1,0:T(8,128)(2,1)S(1)}, u32[]{:S(2)}, u32[]{:S(2)}) collective-permute-start(bf16[2,48,2048]{2,1,0:T(8,128)(2,1)S(1)} %get-tuple-element.90.refs_8_), channel_id=1, source_target_pairs={{0,8},{8,0},{16,24},{24,16},{1,9},{9,1},{17,25},{25,17},{2,10},{10... | collective-permute-start | bytes 1179656 | tf_op jit(solution)/shard_map/ppermute | solution.py:57
  147.6 23.4 %collective-permute-start.17 = (bf16[2,48,2048]{2,1,0:T(8,128)(2,1)S(1)}, bf16[2,48,2048]{2,1,0:T(8,128)(2,1)S(1)}, u32[]{:S(2)}, u32[]{:S(2)}) collective-permute-start(bf16[2,48,2048]{2,1,0:T(8,128)(2,1)S(1)} %get-tuple-element.81.refs_6_), channel_id=1, source_target_pairs={{0,16},{8,24},{16,0},{24,8},{1,17},{9,25},{17,1},{25,9},{2,18},{10... | collective-permute-start | bytes 1179656 | tf_op jit(solution)/shard_map/ppermute | solution.py:57
  155.2 15.9 %collective-permute-start.18 = (bf16[2,48,2048]{2,1,0:T(8,128)(2,1)S(1)}, bf16[2,48,2048]{2,1,0:T(8,128)(2,1)S(1)}, u32[]{:S(2)}, u32[]{:S(2)}) collective-permute-start(bf16[2,48,2048]{2,1,0:T(8,128)(2,1)S(1)} %get-tuple-element.82.refs_8_), channel_id=1, source_target_pairs={{0,8},{8,0},{16,24},{24,16},{1,9},{9,1},{17,25},{25,17},{2,10},{10... | collective-permute-start | bytes 1179656 | tf_op jit(solution)/shard_map/ppermute | solution.py:57
  (12 other events, 102.6 us)

commit v2 on v1

v2 whole, which is shorter than its diff:
```python
import functools
import math

import jax
import jax.numpy as jnp
from jax import lax
from jax.experimental import pallas as pl
from jax.experimental.pallas import tpu as pltpu
from jax.sharding import PartitionSpec as P

BF16 = jnp.bfloat16
F32 = jnp.float32
VMEM_LIMIT = 48 * 2**20


def params():
    return pltpu.CompilerParams(vmem_limit_bytes=VMEM_LIMIT)


def waiting(after):
    return [pl.BlockSpec(memory_space=pl.ANY)] * len(after)


def tree_sum(parts):
    while len(parts) > 1:
        parts = [parts[i] + parts[i + 1] for i in range(0, len(parts), 2)]
    return parts[0]


def divisor(extent, most):
    size = min(extent, most)
    while extent % size:
        size -= 128
    return size


class Plan:
    def __init__(self, layers, peers, rows, stack, feats):
        self.layers, self.peers, self.rows = layers, peers, rows
        self.stack, self.feats = stack, feats
        self.bits = layers.bit_length() - 1
        self.blocks = 1 << max(self.bits - 1, 0)
        order = list(range(self.bits))
        self.orders = (order[::-1], order)
        near = 2
        while near < peers and (near * rows) % (32 * self.blocks):
            near *= 2
        self.near = min(near, peers)

    def block_rows(self, group):
        return group * self.rows // (2 * self.blocks)

    def keys(self):
        me = lax.axis_index("layer")
        out = []
        for order in self.orders:
            key = 0
            for level, bit in enumerate(order[:-1]):
                key = key + (((me >> bit) & 1) << (self.bits - 2 - level))
            out.append(key)
        return out

    def swap(self, array, bit):
        pairs = [(i, i ^ (1 << bit)) for i in range(self.layers)]
        return lax.ppermute(array, "layer", pairs)

    def peer(self, array, distance):
        pairs = [(i, i ^ distance) for i in range(self.peers)]
        return lax.ppermute(array, "feat", pairs)


def place_rows(plan, groups, raws, store):
    keys = plan.keys()
    heights = [plan.block_rows(group) for group in groups]
    step = 16
    first = base = 0
    for group, block in zip(groups, heights):
        for start in range(0, group * plan.rows, step):
            stream, within = divmod(start, block * plan.blocks)
            index, off = divmod(within, block)
            row = (stream * plan.blocks + (index ^ keys[stream])) * sum(heights) + base + off
            row = pl.multiple_of(row, step)
            piece, at = divmod(start, plan.rows)
            for q in range(2):
                store(q, row, raws[first + piece][q, at : at + step, :])
        first += group
        base += block


def partial_kernel(plan, groups, waits, *refs):
    count = sum(groups)
    raws, (enc_ref, dec_ref), outs, (tokens_ref,) = (
        refs[:count],
        refs[count : count + 2],
        refs[count + 2 + waits : -1],
        refs[-1:],
    )

    @pl.when(pl.program_id(0) == 0)
    def _():
        def store(q, row, values):
            tokens_ref[q, pl.ds(row, 16), :] = values

        place_rows(plan, groups, raws, store)

    rows = outs[0].shape[1]
    for q, weight in enumerate((enc_ref, dec_ref)):
        part = jnp.dot(tokens_ref[q], weight[...], preferred_element_type=F32)
        for i, out in enumerate(outs):
            out[q] = part[i * rows : (i + 1) * rows].astype(BF16)


def partials(plan, groups, raws, enc_weight, dec_weight, first, width, after):
    tokens = len(raws) * plan.rows
    outs = 4 if plan.blocks > 1 else 2
    block = divisor(math.gcd(first, width), 1024)
    base = first // block
    weight = pl.BlockSpec((plan.stack, block), lambda i: (0, base + i))
    raw = pl.BlockSpec((2, plan.rows, plan.stack), lambda i: (0, 0, 0))
    out = pl.BlockSpec((2, tokens // outs, block), lambda i: (0, 0, i))
    return pl.pallas_call(
        functools.partial(partial_kernel, plan, groups, len(after)),
        grid=(width // block,),
        in_specs=[raw] * len(raws) + [weight] * 2 + waiting(after),
        out_specs=[out] * outs,
        out_shape=[jax.ShapeDtypeStruct((2, tokens // outs, width), BF16)] * outs,
        scratch_shapes=[pltpu.VMEM((2, tokens, plan.stack), BF16)],
        compiler_params=params(),
        name="partials",
    )(*raws, enc_weight, dec_weight, *after)


def add_kernel(pieces, waits, *refs):
    outs = refs[4 + waits :]
    for stream in range(2):
        total = refs[2 * stream][...].astype(F32) + refs[2 * stream + 1][...].astype(F32)
        rows = total.shape[1] // pieces
        for i in range(pieces):
            outs[stream * pieces + i][...] = total[:, i * rows : (i + 1) * rows].astype(BF16)


def add(plan, kept, got, pieces, after):
    _, rows, width = kept[0].shape
    block = divisor(width, 1024)
    whole = pl.BlockSpec((2, rows, block), lambda i: (0, 0, i))
    part = pl.BlockSpec((2, rows // pieces, block), lambda i: (0, 0, i))
    return pl.pallas_call(
        functools.partial(add_kernel, pieces, len(after)),
        grid=(width // block,),
        in_specs=[whole] * 4 + waiting(after),
        out_specs=[part] * (2 * pieces),
        out_shape=[jax.ShapeDtypeStruct((2, rows // pieces, width), BF16)] * (2 * pieces),
        compiler_params=params(),
        name="add",
    )(kept[0], got[0], kept[1], got[1], *after)


def gate_kernel(waits, *refs):
    outs = refs[5 + waits :]
    bias = refs[4][...]
    for stream in range(2):
        mine, other = refs[2 * stream], refs[2 * stream + 1]
        scaled = 4.0 * (mine[0].astype(F32) + other[0].astype(F32) + bias)
        code_grad = mine[1].astype(F32) + other[1].astype(F32)
        small = jnp.exp(-jnp.abs(scaled))
        code = 0.25 * (jnp.maximum(scaled, 0.0) + jnp.log1p(small))
        gate = jnp.where(scaled >= 0.0, 1.0, small) / (1.0 + small)
        outs[stream][0] = code.astype(BF16)
        outs[stream][1] = (code_grad * gate).astype(BF16)


def gate(plan, mine, other, bias, first, after):
    _, rows, width = mine[0].shape
    block = divisor(math.gcd(first, width), 1024)
    base = first // block
    whole = pl.BlockSpec((2, rows, block), lambda i: (0, 0, i))
    return pl.pallas_call(
        functools.partial(gate_kernel, len(after)),
        grid=(width // block,),
        in_specs=[whole] * 4 + [pl.BlockSpec((1, block), lambda i: (0, base + i))] + waiting(after),
        out_specs=[whole] * 2,
        out_shape=[jax.ShapeDtypeStruct((2, rows, width), BF16)] * 2,
        compiler_params=params(),
        name="gate",
    )(mine[0], other[0], mine[1], other[1], bias, *after)


def turn_kernel(plan, groups, waits, *refs):
    raws, outs, scratch = refs[: sum(groups)], refs[sum(groups) + waits : -1], refs[-1]

    def store(q, row, values):
        scratch[q, pl.ds(row, 16), :] = values

    place_rows(plan, groups, raws, store)
    for q in range(2):
        outs[q][...] = scratch[q].T


def turned(plan, groups, raws, after):
    tokens = len(raws) * plan.rows
    whole = pl.BlockSpec(memory_space=pltpu.VMEM)
    return pl.pallas_call(
        functools.partial(turn_kernel, plan, groups, len(after)),
        in_specs=[whole] * len(raws) + waiting(after),
        out_specs=[whole] * 2,
        out_shape=[jax.ShapeDtypeStruct((plan.stack, tokens), BF16)] * 2,
        scratch_shapes=[pltpu.VMEM((2, tokens, plan.stack), BF16)],
        compiler_params=params(),
        name="turned",
    )(*raws, *after)


def grads_kernel(rows, skips, waits, *refs):
    resid_ref, error_ref = refs[:2]
    parts = refs[2 : 2 + len(skips)]
    enc_ref, dec_ref, bias_ref, code_ref, masked_ref = refs[2 + len(skips) + waits :]
    block = code_ref.shape[1]
    here = pl.program_id(0) * block
    left = iter(zip(parts, skips))
    total = None
    for stream in rows:
        blocks = []
        for row in stream:
            part, skip = next(left)
            height = part.shape[1]
            columns = pl.ds(pl.multiple_of(skip + here, 128), block)
            masked = part[1, :, columns]
            code_ref[row : row + height] = part[0, :, columns]
            masked_ref[row : row + height] = masked
            blocks.append(jnp.sum(masked.astype(F32), axis=0, keepdims=True))
        value = tree_sum(blocks)
        total = value if total is None else total + value
    bias_ref[...] = total
    enc_ref[...] = jnp.dot(resid_ref[...], masked_ref[...], preferred_element_type=F32).astype(BF16)
    dec_ref[...] = jnp.dot(error_ref[...], code_ref[...], preferred_element_type=F32).astype(BF16)


def grads(plan, turned_tokens, held, first, width, before, after):
    tokens = turned_tokens[0].shape[1]
    block = divisor(math.gcd(first, width), 1024)
    base = first // block
    parts, skips = [], []
    for arrays, _, origin in held:
        parts += arrays
        skips += [first - origin] * len(arrays)
    inside = pl.BlockSpec(memory_space=pltpu.VMEM)
    extra = list(before) + after
    return pl.pallas_call(
        functools.partial(grads_kernel, [rows for _, rows, _ in held], skips, len(extra)),
        grid=(width // block,),
        in_specs=[inside] * (2 + len(parts)) + waiting(extra),
        out_specs=[
            pl.BlockSpec((plan.stack, block), lambda i: (0, base + i)),
            pl.BlockSpec((plan.stack, block), lambda i: (0, base + i)),
            pl.BlockSpec((1, block), lambda i: (0, base + i)),
        ],
        out_shape=[
            jax.ShapeDtypeStruct((plan.stack, plan.feats), BF16),
            jax.ShapeDtypeStruct((plan.stack, plan.feats), BF16),
            jax.ShapeDtypeStruct((1, plan.feats), F32),
        ],
        scratch_shapes=[pltpu.VMEM((tokens, block), BF16)] * 2,
        input_output_aliases={2 + len(parts) + i: i for i in range(len(before))},
        compiler_params=params(),
        name="grads",
    )(*turned_tokens, *parts, *extra)


class Piece:
    def __init__(self, plan, which, first, width):
        self.plan, self.first, self.width = plan, first, width
        near, far = plan.near, plan.peers - plan.near
        heights = [plan.block_rows(near), plan.block_rows(far)]
        self.groups = {"near": [near], "far": [far], "all": [near, far]}[which]
        self.skip = plan.near if which == "far" else 0
        base = heights[0] if which == "far" else 0
        self.rows = [
            [(s * plan.blocks + j) * sum(heights) + base for j in range(plan.blocks)]
            for s in range(2)
        ]

    def start(self, raws, enc_weight, dec_weight, after):
        plan = self.plan
        raws = raws[self.skip : self.skip + sum(self.groups)]
        outs = partials(plan, self.groups, raws, enc_weight, dec_weight, self.first, self.width, after)
        self.level = 0
        if plan.blocks > 1:
            self.kept = [outs[0], outs[2]]
            self.swap([outs[1], outs[3]])
        else:
            self.kept = list(outs)
            self.swap(self.kept)
        return outs[0]

    def swap(self, sent):
        self.got = [self.plan.swap(sent[s], self.plan.orders[s][self.level]) for s in range(2)]
        self.level += 1

    def add(self, after):
        last = self.plan.bits - 1
        while self.level <= last:
            pieces = 2 if self.level < last else 1
            cut = add(self.plan, self.kept, self.got, pieces, after)
            after = [cut[0]]
            if pieces == 2:
                self.kept = [cut[0], cut[2]]
                self.swap([cut[1], cut[3]])
            else:
                self.kept = list(cut)
                self.swap(self.kept)
        return after[0]

    def gate(self, bias, after):
        plan = self.plan
        gated = gate(plan, self.kept, self.got, bias, self.first, after)
        self.held = [[gated[0]], [gated[1]]]
        for level in reversed(range(plan.bits - 1)):
            for s in range(2):
                self.held[s] = self.held[s] + [
                    plan.swap(array, plan.orders[s][level]) for array in self.held[s]
                ]
        return gated[0]


PIECES = (("all", 0, 3), ("all", 3, 3), ("all", 6, 3), ("all", 9, 3), ("all", 12, 2), ("all", 14, 2))
GRADS = tuple((first, width) for _, first, width in PIECES)
ORDER = (
    "P0", "P1", "T0", "A0", "A1", "N0", "N1", "P2",
    "G0", "P3", "G1", "A2", "A3", "N2", "N3", "P4",
    "G2", "P5", "G3", "A4", "A5", "N4", "N5", "G4",
    "G5",
)
CHAIN = True


def per_device(plan, residuals, errors, enc_weight, dec_weight, enc_bias):
    feats = plan.feats
    unit = feats // 16
    bias = enc_bias.reshape(1, feats)
    own = jnp.stack([residuals, errors])
    raws = [own] + [plan.peer(own, m) for m in range(1, plan.near)]
    for m in range(plan.near, plan.peers, 2):
        came = plan.peer(own, m)
        raws += [came, plan.peer(came, 1)]

    pieces = [Piece(plan, which, first * unit, width * unit) for which, first, width in PIECES]
    result, tokens, chain = [], {}, []
    for entry in ORDER:
        op, *behind = entry.split("<")
        step, index = op[0], int(op[1:])
        after = list(chain)
        for name in behind:
            if name[0] == "H":
                after += [part[-1] for part in pieces[int(name[1:])].held]
            else:
                after.append(tokens[name])
        if step == "P":
            token = pieces[index].start(raws, enc_weight, dec_weight, after)
        elif step == "A":
            token = pieces[index].add(after)
        elif step == "N":
            token = pieces[index].gate(bias, after)
        elif step == "T":
            flipped = turned(plan, [plan.near, plan.peers - plan.near], raws, after)
            token = flipped[0]
        else:
            first, width = (unit * v for v in GRADS[index])
            held = []
            for piece in pieces:
                if piece.first <= first < piece.first + piece.width:
                    held += [(piece.held[s], piece.rows[s], piece.first) for s in range(2)]
            result = grads(plan, flipped, held, first, width, result, after)
            token = result[2]
        tokens[op] = token
        chain = [token] if CHAIN else []
    enc_grad, dec_grad, bias_grad = result
    return enc_grad, dec_grad, bias_grad.reshape(feats)


def solution(mesh):
    placed = (
        P("feat", "layer"),
        P("feat", "layer"),
        P("layer", "feat"),
        P("layer", "feat"),
        P("feat"),
    )
    layers, peers = mesh.shape["layer"], mesh.shape["feat"]

    def body(residuals, errors, enc_weight, dec_weight, enc_bias):
        plan = Plan(layers, peers, residuals.shape[0], residuals.shape[1], enc_bias.shape[0])
        return per_device(plan, residuals, errors, enc_weight, dec_weight, enc_bias)

    return jax.shard_map(
        body,
        mesh=mesh,
        in_specs=placed,
        out_specs=(P("layer", "feat"), P("layer", "feat"), P("feat")),
        check_vma=False,
    )
```

time: 176 us -> 165 us (0.938)
  Pallas kernels: 67.5 us -> 51.8 us
  waiting for transfers between devices: 63.2 us -> 66.8 us
    pallas_call x23 -> x25, Pallas kernels: 67.5 us -> 51.8 us  [the longest x6 23.4 us: partials(): pl.pallas_call(functools.partial(partial_kernel, plan, groups, len(after)...]
    ppermute x7, waiting for transfers between devices: 1 us -> 11.4 us  [peer(): return lax.ppermute(array, 'feat', pairs)]
    ppermute x36, waiting for transfers between devices: 62.2 us -> 55.3 us  [swap(): return lax.ppermute(array, 'layer', pairs)]
  transfers between devices with their start and end apart: 43 -> 43, of which waited for: 11 -> 29; matrix products, arithmetic and copies ran while one was open for 0% -> 0% of each run, Pallas kernels for 33% -> 27%
where the time goes in v2:
time: 165 us
  waiting for transfers between devices  66.8 us (40%)
  Pallas kernels  51.8 us (31%)
  starting transfers between devices  44.2 us (27%)
    ppermute x36, waiting for transfers between devices, swap(): return lax.ppermute(array, 'layer', pairs)  55.3 us
    ppermute x36, starting transfers between devices, swap(): return lax.ppermute(array, 'layer', pairs)  37.9 us
    pallas_call x6, Pallas kernels, partials(): pl.pallas_call(functools.partial(partial_kernel, plan, groups, len(after)...  23.4 us
    pallas_call x6, Pallas kernels, grads(): pl.pallas_call(functools.partial(grads_kernel, [rows for _, rows, _ in he...  20.8 us
    ppermute x7, waiting for transfers between devices, peer(): return lax.ppermute(array, 'feat', pairs)  11.4 us
    ppermute x7, starting transfers between devices, peer(): return lax.ppermute(array, 'feat', pairs)  6.27 us
    pallas_call x6, Pallas kernels, gate(): pl.pallas_call(functools.partial(gate_kernel, len(after)), grid=(width //...  5.36 us
  transfers between devices with their start and end apart: 43, of which 29 were waited for; matrix products, arithmetic and copies ran while one was open for 0% of the time, Pallas kernels for 27%

profile of v2, /device:TPU:0, one launch (start us, length us, event | category | flops | bytes accessed | tf_op | source)
XLA Modules:
  0.0 165.1 jit_solution(3529318639450970268)
XLA Ops:
  1.5 5.1 %collective-permute-start.5 = (bf16[2,32,1024]{2,1,0:T(8,128)(2,1)S(1)}, bf16[2,32,1024]{2,1,0:T(8,128)(2,1)S(1)}, u32[]{:S(2)}, u32[]{:S(2)}) collective-permute-start(bf16[2,32,1024]{2,1,0:T(8,128)(2,1)S(1)} %pad_maximum_fusion.refs_0_), channel_id=1, source_target_pairs={{0,6},{1,7},{2,4},{3,5},{4,2},{5,3},{6,0},{7,1},{8,14},{9,15},{10,... | collective-permute-start | bytes 393224 | tf_op jit(solution)/shard_map/ppermute | solution.py:69
  7.3 3.8 %collective-permute-done.5.refs_6_ = bf16[2,32,1024]{2,1,0:T(8,128)(2,1)S(1)} collective-permute-done((bf16[2,32,1024]{2,1,0:T(8,128)(2,1)S(1)}, bf16[2,32,1024]{2,1,0:T(8,128)(2,1)S(1)}, u32[]{:S(2)}, u32[]{:S(2)}) %collective-permute-start.5) | collective-permute-done | bytes 131104 | tf_op jit(solution)/shard_map/ppermute | solution.py:69
  11.1 6.6 %collective-permute-done.3.refs_4_ = bf16[2,32,1024]{2,1,0:T(8,128)(2,1)S(1)} collective-permute-done((bf16[2,32,1024]{2,1,0:T(8,128)(2,1)S(1)}, bf16[2,32,1024]{2,1,0:T(8,128)(2,1)S(1)}, u32[]{:S(2)}, u32[]{:S(2)}) %collective-permute-start.3) | collective-permute-done | bytes 131104 | tf_op jit(solution)/shard_map/ppermute | solution.py:69
  19.2 4.1 %partials.6 = (bf16[2,64,1536]{2,1,0:T(8,128)(2,1)S(1)}, bf16[2,64,1536]{2,1,0:T(8,128)(2,1)S(1)}, bf16[2,64,1536]{2,1,0:T(8,128)(2,1)S(1)}, bf16[2,64,1536]{2,1,0:T(8,128)(2,1)S(1)}) custom-call(bf16[2,32,1024]{2,1,0:T(8,128)(2,1)S(1)} %pad_maximum_fusion.refs_0_, bf16[2,32,1024]{2,1,0:T(8,128)(2,1)S(1)} %collective-permute-done.refs_1_, ...), custom_call_target="tpu_custom_call" | custom-call | tf_op jit(solution)/shard_map/partials/pallas_call | solution.py:121
  23.3 1.6 collective-permute-start.9
  26.4 4.1 %partials.7 = (bf16[2,64,1536]{2,1,0:T(8,128)(2,1)S(1)}, bf16[2,64,1536]{2,1,0:T(8,128)(2,1)S(1)}, bf16[2,64,1536]{2,1,0:T(8,128)(2,1)S(1)}, bf16[2,64,1536]{2,1,0:T(8,128)(2,1)S(1)}) custom-call(bf16[2,32,1024]{2,1,0:T(8,128)(2,1)S(1)} %pad_maximum_fusion.refs_0_, bf16[2,32,1024]{2,1,0:T(8,128)(2,1)S(1)} %collective-permute-done.refs_1_, ...), custom_call_target="tpu_custom_call" | custom-call | tf_op jit(solution)/shard_map/partials/pallas_call | solution.py:121
  32.0 3.3 %collective-permute-done.9.refs_1_ = bf16[2,64,1536]{2,1,0:T(8,128)(2,1)S(1)} collective-permute-done((bf16[2,64,1536]{2,1,0:T(8,128)(2,1)S(1)}, bf16[2,64,1536]{2,1,0:T(8,128)(2,1)S(1)}, u32[]{:S(2)}, u32[]{:S(2)}) %collective-permute-start.9) | collective-permute-done | bytes 393248 | tf_op jit(solution)/shard_map/ppermute | solution.py:65
  35.3 1.6 collective-permute-done.10.refs_3_
  39.4 4.4 %collective-permute-done.7.refs_1_ = bf16[2,64,1536]{2,1,0:T(8,128)(2,1)S(1)} collective-permute-done((bf16[2,64,1536]{2,1,0:T(8,128)(2,1)S(1)}, bf16[2,64,1536]{2,1,0:T(8,128)(2,1)S(1)}, u32[]{:S(2)}, u32[]{:S(2)}) %collective-permute-start.7) | collective-permute-done | bytes 393248 | tf_op jit(solution)/shard_map/ppermute | solution.py:65
  43.8 1.6 collective-permute-done.8.refs_3_
  47.8 4.4 %collective-permute-done.14.refs_3_ = bf16[2,64,1536]{2,1,0:T(8,128)(2,1)S(1)} collective-permute-done((bf16[2,64,1536]{2,1,0:T(8,128)(2,1)S(1)}, bf16[2,64,1536]{2,1,0:T(8,128)(2,1)S(1)}, u32[]{:S(2)}, u32[]{:S(2)}) %collective-permute-start.14) | collective-permute-done | bytes 393248 | tf_op jit(solution)/shard_map/ppermute | solution.py:65
  52.2 1.6 collective-permute-done.13.refs_1_
  56.9 3.8 %collective-permute-done.12.refs_3_ = bf16[2,64,1536]{2,1,0:T(8,128)(2,1)S(1)} collective-permute-done((bf16[2,64,1536]{2,1,0:T(8,128)(2,1)S(1)}, bf16[2,64,1536]{2,1,0:T(8,128)(2,1)S(1)}, u32[]{:S(2)}, u32[]{:S(2)}) %collective-permute-start.12) | collective-permute-done | bytes 393248 | tf_op jit(solution)/shard_map/ppermute | solution.py:65
  65.3 4.1 %partials.8 = (bf16[2,64,1536]{2,1,0:T(8,128)(2,1)S(1)}, bf16[2,64,1536]{2,1,0:T(8,128)(2,1)S(1)}, bf16[2,64,1536]{2,1,0:T(8,128)(2,1)S(1)}, bf16[2,64,1536]{2,1,0:T(8,128)(2,1)S(1)}) custom-call(bf16[2,32,1024]{2,1,0:T(8,128)(2,1)S(1)} %pad_maximum_fusion.refs_0_, bf16[2,32,1024]{2,1,0:T(8,128)(2,1)S(1)} %collective-permute-done.refs_1_, ...), custom_call_target="tpu_custom_call" | custom-call | tf_op jit(solution)/shard_map/partials/pallas_call | solution.py:121
  69.4 1.6 collective-permute-start.15
  72.1 3.7 %grads.6 = (bf16[1024,8192]{1,0:T(8,128)(2,1)}, bf16[1024,8192]{1,0:T(8,128)(2,1)}, f32[1,8192]{1,0:T(1,128)S(1)}) custom-call(bf16[1024,256]{1,0:T(8,128)(2,1)S(1)} %get-tuple-element.73.refs_4_.refs_0_, bf16[1024,256]{1,0:T(8,128)(2,1)S(1)} %get-tuple-element.74.refs_1_, bf16[2,64,1536]{2,1,0:T(8,128)(2,1)S(1)} %get-tuple-element.85.refs_5_.refs_2_, ...), custom_call_target="tpu_custom_call" | custom-call | tf_op jit(solution)/shard_map/grads/pallas_call | solution.py:248
  75.8 4.1 %partials.9 = (bf16[2,64,1536]{2,1,0:T(8,128)(2,1)S(1)}, bf16[2,64,1536]{2,1,0:T(8,128)(2,1)S(1)}, bf16[2,64,1536]{2,1,0:T(8,128)(2,1)S(1)}, bf16[2,64,1536]{2,1,0:T(8,128)(2,1)S(1)}) custom-call(bf16[2,32,1024]{2,1,0:T(8,128)(2,1)S(1)} %pad_maximum_fusion.refs_0_, bf16[2,32,1024]{2,1,0:T(8,128)(2,1)S(1)} %collective-permute-done.refs_1_, ...), custom_call_target="tpu_custom_call" | custom-call | tf_op jit(solution)/shard_map/partials/pallas_call | solution.py:121
  81.4 3.7 %grads.7 = (bf16[1024,8192]{1,0:T(8,128)(2,1)}, bf16[1024,8192]{1,0:T(8,128)(2,1)}, f32[1,8192]{1,0:T(1,128)S(1)}) custom-call(bf16[1024,256]{1,0:T(8,128)(2,1)S(1)} %get-tuple-element.73.refs_4_.refs_0_, bf16[1024,256]{1,0:T(8,128)(2,1)S(1)} %get-tuple-element.74.refs_1_, ...), custom_call_target="tpu_custom_call", output_to_operand_aliasing={{0}: (6, {}), {1}: (7, {}), {2}: (8, {})} | custom-call | tf_op jit(solution)/shard_map/grads/pallas_call | solution.py:248
  85.9 1.6 collective-permute-done.16.refs_3_
  89.9 4.4 %collective-permute-done.23.refs_1_ = bf16[2,64,1536]{2,1,0:T(8,128)(2,1)S(1)} collective-permute-done((bf16[2,64,1536]{2,1,0:T(8,128)(2,1)S(1)}, bf16[2,64,1536]{2,1,0:T(8,128)(2,1)S(1)}, u32[]{:S(2)}, u32[]{:S(2)}) %collective-permute-start.23) | collective-permute-done | bytes 393248 | tf_op jit(solution)/shard_map/ppermute | solution.py:65
  94.3 1.6 collective-permute-done.24.refs_3_
  98.4 4.4 %collective-permute-done.22.refs_3_ = bf16[2,64,1536]{2,1,0:T(8,128)(2,1)S(1)} collective-permute-done((bf16[2,64,1536]{2,1,0:T(8,128)(2,1)S(1)}, bf16[2,64,1536]{2,1,0:T(8,128)(2,1)S(1)}, u32[]{:S(2)}, u32[]{:S(2)}) %collective-permute-start.22) | collective-permute-done | bytes 393248 | tf_op jit(solution)/shard_map/ppermute | solution.py:65
  107.4 3.8 %collective-permute-done.28.refs_3_ = bf16[2,64,1536]{2,1,0:T(8,128)(2,1)S(1)} collective-permute-done((bf16[2,64,1536]{2,1,0:T(8,128)(2,1)S(1)}, bf16[2,64,1536]{2,1,0:T(8,128)(2,1)S(1)}, u32[]{:S(2)}, u32[]{:S(2)}) %collective-permute-start.28) | collective-permute-done | bytes 393248 | tf_op jit(solution)/shard_map/ppermute | solution.py:65
  116.0 3.5 %partials.10 = (bf16[2,64,1024]{2,1,0:T(8,128)(2,1)S(1)}, bf16[2,64,1024]{2,1,0:T(8,128)(2,1)S(1)}, bf16[2,64,1024]{2,1,0:T(8,128)(2,1)S(1)}, bf16[2,64,1024]{2,1,0:T(8,128)(2,1)S(1)}) custom-call(bf16[2,32,1024]{2,1,0:T(8,128)(2,1)S(1)} %pad_maximum_fusion.refs_0_, bf16[2,32,1024]{2,1,0:T(8,128)(2,1)S(1)} %collective-permute-done.refs_1_, ...), custom_call_target="tpu_custom_call" | custom-call | tf_op jit(solution)/shard_map/partials/pallas_call | solution.py:121
  119.5 1.6 collective-permute-start.31
  122.7 3.7 %grads.8 = (bf16[1024,8192]{1,0:T(8,128)(2,1)}, bf16[1024,8192]{1,0:T(8,128)(2,1)}, f32[1,8192]{1,0:T(1,128)S(1)}) custom-call(bf16[1024,256]{1,0:T(8,128)(2,1)S(1)} %get-tuple-element.73.refs_4_.refs_0_, bf16[1024,256]{1,0:T(8,128)(2,1)S(1)} %get-tuple-element.74.refs_1_, ...), custom_call_target="tpu_custom_call", output_to_operand_aliasing={{0}: (6, {}), {1}: (7, {}), {2}: (8, {})} | custom-call | tf_op jit(solution)/shard_map/grads/pallas_call | solution.py:248
  126.4 3.5 %partials.11 = (bf16[2,64,1024]{2,1,0:T(8,128)(2,1)S(1)}, bf16[2,64,1024]{2,1,0:T(8,128)(2,1)S(1)}, bf16[2,64,1024]{2,1,0:T(8,128)(2,1)S(1)}, bf16[2,64,1024]{2,1,0:T(8,128)(2,1)S(1)}) custom-call(bf16[2,32,1024]{2,1,0:T(8,128)(2,1)S(1)} %pad_maximum_fusion.refs_0_, bf16[2,32,1024]{2,1,0:T(8,128)(2,1)S(1)} %collective-permute-done.refs_1_, ...), custom_call_target="tpu_custom_call" | custom-call | tf_op jit(solution)/shard_map/partials/pallas_call | solution.py:121
  131.1 3.7 %grads.9 = (bf16[1024,8192]{1,0:T(8,128)(2,1)}, bf16[1024,8192]{1,0:T(8,128)(2,1)}, f32[1,8192]{1,0:T(1,128)S(1)}) custom-call(bf16[1024,256]{1,0:T(8,128)(2,1)S(1)} %get-tuple-element.73.refs_4_.refs_0_, bf16[1024,256]{1,0:T(8,128)(2,1)S(1)} %get-tuple-element.74.refs_1_, ...), custom_call_target="tpu_custom_call", output_to_operand_aliasing={{0}: (6, {}), {1}: (7, {}), {2}: (8, {})} | custom-call | tf_op jit(solution)/shard_map/grads/pallas_call | solution.py:248
  143.0 1.9 %collective-permute-done.38.refs_3_ = bf16[2,64,1024]{2,1,0:T(8,128)(2,1)S(1)} collective-permute-done((bf16[2,64,1024]{2,1,0:T(8,128)(2,1)S(1)}, bf16[2,64,1024]{2,1,0:T(8,128)(2,1)S(1)}, u32[]{:S(2)}, u32[]{:S(2)}) %collective-permute-start.38) | collective-permute-done | bytes 262176 | tf_op jit(solution)/shard_map/ppermute | solution.py:65
  154.7 3.0 %collective-permute-done.42.refs_5_ = bf16[2,64,1024]{2,1,0:T(8,128)(2,1)S(1)} collective-permute-done((bf16[2,64,1024]{2,1,0:T(8,128)(2,1)S(1)}, bf16[2,64,1024]{2,1,0:T(8,128)(2,1)S(1)}, u32[]{:S(2)}, u32[]{:S(2)}) %collective-permute-start.42) | collective-permute-done | bytes 262176 | tf_op jit(solution)/shard_map/ppermute | solution.py:65
  157.7 3.2 %grads.10 = (bf16[1024,8192]{1,0:T(8,128)(2,1)}, bf16[1024,8192]{1,0:T(8,128)(2,1)}, f32[1,8192]{1,0:T(1,128)S(1)}) custom-call(bf16[1024,256]{1,0:T(8,128)(2,1)S(1)} %get-tuple-element.73.refs_4_.refs_0_, bf16[1024,256]{1,0:T(8,128)(2,1)S(1)} %get-tuple-element.74.refs_1_, ...), custom_call_target="tpu_custom_call", output_to_operand_aliasing={{0}: (6, {}), {1}: (7, {}), {2}: (8, {})} | custom-call | tf_op jit(solution)/shard_map/grads/pallas_call | solution.py:248
  162.4 2.7 %grads.11 = (bf16[1024,8192]{1,0:T(8,128)(2,1)}, bf16[1024,8192]{1,0:T(8,128)(2,1)}, f32[1,8192]{1,0:T(1,128)}) custom-call(bf16[1024,256]{1,0:T(8,128)(2,1)S(1)} %get-tuple-element.73.refs_4_.refs_0_, bf16[1024,256]{1,0:T(8,128)(2,1)S(1)} %get-tuple-element.74.refs_1_, ...), custom_call_target="tpu_custom_call", output_to_operand_aliasing={{0}: (6, {}), {1}: (7, {}), {2}: (8, {})} | custom-call | tf_op jit(solution)/shard_map/grads/pallas_call | solution.py:248
  (83 shorter events, 58.8 us)
Async XLA Ops:
  6.6 11.1 %collective-permute-start.3 = (bf16[2,32,1024]{2,1,0:T(8,128)(2,1)S(1)}, bf16[2,32,1024]{2,1,0:T(8,128)(2,1)S(1)}, u32[]{:S(2)}, u32[]{:S(2)}) collective-permute-start(bf16[2,32,1024]{2,1,0:T(8,128)(2,1)S(1)} %pad_maximum_fusion.refs_0_), channel_id=1, source_target_pairs={{0,4},{1,5},{2,6},{3,7},{4,0},{5,1},{6,2},{7,3},{8,12},{9,13},{10,... | collective-permute-start | bytes 393224 | tf_op jit(solution)/shard_map/ppermute | solution.py:69
  6.6 11.1 %collective-permute-start.1 = (bf16[2,32,1024]{2,1,0:T(8,128)(2,1)S(1)}, bf16[2,32,1024]{2,1,0:T(8,128)(2,1)S(1)}, u32[]{:S(2)}, u32[]{:S(2)}) collective-permute-start(bf16[2,32,1024]{2,1,0:T(8,128)(2,1)S(1)} %pad_maximum_fusion.refs_0_), channel_id=1, source_target_pairs={{0,2},{1,3},{2,0},{3,1},{4,6},{5,7},{6,4},{7,5},{8,10},{9,11},{10,... | collective-permute-start | bytes 393224 | tf_op jit(solution)/shard_map/ppermute | solution.py:69
  7.3 10.9 %collective-permute-start = (bf16[2,32,1024]{2,1,0:T(8,128)(2,1)S(1)}, bf16[2,32,1024]{2,1,0:T(8,128)(2,1)S(1)}, u32[]{:S(2)}, u32[]{:S(2)}) collective-permute-start(bf16[2,32,1024]{2,1,0:T(8,128)(2,1)S(1)} %pad_maximum_fusion.refs_0_), channel_id=1, source_target_pairs={{0,1},{1,0},{2,3},{3,2},{4,5},{5,4},{6,7},{7,6},{8,9},{9,8},{10,11... | collective-permute-start | bytes 393224 | tf_op jit(solution)/shard_map/ppermute | solution.py:69
  23.3 12.0 %collective-permute-start.9 = (bf16[2,64,1536]{2,1,0:T(8,128)(2,1)S(1)}, bf16[2,64,1536]{2,1,0:T(8,128)(2,1)S(1)}, u32[]{:S(2)}, u32[]{:S(2)}) collective-permute-start(bf16[2,64,1536]{2,1,0:T(8,128)(2,1)S(1)} %get-tuple-element.78), channel_id=1, source_target_pairs={{0,16},{8,24},{16,0},{24,8},{1,17},{9,25},{17,1},{25,9},{2,18},{10... | collective-permute-start | bytes 1179656 | tf_op jit(solution)/shard_map/ppermute | solution.py:65
  24.9 12.0 %collective-permute-start.10 = (bf16[2,64,1536]{2,1,0:T(8,128)(2,1)S(1)}, bf16[2,64,1536]{2,1,0:T(8,128)(2,1)S(1)}, u32[]{:S(2)}, u32[]{:S(2)}) collective-permute-start(bf16[2,64,1536]{2,1,0:T(8,128)(2,1)S(1)} %get-tuple-element.80), channel_id=1, source_target_pairs={{0,8},{8,0},{16,24},{24,16},{1,9},{9,1},{17,25},{25,17},{2,10},{10... | collective-permute-start | bytes 1179656 | tf_op jit(solution)/shard_map/ppermute | solution.py:65
  30.5 13.2 %collective-permute-start.7 = (bf16[2,64,1536]{2,1,0:T(8,128)(2,1)S(1)}, bf16[2,64,1536]{2,1,0:T(8,128)(2,1)S(1)}, u32[]{:S(2)}, u32[]{:S(2)}) collective-permute-start(bf16[2,64,1536]{2,1,0:T(8,128)(2,1)S(1)} %get-tuple-element.75), channel_id=1, source_target_pairs={{0,16},{8,24},{16,0},{24,8},{1,17},{9,25},{17,1},{25,9},{2,18},{10... | collective-permute-start | bytes 1179656 | tf_op jit(solution)/shard_map/ppermute | solution.py:65
  31.1 14.2 %collective-permute-start.8 = (bf16[2,64,1536]{2,1,0:T(8,128)(2,1)S(1)}, bf16[2,64,1536]{2,1,0:T(8,128)(2,1)S(1)}, u32[]{:S(2)}, u32[]{:S(2)}) collective-permute-start(bf16[2,64,1536]{2,1,0:T(8,128)(2,1)S(1)} %get-tuple-element.77), channel_id=1, source_target_pairs={{0,8},{8,0},{16,24},{24,16},{1,9},{9,1},{17,25},{25,17},{2,10},{10... | collective-permute-start | bytes 1179656 | tf_op jit(solution)/shard_map/ppermute | solution.py:65
  37.3 14.9 %collective-permute-start.14 = (bf16[2,64,1536]{2,1,0:T(8,128)(2,1)S(1)}, bf16[2,64,1536]{2,1,0:T(8,128)(2,1)S(1)}, u32[]{:S(2)}, u32[]{:S(2)}) collective-permute-start(bf16[2,64,1536]{2,1,0:T(8,128)(2,1)S(1)} %get-tuple-element.84.refs_2_), channel_id=1, source_target_pairs={{0,16},{8,24},{16,0},{24,8},{1,17},{9,25},{17,1},{25,9},{2,18},{10... | collective-permute-start | bytes 1179656 | tf_op jit(solution)/shard_map/ppermute | solution.py:65
  37.9 15.9 %collective-permute-start.13 = (bf16[2,64,1536]{2,1,0:T(8,128)(2,1)S(1)}, bf16[2,64,1536]{2,1,0:T(8,128)(2,1)S(1)}, u32[]{:S(2)}, u32[]{:S(2)}) collective-permute-start(bf16[2,64,1536]{2,1,0:T(8,128)(2,1)S(1)} %get-tuple-element.81.refs_4_.refs_0_), channel_id=1, source_target_pairs={{0,8},{8,0},{16,24},{24,16},{1,9},{9,1},{17,25},{25,17},{2,10},{10... | collective-permute-start | bytes 1179656 | tf_op jit(solution)/shard_map/ppermute | solution.py:65
  45.7 14.9 %collective-permute-start.12 = (bf16[2,64,1536]{2,1,0:T(8,128)(2,1)S(1)}, bf16[2,64,1536]{2,1,0:T(8,128)(2,1)S(1)}, u32[]{:S(2)}, u32[]{:S(2)}) collective-permute-start(bf16[2,64,1536]{2,1,0:T(8,128)(2,1)S(1)} %get-tuple-element.83.refs_2_), channel_id=1, source_target_pairs={{0,16},{8,24},{16,0},{24,8},{1,17},{9,25},{17,1},{25,9},{2,18},{10... | collective-permute-start | bytes 1179656 | tf_op jit(solution)/shard_map/ppermute | solution.py:65
  46.3 15.9 %collective-permute-start.11 = (bf16[2,64,1536]{2,1,0:T(8,128)(2,1)S(1)}, bf16[2,64,1536]{2,1,0:T(8,128)(2,1)S(1)}, u32[]{:S(2)}, u32[]{:S(2)}) collective-permute-start(bf16[2,64,1536]{2,1,0:T(8,128)(2,1)S(1)} %get-tuple-element.82.refs_5_.refs_0_), channel_id=1, source_target_pairs={{0,8},{8,0},{16,24},{24,16},{1,9},{9,1},{17,25},{25,17},{2,10},{10... | collective-permute-start | bytes 1179656 | tf_op jit(solution)/shard_map/ppermute | solution.py:65
  54.8 16.2 %collective-permute-start.20 = (bf16[2,64,1536]{2,1,0:T(8,128)(2,1)S(1)}, bf16[2,64,1536]{2,1,0:T(8,128)(2,1)S(1)}, u32[]{:S(2)}, u32[]{:S(2)}) collective-permute-start(bf16[2,64,1536]{2,1,0:T(8,128)(2,1)S(1)} %get-tuple-element.92.refs_4_), channel_id=1, source_target_pairs={{0,8},{8,0},{16,24},{24,16},{1,9},{9,1},{17,25},{25,17},{2,10},{10... | collective-permute-start | bytes 1179656 | tf_op jit(solution)/shard_map/ppermute | solution.py:65
  56.3 15.8 %collective-permute-start.19 = (bf16[2,64,1536]{2,1,0:T(8,128)(2,1)S(1)}, bf16[2,64,1536]{2,1,0:T(8,128)(2,1)S(1)}, u32[]{:S(2)}, u32[]{:S(2)}) collective-permute-start(bf16[2,64,1536]{2,1,0:T(8,128)(2,1)S(1)} %get-tuple-element.85.refs_5_.refs_2_), channel_id=1, source_target_pairs={{0,16},{8,24},{16,0},{24,8},{1,17},{9,25},{17,1},{25,9},{2,18},{10... | collective-permute-start | bytes 1179656 | tf_op jit(solution)/shard_map/ppermute | solution.py:65
  63.2 17.3 %collective-permute-start.18 = (bf16[2,64,1536]{2,1,0:T(8,128)(2,1)S(1)}, bf16[2,64,1536]{2,1,0:T(8,128)(2,1)S(1)}, u32[]{:S(2)}, u32[]{:S(2)}) collective-permute-start(bf16[2,64,1536]{2,1,0:T(8,128)(2,1)S(1)} %get-tuple-element.91.refs_4_), channel_id=1, source_target_pairs={{0,8},{8,0},{16,24},{24,16},{1,9},{9,1},{17,25},{25,17},{2,10},{10... | collective-permute-start | bytes 1179656 | tf_op jit(solution)/shard_map/ppermute | solution.py:65
  64.8 16.6 %collective-permute-start.17 = (bf16[2,64,1536]{2,1,0:T(8,128)(2,1)S(1)}, bf16[2,64,1536]{2,1,0:T(8,128)(2,1)S(1)}, u32[]{:S(2)}, u32[]{:S(2)}) collective-permute-start(bf16[2,64,1536]{2,1,0:T(8,128)(2,1)S(1)} %get-tuple-element.86.refs_10_.refs_2_), channel_id=1, source_target_pairs={{0,16},{8,24},{16,0},{24,8},{1,17},{9,25},{17,1},{25,9},{2,18},{10... | collective-permute-start | bytes 1179656 | tf_op jit(solution)/shard_map/ppermute | solution.py:65
  69.4 16.5 %collective-permute-start.15 = (bf16[2,64,1536]{2,1,0:T(8,128)(2,1)S(1)}, bf16[2,64,1536]{2,1,0:T(8,128)(2,1)S(1)}, u32[]{:S(2)}, u32[]{:S(2)}) collective-permute-start(bf16[2,64,1536]{2,1,0:T(8,128)(2,1)S(1)} %get-tuple-element.88), channel_id=1, source_target_pairs={{0,16},{8,24},{16,0},{24,8},{1,17},{9,25},{17,1},{25,9},{2,18},{10... | collective-permute-start | bytes 1179656 | tf_op jit(solution)/shard_map/ppermute | solution.py:65
  71.0 16.5 %collective-permute-start.16 = (bf16[2,64,1536]{2,1,0:T(8,128)(2,1)S(1)}, bf16[2,64,1536]{2,1,0:T(8,128)(2,1)S(1)}, u32[]{:S(2)}, u32[]{:S(2)}) collective-permute-start(bf16[2,64,1536]{2,1,0:T(8,128)(2,1)S(1)} %get-tuple-element.90), channel_id=1, source_target_pairs={{0,8},{8,0},{16,24},{24,16},{1,9},{9,1},{17,25},{25,17},{2,10},{10... | collective-permute-start | bytes 1179656 | tf_op jit(solution)/shard_map/ppermute | solution.py:65
  79.9 14.4 %collective-permute-start.23 = (bf16[2,64,1536]{2,1,0:T(8,128)(2,1)S(1)}, bf16[2,64,1536]{2,1,0:T(8,128)(2,1)S(1)}, u32[]{:S(2)}, u32[]{:S(2)}) collective-permute-start(bf16[2,64,1536]{2,1,0:T(8,128)(2,1)S(1)} %get-tuple-element.100), channel_id=1, source_target_pairs={{0,16},{8,24},{16,0},{24,8},{1,17},{9,25},{17,1},{25,9},{2,18},{10... | collective-permute-start | bytes 1179656 | tf_op jit(solution)/shard_map/ppermute | solution.py:65
  80.5 15.4 %collective-permute-start.24 = (bf16[2,64,1536]{2,1,0:T(8,128)(2,1)S(1)}, bf16[2,64,1536]{2,1,0:T(8,128)(2,1)S(1)}, u32[]{:S(2)}, u32[]{:S(2)}) collective-permute-start(bf16[2,64,1536]{2,1,0:T(8,128)(2,1)S(1)} %get-tuple-element.102), channel_id=1, source_target_pairs={{0,8},{8,0},{16,24},{24,16},{1,9},{9,1},{17,25},{25,17},{2,10},{10... | collective-permute-start | bytes 1179656 | tf_op jit(solution)/shard_map/ppermute | solution.py:65
  87.9 14.9 %collective-permute-start.22 = (bf16[2,64,1536]{2,1,0:T(8,128)(2,1)S(1)}, bf16[2,64,1536]{2,1,0:T(8,128)(2,1)S(1)}, u32[]{:S(2)}, u32[]{:S(2)}) collective-permute-start(bf16[2,64,1536]{2,1,0:T(8,128)(2,1)S(1)} %get-tuple-element.99.refs_2_), channel_id=1, source_target_pairs={{0,16},{8,24},{16,0},{24,8},{1,17},{9,25},{17,1},{25,9},{2,18},{10... | collective-permute-start | bytes 1179656 | tf_op jit(solution)/shard_map/ppermute | solution.py:65
  88.4 15.9 %collective-permute-start.21 = (bf16[2,64,1536]{2,1,0:T(8,128)(2,1)S(1)}, bf16[2,64,1536]{2,1,0:T(8,128)(2,1)S(1)}, u32[]{:S(2)}, u32[]{:S(2)}) collective-permute-start(bf16[2,64,1536]{2,1,0:T(8,128)(2,1)S(1)} %get-tuple-element.98.refs_4_.refs_0_), channel_id=1, source_target_pairs={{0,8},{8,0},{16,24},{24,16},{1,9},{9,1},{17,25},{25,17},{2,10},{10... | collective-permute-start | bytes 1179656 | tf_op jit(solution)/shard_map/ppermute | solution.py:65
  96.3 14.9 %collective-permute-start.28 = (bf16[2,64,1536]{2,1,0:T(8,128)(2,1)S(1)}, bf16[2,64,1536]{2,1,0:T(8,128)(2,1)S(1)}, u32[]{:S(2)}, u32[]{:S(2)}) collective-permute-start(bf16[2,64,1536]{2,1,0:T(8,128)(2,1)S(1)} %get-tuple-element.108.refs_2_), channel_id=1, source_target_pairs={{0,16},{8,24},{16,0},{24,8},{1,17},{9,25},{17,1},{25,9},{2,18},{10... | collective-permute-start | bytes 1179656 | tf_op jit(solution)/shard_map/ppermute | solution.py:65
  96.9 15.9 %collective-permute-start.27 = (bf16[2,64,1536]{2,1,0:T(8,128)(2,1)S(1)}, bf16[2,64,1536]{2,1,0:T(8,128)(2,1)S(1)}, u32[]{:S(2)}, u32[]{:S(2)}) collective-permute-start(bf16[2,64,1536]{2,1,0:T(8,128)(2,1)S(1)} %get-tuple-element.103.refs_5_.refs_0_), channel_id=1, source_target_pairs={{0,8},{8,0},{16,24},{24,16},{1,9},{9,1},{17,25},{25,17},{2,10},{10... | collective-permute-start | bytes 1179656 | tf_op jit(solution)/shard_map/ppermute | solution.py:65
  105.3 15.8 %collective-permute-start.26 = (bf16[2,64,1536]{2,1,0:T(8,128)(2,1)S(1)}, bf16[2,64,1536]{2,1,0:T(8,128)(2,1)S(1)}, u32[]{:S(2)}, u32[]{:S(2)}) collective-permute-start(bf16[2,64,1536]{2,1,0:T(8,128)(2,1)S(1)} %get-tuple-element.105.refs_4_), channel_id=1, source_target_pairs={{0,8},{8,0},{16,24},{24,16},{1,9},{9,1},{17,25},{25,17},{2,10},{10... | collective-permute-start | bytes 1179656 | tf_op jit(solution)/shard_map/ppermute | solution.py:65
  106.9 15.8 %collective-permute-start.25 = (bf16[2,64,1536]{2,1,0:T(8,128)(2,1)S(1)}, bf16[2,64,1536]{2,1,0:T(8,128)(2,1)S(1)}, u32[]{:S(2)}, u32[]{:S(2)}) collective-permute-start(bf16[2,64,1536]{2,1,0:T(8,128)(2,1)S(1)} %get-tuple-element.104.refs_5_.refs_2_), channel_id=1, source_target_pairs={{0,16},{8,24},{16,0},{24,8},{1,17},{9,25},{17,1},{25,9},{2,18},{10... | collective-permute-start | bytes 1179656 | tf_op jit(solution)/shard_map/ppermute | solution.py:65
  114.0 16.5 %collective-permute-start.34 = (bf16[2,64,1536]{2,1,0:T(8,128)(2,1)S(1)}, bf16[2,64,1536]{2,1,0:T(8,128)(2,1)S(1)}, u32[]{:S(2)}, u32[]{:S(2)}) collective-permute-start(bf16[2,64,1536]{2,1,0:T(8,128)(2,1)S(1)} %get-tuple-element.119.refs_4_), channel_id=1, source_target_pairs={{0,8},{8,0},{16,24},{24,16},{1,9},{9,1},{17,25},{25,17},{2,10},{10... | collective-permute-start | bytes 1179656 | tf_op jit(solution)/shard_map/ppermute | solution.py:65
  115.5 15.6 %collective-permute-start.33 = (bf16[2,64,1536]{2,1,0:T(8,128)(2,1)S(1)}, bf16[2,64,1536]{2,1,0:T(8,128)(2,1)S(1)}, u32[]{:S(2)}, u32[]{:S(2)}) collective-permute-start(bf16[2,64,1536]{2,1,0:T(8,128)(2,1)S(1)} %get-tuple-element.109.refs_10_.refs_2_), channel_id=1, source_target_pairs={{0,16},{8,24},{16,0},{24,8},{1,17},{9,25},{17,1},{25,9},{2,18},{10... | collective-permute-start | bytes 1179656 | tf_op jit(solution)/shard_map/ppermute | solution.py:65
  119.5 15.3 %collective-permute-start.31 = (bf16[2,64,1024]{2,1,0:T(8,128)(2,1)S(1)}, bf16[2,64,1024]{2,1,0:T(8,128)(2,1)S(1)}, u32[]{:S(2)}, u32[]{:S(2)}) collective-permute-start(bf16[2,64,1024]{2,1,0:T(8,128)(2,1)S(1)} %get-tuple-element.116), channel_id=1, source_target_pairs={{0,16},{8,24},{16,0},{24,8},{1,17},{9,25},{17,1},{25,9},{2,18},{10... | collective-permute-start | bytes 786440 | tf_op jit(solution)/shard_map/ppermute | solution.py:65
  121.2 14.0 %collective-permute-start.32 = (bf16[2,64,1024]{2,1,0:T(8,128)(2,1)S(1)}, bf16[2,64,1024]{2,1,0:T(8,128)(2,1)S(1)}, u32[]{:S(2)}, u32[]{:S(2)}) collective-permute-start(bf16[2,64,1024]{2,1,0:T(8,128)(2,1)S(1)} %get-tuple-element.118), channel_id=1, source_target_pairs={{0,8},{8,0},{16,24},{24,16},{1,9},{9,1},{17,25},{25,17},{2,10},{10... | collective-permute-start | bytes 786440 | tf_op jit(solution)/shard_map/ppermute | solution.py:65
  130.5 10.3 %collective-permute-start.30 = (bf16[2,64,1024]{2,1,0:T(8,128)(2,1)S(1)}, bf16[2,64,1024]{2,1,0:T(8,128)(2,1)S(1)}, u32[]{:S(2)}, u32[]{:S(2)}) collective-permute-start(bf16[2,64,1024]{2,1,0:T(8,128)(2,1)S(1)} %get-tuple-element.115), channel_id=1, source_target_pairs={{0,8},{8,0},{16,24},{24,16},{1,9},{9,1},{17,25},{25,17},{2,10},{10... | collective-permute-start | bytes 786440 | tf_op jit(solution)/shard_map/ppermute | solution.py:65
  141.5 10.5 %collective-permute-start.35 = (bf16[2,64,1024]{2,1,0:T(8,128)(2,1)S(1)}, bf16[2,64,1024]{2,1,0:T(8,128)(2,1)S(1)}, u32[]{:S(2)}, u32[]{:S(2)}) collective-permute-start(bf16[2,64,1024]{2,1,0:T(8,128)(2,1)S(1)} %get-tuple-element.124.refs_5_.refs_0_), channel_id=1, source_target_pairs={{0,8},{8,0},{16,24},{24,16},{1,9},{9,1},{17,25},{25,17},{2,10},{10... | collective-permute-start | bytes 786440 | tf_op jit(solution)/shard_map/ppermute | solution.py:65
  147.0 10.7 %collective-permute-start.42 = (bf16[2,64,1024]{2,1,0:T(8,128)(2,1)S(1)}, bf16[2,64,1024]{2,1,0:T(8,128)(2,1)S(1)}, u32[]{:S(2)}, u32[]{:S(2)}) collective-permute-start(bf16[2,64,1024]{2,1,0:T(8,128)(2,1)S(1)} %get-tuple-element.130.refs_4_), channel_id=1, source_target_pairs={{0,8},{8,0},{16,24},{24,16},{1,9},{9,1},{17,25},{25,17},{2,10},{10... | collective-permute-start | bytes 786440 | tf_op jit(solution)/shard_map/ppermute | solution.py:65
  (12 other events, 112.5 us)

commit v3 on v2

--- a/solution.py
+++ b/solution.py
@@ -73,22 +73,42 @@
     keys = plan.keys()
     heights = [plan.block_rows(group) for group in groups]
     step = 16
-    first = base = 0
+    slabs = iter([(raw, at) for raw in raws for at in range(0, raw.shape[1], step)])
+    base = 0
     for group, block in zip(groups, heights):
         for start in range(0, group * plan.rows, step):
             stream, within = divmod(start, block * plan.blocks)
             index, off = divmod(within, block)
             row = (stream * plan.blocks + (index ^ keys[stream])) * sum(heights) + base + off
             row = pl.multiple_of(row, step)
-            piece, at = divmod(start, plan.rows)
+            raw, at = next(slabs)
             for q in range(2):
-                store(q, row, raws[first + piece][q, at : at + step, :])
-        first += group
+                store(q, row, raw[q, at : at + step, :])
         base += block
 
 
-def partial_kernel(plan, groups, waits, *refs):
-    count = sum(groups)
+def collect_kernel(waits, *refs):
+    out = refs[-1]
+    row = 0
+    for ref in refs[: -1 - waits]:
+        out[:, row : row + ref.shape[1]] = ref[...]
+        row += ref.shape[1]
+
+
+def collect(pieces, after):
+    rows = sum(piece.shape[1] for piece in pieces)
+    inside = pl.BlockSpec(memory_space=pltpu.VMEM)
+    return pl.pallas_call(
+        functools.partial(collect_kernel, len(after)),
+        in_specs=[inside] * len(pieces) + waiting(after),
+        out_specs=inside,
+        out_shape=jax.ShapeDtypeStruct((2, rows, pieces[0].shape[2]), BF16),
+        compiler_params=params(),
+        name="collect",
+    )(*pieces, *after)
+
+
+def partial_kernel(plan, groups, count, waits, *refs):
     raws, (enc_ref, dec_ref), outs, (tokens_ref,) = (
         refs[:count],
         refs[count : count + 2],
@@ -111,23 +131,64 @@
 
 
 def partials(plan, groups, raws, enc_weight, dec_weight, first, width, after):
-    tokens = len(raws) * plan.rows
+    tokens = sum(groups) * plan.rows
     outs = 4 if plan.blocks > 1 else 2
     block = divisor(math.gcd(first, width), 1024)
     base = first // block
     weight = pl.BlockSpec((plan.stack, block), lambda i: (0, base + i))
-    raw = pl.BlockSpec((2, plan.rows, plan.stack), lambda i: (0, 0, 0))
+    inputs = [pl.BlockSpec(raw.shape, lambda i: (0, 0, 0)) for raw in raws]
     out = pl.BlockSpec((2, tokens // outs, block), lambda i: (0, 0, i))
     return pl.pallas_call(
-        functools.partial(partial_kernel, plan, groups, len(after)),
+        functools.partial(partial_kernel, plan, groups, len(raws), len(after)),
         grid=(width // block,),
-        in_specs=[raw] * len(raws) + [weight] * 2 + waiting(after),
+        in_specs=inputs + [weight] * 2 + waiting(after),
         out_specs=[out] * outs,
         out_shape=[jax.ShapeDtypeStruct((2, tokens // outs, width), BF16)] * outs,
         scratch_shapes=[pltpu.VMEM((2, tokens, plan.stack), BF16)],
         compiler_params=params(),
         name="partials",
     )(*raws, enc_weight, dec_weight, *after)
+
+
+def joined_kernel(waits, *refs):
+    outs = refs[8 + waits :]
+    pieces = len(outs) // 2
+    for stream in range(2):
+        base = 0
+        for kept, got in (refs[4 * stream : 4 * stream + 2], refs[4 * stream + 2 : 4 * stream + 4]):
+            total = kept[...].astype(F32) + got[...].astype(F32)
+            rows = total.shape[1] // pieces
+            for i in range(pieces):
+                part = total[:, i * rows : (i + 1) * rows]
+                outs[stream * pieces + i][:, base : base + rows] = part.astype(BF16)
+            base += rows
+
+
+def joined(plan, near, far, skip, after):
+    pieces = plan.blocks // 2
+    width = far[0][0].shape[2]
+    block = divisor(math.gcd(skip, width), 1024)
+    base = skip // block
+    operands, specs = [], []
+    for stream in range(2):
+        for pair, start in ((near[stream], base), (far[stream], 0)):
+            for array in pair:
+                operands.append(array)
+                specs.append(
+                    pl.BlockSpec(
+                        (2, array.shape[1], block), lambda i, start=start: (0, 0, start + i)
+                    )
+                )
+    rows = (near[0][0].shape[1] + far[0][0].shape[1]) // pieces
+    return pl.pallas_call(
+        functools.partial(joined_kernel, len(after)),
+        grid=(width // block,),
+        in_specs=specs + waiting(after),
+        out_specs=[pl.BlockSpec((2, rows, block), lambda i: (0, 0, i))] * (2 * pieces),
+        out_shape=[jax.ShapeDtypeStruct((2, rows, width), BF16)] * (2 * pieces),
+        compiler_params=params(),
+        name="joined",
+    )(*operands, *after)
 
 
 def add_kernel(pieces, waits, *refs):
@@ -185,8 +246,8 @@
     )(mine[0], other[0], mine[1], other[1], bias, *after)
 
 
-def turn_kernel(plan, groups, waits, *refs):
-    raws, outs, scratch = refs[: sum(groups)], refs[sum(groups) + waits : -1], refs[-1]
+def turn_kernel(plan, groups, count, waits, *refs):
+    raws, outs, scratch = refs[:count], refs[count + waits : -1], refs[-1]
 
     def store(q, row, values):
         scratch[q, pl.ds(row, 16), :] = values
@@ -197,10 +258,10 @@
 
 
 def turned(plan, groups, raws, after):
-    tokens = len(raws) * plan.rows
+    tokens = sum(groups) * plan.rows
     whole = pl.BlockSpec(memory_space=pltpu.VMEM)
     return pl.pallas_call(
-        functools.partial(turn_kernel, plan, groups, len(after)),
+        functools.partial(turn_kernel, plan, groups, len(raws), len(after)),
         in_specs=[whole] * len(raws) + waiting(after),
         out_specs=[whole] * 2,
         out_shape=[jax.ShapeDtypeStruct((plan.stack, tokens), BF16)] * 2,
@@ -272,17 +333,19 @@
         near, far = plan.near, plan.peers - plan.near
         heights = [plan.block_rows(near), plan.block_rows(far)]
         self.groups = {"near": [near], "far": [far], "all": [near, far]}[which]
-        self.skip = plan.near if which == "far" else 0
         base = heights[0] if which == "far" else 0
         self.rows = [
             [(s * plan.blocks + j) * sum(heights) + base for j in range(plan.blocks)]
             for s in range(2)
         ]
 
-    def start(self, raws, enc_weight, dec_weight, after):
+    def start(self, raws, enc_weight, dec_weight, early, after):
         plan = self.plan
-        raws = raws[self.skip : self.skip + sum(self.groups)]
-        outs = partials(plan, self.groups, raws, enc_weight, dec_weight, self.first, self.width, after)
+        self.early = early
+        groups = self.groups
+        if early is not None:
+            groups, raws = groups[1:], raws[plan.near :]
+        outs = partials(plan, groups, raws, enc_weight, dec_weight, self.first, self.width, after)
         self.level = 0
         if plan.blocks > 1:
             self.kept = [outs[0], outs[2]]
@@ -300,7 +363,12 @@
         last = self.plan.bits - 1
         while self.level <= last:
             pieces = 2 if self.level < last else 1
-            cut = add(self.plan, self.kept, self.got, pieces, after)
+            if self.level == 1 and self.early is not None:
+                near = list(zip(self.early.kept, self.early.got))
+                far = list(zip(self.kept, self.got))
+                cut = joined(self.plan, near, far, self.first - self.early.first, after)
+            else:
+                cut = add(self.plan, self.kept, self.got, pieces, after)
             after = [cut[0]]
             if pieces == 2:
                 self.kept = [cut[0], cut[2]]
@@ -331,6 +399,7 @@
     "G5",
 )
 CHAIN = True
+AHEAD = 2
 
 
 def per_device(plan, residuals, errors, enc_weight, dec_weight, enc_bias):
@@ -339,12 +408,19 @@
     bias = enc_bias.reshape(1, feats)
     own = jnp.stack([residuals, errors])
     raws = [own] + [plan.peer(own, m) for m in range(1, plan.near)]
-    for m in range(plan.near, plan.peers, 2):
-        came = plan.peer(own, m)
-        raws += [came, plan.peer(came, 1)]
+    far = [plan.peer(own, m) for m in range(plan.near, plan.peers, 2)]
 
     pieces = [Piece(plan, which, first * unit, width * unit) for which, first, width in PIECES]
     result, tokens, chain = [], {}, []
+    early = None
+    if AHEAD and plan.bits > 1 and plan.near < plan.peers:
+        ahead = pieces[:AHEAD]
+        width = sum(piece.width for piece in ahead)
+        early = Piece(plan, "near", ahead[0].first, width)
+        chain = [early.start(raws, enc_weight, dec_weight, None, [])]
+    if far:
+        mine = collect(far, chain)
+        raws += [mine, plan.peer(mine, 1)]
     for entry in ORDER:
         op, *behind = entry.split("<")
         step, index = op[0], int(op[1:])
@@ -355,7 +431,12 @@
             else:
                 after.append(tokens[name])
         if step == "P":
-            token = pieces[index].start(raws, enc_weight, dec_weight, after)
+            covers = early is not None and index < AHEAD
+            if covers and index == AHEAD - 1:
+                after = after + early.got
+            token = pieces[index].start(
+                raws, enc_weight, dec_weight, early if covers else None, after
+            )
         elif step == "A":
             token = pieces[index].add(after)
         elif step == "N":

time: 165 us -> 162 us (0.982)
  waiting for transfers between devices: 66.8 us -> 49 us
  starting transfers between devices: 44.2 us -> 52.6 us
  Pallas kernels: 51.8 us -> 57.5 us
    ppermute x36 -> x38, waiting for transfers between devices: 55.3 us -> 44.3 us  [swap(): return lax.ppermute(array, 'layer', pairs)]
    ppermute x36 -> x38, starting transfers between devices: 37.9 us -> 46.7 us  [swap(): return lax.ppermute(array, 'layer', pairs)]
    ppermute x7 -> x5, waiting for transfers between devices: 11.4 us -> 4.68 us  [peer(): return lax.ppermute(array, 'feat', pairs)]
    pallas_call x7 -> x11, Pallas kernels: 23.8 us -> 30.3 us  [the longest x7 29 us: partials(): pl.pallas_call(functools.partial(partial_kernel, plan, groups, len(raws),...]
    ppermute x7 -> x5, starting transfers between devices: 6.27 us -> 5.91 us  [peer(): return lax.ppermute(array, 'feat', pairs)]
  transfers between devices with their start and end apart: 43 -> 43, of which waited for: 29 -> 27; matrix products, arithmetic and copies ran while one was open for 0% -> 0% of each run, Pallas kernels for 27% -> 34%
where the time goes in v3:
time: 162 us; the launch traced here: 161 us
  Pallas kernels  57.5 us (35%)
  starting transfers between devices  52.6 us (32%)
  waiting for transfers between devices  49 us (30%)
    ppermute x38, starting transfers between devices, swap(): return lax.ppermute(array, 'layer', pairs)  46.7 us
    ppermute x38, waiting for transfers between devices, swap(): return lax.ppermute(array, 'layer', pairs)  44.3 us
    pallas_call x7, Pallas kernels, partials(): pl.pallas_call(functools.partial(partial_kernel, plan, groups, len(raws),...  29 us
    pallas_call x6, Pallas kernels, grads(): pl.pallas_call(functools.partial(grads_kernel, [rows for _, rows, _ in he...  20.8 us
    ppermute x5, starting transfers between devices, peer(): return lax.ppermute(array, 'feat', pairs)  5.91 us
    pallas_call x6, Pallas kernels, gate(): pl.pallas_call(functools.partial(gate_kernel, len(after)), grid=(width //...  5.36 us
    ppermute x5, waiting for transfers between devices, peer(): return lax.ppermute(array, 'feat', pairs)  4.68 us
  transfers between devices with their start and end apart: 43, of which 27 were waited for; matrix products, arithmetic and copies ran while one was open for 0% of the time, Pallas kernels for 34%

profile of v3, /device:TPU:0, one launch (start us, length us, event | category | flops | bytes accessed | tf_op | source)
XLA Modules:
  0.0 161.4 jit_solution(6445066007285335396)
XLA Ops:
  2.0 4.7 %collective-permute-start.3 = (bf16[2,32,1024]{2,1,0:T(8,128)(2,1)S(1)}, bf16[2,32,1024]{2,1,0:T(8,128)(2,1)S(1)}, u32[]{:S(2)}, u32[]{:S(2)}) collective-permute-start(bf16[2,32,1024]{2,1,0:T(8,128)(2,1)S(1)} %pad_maximum_fusion.refs_0_), channel_id=1, source_target_pairs={{0,6},{1,7},{2,4},{3,5},{4,2},{5,3},{6,0},{7,1},{8,14},{9,15},{10,... | collective-permute-start | bytes 393224 | tf_op jit(solution)/shard_map/ppermute | solution.py:69
  7.4 6.3 %partials.7 = (bf16[2,16,3072]{2,1,0:T(8,128)(2,1)S(1)}, bf16[2,16,3072]{2,1,0:T(8,128)(2,1)S(1)}, bf16[2,16,3072]{2,1,0:T(8,128)(2,1)S(1)}, bf16[2,16,3072]{2,1,0:T(8,128)(2,1)S(1)}) custom-call(bf16[2,32,1024]{2,1,0:T(8,128)(2,1)S(1)} %pad_maximum_fusion.refs_0_, bf16[2,32,1024]{2,1,0:T(8,128)(2,1)S(1)} %collective-permute-done.refs_1_, ...), custom_call_target="tpu_custom_call" | custom-call | tf_op jit(solution)/shard_map/partials/pallas_call | solution.py:141
  13.7 4.7 %collective-permute-done.2.refs_1_ = bf16[2,32,1024]{2,1,0:T(8,128)(2,1)S(1)} collective-permute-done((bf16[2,32,1024]{2,1,0:T(8,128)(2,1)S(1)}, bf16[2,32,1024]{2,1,0:T(8,128)(2,1)S(1)}, u32[]{:S(2)}, u32[]{:S(2)}) %collective-permute-start.2) | collective-permute-done | bytes 131104 | tf_op jit(solution)/shard_map/ppermute | solution.py:69
  18.5 1.6 collective-permute-start.5
  21.6 3.7 %partials.8 = (bf16[2,48,1536]{2,1,0:T(8,128)(2,1)S(1)}, bf16[2,48,1536]{2,1,0:T(8,128)(2,1)S(1)}, bf16[2,48,1536]{2,1,0:T(8,128)(2,1)S(1)}, bf16[2,48,1536]{2,1,0:T(8,128)(2,1)S(1)}) custom-call(bf16[2,96,1024]{2,1,0:T(8,128)(2,1)S(1)} %collect.1.refs_0_.refs_2_, bf16[2,96,1024]{2,1,0:T(8,128)(2,1)S(1)} %collective-permute-done.4.refs_1_.refs_3_, ...), custom_call_target="tpu_custom_call" | custom-call | tf_op jit(solution)/shard_map/partials/pallas_call | solution.py:141
  27.1 3.7 %partials.9 = (bf16[2,48,1536]{2,1,0:T(8,128)(2,1)S(1)}, bf16[2,48,1536]{2,1,0:T(8,128)(2,1)S(1)}, bf16[2,48,1536]{2,1,0:T(8,128)(2,1)S(1)}, bf16[2,48,1536]{2,1,0:T(8,128)(2,1)S(1)}) custom-call(bf16[2,96,1024]{2,1,0:T(8,128)(2,1)S(1)} %collect.1.refs_0_.refs_2_, bf16[2,96,1024]{2,1,0:T(8,128)(2,1)S(1)} %collective-permute-done.4.refs_1_.refs_3_, ...), custom_call_target="tpu_custom_call" | custom-call | tf_op jit(solution)/shard_map/partials/pallas_call | solution.py:141
  33.7 1.6 collective-permute-done.9.refs_3_
  35.8 1.7 %collective-permute-start.14 = (bf16[2,64,1536]{2,1,0:T(8,128)(2,1)S(1)}, bf16[2,64,1536]{2,1,0:T(8,128)(2,1)S(1)}, u32[]{:S(2)}, u32[]{:S(2)}) collective-permute-start(bf16[2,64,1536]{2,1,0:T(8,128)(2,1)S(1)} %get-tuple-element.92.refs_2_), channel_id=1, source_target_pairs={{0,16},{8,24},{16,0},{24,8},{1,17},{9,25},{17,1},{25,9},{2,18},{10... | collective-permute-start | bytes 1179656 | tf_op jit(solution)/shard_map/ppermute | solution.py:65
  37.5 4.1 %collective-permute-done.7.refs_3_ = bf16[2,48,1536]{2,1,0:T(8,128)(2,1)S(1)} collective-permute-done((bf16[2,48,1536]{2,1,0:T(8,128)(2,1)S(1)}, bf16[2,48,1536]{2,1,0:T(8,128)(2,1)S(1)}, u32[]{:S(2)}, u32[]{:S(2)}) %collective-permute-start.7) | collective-permute-done | bytes 294944 | tf_op jit(solution)/shard_map/ppermute | solution.py:65
  42.2 1.7 %collective-permute-start.12 = (bf16[2,64,1536]{2,1,0:T(8,128)(2,1)S(1)}, bf16[2,64,1536]{2,1,0:T(8,128)(2,1)S(1)}, u32[]{:S(2)}, u32[]{:S(2)}) collective-permute-start(bf16[2,64,1536]{2,1,0:T(8,128)(2,1)S(1)} %get-tuple-element.91.refs_2_), channel_id=1, source_target_pairs={{0,16},{8,24},{16,0},{24,8},{1,17},{9,25},{17,1},{25,9},{2,18},{10... | collective-permute-start | bytes 1179656 | tf_op jit(solution)/shard_map/ppermute | solution.py:65
  44.8 5.2 %collective-permute-done.14.refs_3_ = bf16[2,64,1536]{2,1,0:T(8,128)(2,1)S(1)} collective-permute-done((bf16[2,64,1536]{2,1,0:T(8,128)(2,1)S(1)}, bf16[2,64,1536]{2,1,0:T(8,128)(2,1)S(1)}, u32[]{:S(2)}, u32[]{:S(2)}) %collective-permute-start.14) | collective-permute-done | bytes 393248 | tf_op jit(solution)/shard_map/ppermute | solution.py:65
  53.9 4.6 %collective-permute-done.12.refs_3_ = bf16[2,64,1536]{2,1,0:T(8,128)(2,1)S(1)} collective-permute-done((bf16[2,64,1536]{2,1,0:T(8,128)(2,1)S(1)}, bf16[2,64,1536]{2,1,0:T(8,128)(2,1)S(1)}, u32[]{:S(2)}, u32[]{:S(2)}) %collective-permute-start.12) | collective-permute-done | bytes 393248 | tf_op jit(solution)/shard_map/ppermute | solution.py:65
  62.3 4.1 %partials.10 = (bf16[2,64,1536]{2,1,0:T(8,128)(2,1)S(1)}, bf16[2,64,1536]{2,1,0:T(8,128)(2,1)S(1)}, bf16[2,64,1536]{2,1,0:T(8,128)(2,1)S(1)}, bf16[2,64,1536]{2,1,0:T(8,128)(2,1)S(1)}) custom-call(bf16[2,32,1024]{2,1,0:T(8,128)(2,1)S(1)} %pad_maximum_fusion.refs_0_, bf16[2,32,1024]{2,1,0:T(8,128)(2,1)S(1)} %collective-permute-done.refs_1_, ...), custom_call_target="tpu_custom_call" | custom-call | tf_op jit(solution)/shard_map/partials/pallas_call | solution.py:141
  68.5 3.7 %grads.6 = (bf16[1024,8192]{1,0:T(8,128)(2,1)}, bf16[1024,8192]{1,0:T(8,128)(2,1)}, f32[1,8192]{1,0:T(1,128)S(1)}) custom-call(bf16[1024,256]{1,0:T(8,128)(2,1)S(1)} %get-tuple-element.80.refs_8_.refs_0_, bf16[1024,256]{1,0:T(8,128)(2,1)S(1)} %get-tuple-element.81.refs_1_, bf16[2,64,1536]{2,1,0:T(8,128)(2,1)S(1)} %get-tuple-element.93.refs_5_.refs_2_, ...), custom_call_target="tpu_custom_call" | custom-call | tf_op jit(solution)/shard_map/grads/pallas_call | solution.py:309
  72.2 4.1 %partials.11 = (bf16[2,64,1536]{2,1,0:T(8,128)(2,1)S(1)}, bf16[2,64,1536]{2,1,0:T(8,128)(2,1)S(1)}, bf16[2,64,1536]{2,1,0:T(8,128)(2,1)S(1)}, bf16[2,64,1536]{2,1,0:T(8,128)(2,1)S(1)}) custom-call(bf16[2,32,1024]{2,1,0:T(8,128)(2,1)S(1)} %pad_maximum_fusion.refs_0_, bf16[2,32,1024]{2,1,0:T(8,128)(2,1)S(1)} %collective-permute-done.refs_1_, ...), custom_call_target="tpu_custom_call" | custom-call | tf_op jit(solution)/shard_map/partials/pallas_call | solution.py:141
  78.5 3.7 %grads.7 = (bf16[1024,8192]{1,0:T(8,128)(2,1)}, bf16[1024,8192]{1,0:T(8,128)(2,1)}, f32[1,8192]{1,0:T(1,128)S(1)}) custom-call(bf16[1024,256]{1,0:T(8,128)(2,1)S(1)} %get-tuple-element.80.refs_8_.refs_0_, bf16[1024,256]{1,0:T(8,128)(2,1)S(1)} %get-tuple-element.81.refs_1_, ...), custom_call_target="tpu_custom_call", output_to_operand_aliasing={{0}: (6, {}), {1}: (7, {}), {2}: (8, {})} | custom-call | tf_op jit(solution)/shard_map/grads/pallas_call | solution.py:309
  84.3 1.7 %collective-permute-start.22 = (bf16[2,64,1536]{2,1,0:T(8,128)(2,1)S(1)}, bf16[2,64,1536]{2,1,0:T(8,128)(2,1)S(1)}, u32[]{:S(2)}, u32[]{:S(2)}) collective-permute-start(bf16[2,64,1536]{2,1,0:T(8,128)(2,1)S(1)} %get-tuple-element.107.refs_2_), channel_id=1, source_target_pairs={{0,16},{8,24},{16,0},{24,8},{1,17},{9,25},{17,1},{25,9},{2,18},{10... | collective-permute-start | bytes 1179656 | tf_op jit(solution)/shard_map/ppermute | solution.py:65
  86.9 5.2 %collective-permute-done.23.refs_1_ = bf16[2,64,1536]{2,1,0:T(8,128)(2,1)S(1)} collective-permute-done((bf16[2,64,1536]{2,1,0:T(8,128)(2,1)S(1)}, bf16[2,64,1536]{2,1,0:T(8,128)(2,1)S(1)}, u32[]{:S(2)}, u32[]{:S(2)}) %collective-permute-start.23) | collective-permute-done | bytes 393248 | tf_op jit(solution)/shard_map/ppermute | solution.py:65
  92.7 1.7 %collective-permute-start.28 = (bf16[2,64,1536]{2,1,0:T(8,128)(2,1)S(1)}, bf16[2,64,1536]{2,1,0:T(8,128)(2,1)S(1)}, u32[]{:S(2)}, u32[]{:S(2)}) collective-permute-start(bf16[2,64,1536]{2,1,0:T(8,128)(2,1)S(1)} %get-tuple-element.116.refs_2_), channel_id=1, source_target_pairs={{0,16},{8,24},{16,0},{24,8},{1,17},{9,25},{17,1},{25,9},{2,18},{10... | collective-permute-start | bytes 1179656 | tf_op jit(solution)/shard_map/ppermute | solution.py:65
  95.4 5.2 %collective-permute-done.22.refs_3_ = bf16[2,64,1536]{2,1,0:T(8,128)(2,1)S(1)} collective-permute-done((bf16[2,64,1536]{2,1,0:T(8,128)(2,1)S(1)}, bf16[2,64,1536]{2,1,0:T(8,128)(2,1)S(1)}, u32[]{:S(2)}, u32[]{:S(2)}) %collective-permute-start.22) | collective-permute-done | bytes 393248 | tf_op jit(solution)/shard_map/ppermute | solution.py:65
  104.4 4.6 %collective-permute-done.28.refs_3_ = bf16[2,64,1536]{2,1,0:T(8,128)(2,1)S(1)} collective-permute-done((bf16[2,64,1536]{2,1,0:T(8,128)(2,1)S(1)}, bf16[2,64,1536]{2,1,0:T(8,128)(2,1)S(1)}, u32[]{:S(2)}, u32[]{:S(2)}) %collective-permute-start.28) | collective-permute-done | bytes 393248 | tf_op jit(solution)/shard_map/ppermute | solution.py:65
  113.0 3.5 %partials.12 = (bf16[2,64,1024]{2,1,0:T(8,128)(2,1)S(1)}, bf16[2,64,1024]{2,1,0:T(8,128)(2,1)S(1)}, bf16[2,64,1024]{2,1,0:T(8,128)(2,1)S(1)}, bf16[2,64,1024]{2,1,0:T(8,128)(2,1)S(1)}) custom-call(bf16[2,32,1024]{2,1,0:T(8,128)(2,1)S(1)} %pad_maximum_fusion.refs_0_, bf16[2,32,1024]{2,1,0:T(8,128)(2,1)S(1)} %collective-permute-done.refs_1_, ...), custom_call_target="tpu_custom_call" | custom-call | tf_op jit(solution)/shard_map/partials/pallas_call | solution.py:141
  119.1 3.7 %grads.8 = (bf16[1024,8192]{1,0:T(8,128)(2,1)}, bf16[1024,8192]{1,0:T(8,128)(2,1)}, f32[1,8192]{1,0:T(1,128)S(1)}) custom-call(bf16[1024,256]{1,0:T(8,128)(2,1)S(1)} %get-tuple-element.80.refs_8_.refs_0_, bf16[1024,256]{1,0:T(8,128)(2,1)S(1)} %get-tuple-element.81.refs_1_, ...), custom_call_target="tpu_custom_call", output_to_operand_aliasing={{0}: (6, {}), {1}: (7, {}), {2}: (8, {})} | custom-call | tf_op jit(solution)/shard_map/grads/pallas_call | solution.py:309
  122.8 3.5 %partials.13 = (bf16[2,64,1024]{2,1,0:T(8,128)(2,1)S(1)}, bf16[2,64,1024]{2,1,0:T(8,128)(2,1)S(1)}, bf16[2,64,1024]{2,1,0:T(8,128)(2,1)S(1)}, bf16[2,64,1024]{2,1,0:T(8,128)(2,1)S(1)}) custom-call(bf16[2,32,1024]{2,1,0:T(8,128)(2,1)S(1)} %pad_maximum_fusion.refs_0_, bf16[2,32,1024]{2,1,0:T(8,128)(2,1)S(1)} %collective-permute-done.refs_1_, ...), custom_call_target="tpu_custom_call" | custom-call | tf_op jit(solution)/shard_map/partials/pallas_call | solution.py:141
  128.5 3.7 %grads.9 = (bf16[1024,8192]{1,0:T(8,128)(2,1)}, bf16[1024,8192]{1,0:T(8,128)(2,1)}, f32[1,8192]{1,0:T(1,128)S(1)}) custom-call(bf16[1024,256]{1,0:T(8,128)(2,1)S(1)} %get-tuple-element.80.refs_8_.refs_0_, bf16[1024,256]{1,0:T(8,128)(2,1)S(1)} %get-tuple-element.81.refs_1_, ...), custom_call_target="tpu_custom_call", output_to_operand_aliasing={{0}: (6, {}), {1}: (7, {}), {2}: (8, {})} | custom-call | tf_op jit(solution)/shard_map/grads/pallas_call | solution.py:309
  134.4 2.7 %collective-permute-done.29.refs_1_ = bf16[2,64,1024]{2,1,0:T(8,128)(2,1)S(1)} collective-permute-done((bf16[2,64,1024]{2,1,0:T(8,128)(2,1)S(1)}, bf16[2,64,1024]{2,1,0:T(8,128)(2,1)S(1)}, u32[]{:S(2)}, u32[]{:S(2)}) %collective-permute-start.29) | collective-permute-done | bytes 262176 | tf_op jit(solution)/shard_map/ppermute | solution.py:65
  137.3 1.7 %collective-permute-start.36 = (bf16[2,64,1024]{2,1,0:T(8,128)(2,1)S(1)}, bf16[2,64,1024]{2,1,0:T(8,128)(2,1)S(1)}, u32[]{:S(2)}, u32[]{:S(2)}) collective-permute-start(bf16[2,64,1024]{2,1,0:T(8,128)(2,1)S(1)} %get-tuple-element.133.refs_2_), channel_id=1, source_target_pairs={{0,16},{8,24},{16,0},{24,8},{1,17},{9,25},{17,1},{25,9},{2,18},{10... | collective-permute-start | bytes 786440 | tf_op jit(solution)/shard_map/ppermute | solution.py:65
  140.0 2.7 %collective-permute-done.38.refs_3_ = bf16[2,64,1024]{2,1,0:T(8,128)(2,1)S(1)} collective-permute-done((bf16[2,64,1024]{2,1,0:T(8,128)(2,1)S(1)}, bf16[2,64,1024]{2,1,0:T(8,128)(2,1)S(1)}, u32[]{:S(2)}, u32[]{:S(2)}) %collective-permute-start.38) | collective-permute-done | bytes 262176 | tf_op jit(solution)/shard_map/ppermute | solution.py:65
  146.1 2.3 %collective-permute-done.36.refs_3_ = bf16[2,64,1024]{2,1,0:T(8,128)(2,1)S(1)} collective-permute-done((bf16[2,64,1024]{2,1,0:T(8,128)(2,1)S(1)}, bf16[2,64,1024]{2,1,0:T(8,128)(2,1)S(1)}, u32[]{:S(2)}, u32[]{:S(2)}) %collective-permute-start.36) | collective-permute-done | bytes 262176 | tf_op jit(solution)/shard_map/ppermute | solution.py:65
  151.7 2.4 %collective-permute-done.42.refs_5_ = bf16[2,64,1024]{2,1,0:T(8,128)(2,1)S(1)} collective-permute-done((bf16[2,64,1024]{2,1,0:T(8,128)(2,1)S(1)}, bf16[2,64,1024]{2,1,0:T(8,128)(2,1)S(1)}, u32[]{:S(2)}, u32[]{:S(2)}) %collective-permute-start.42) | collective-permute-done | bytes 262176 | tf_op jit(solution)/shard_map/ppermute | solution.py:65
  154.2 3.2 %grads.10 = (bf16[1024,8192]{1,0:T(8,128)(2,1)}, bf16[1024,8192]{1,0:T(8,128)(2,1)}, f32[1,8192]{1,0:T(1,128)S(1)}) custom-call(bf16[1024,256]{1,0:T(8,128)(2,1)S(1)} %get-tuple-element.80.refs_8_.refs_0_, bf16[1024,256]{1,0:T(8,128)(2,1)S(1)} %get-tuple-element.81.refs_1_, ...), custom_call_target="tpu_custom_call", output_to_operand_aliasing={{0}: (6, {}), {1}: (7, {}), {2}: (8, {})} | custom-call | tf_op jit(solution)/shard_map/grads/pallas_call | solution.py:309
  158.7 2.7 %grads.11 = (bf16[1024,8192]{1,0:T(8,128)(2,1)}, bf16[1024,8192]{1,0:T(8,128)(2,1)}, f32[1,8192]{1,0:T(1,128)}) custom-call(bf16[1024,256]{1,0:T(8,128)(2,1)S(1)} %get-tuple-element.80.refs_8_.refs_0_, bf16[1024,256]{1,0:T(8,128)(2,1)S(1)} %get-tuple-element.81.refs_1_, ...), custom_call_target="tpu_custom_call", output_to_operand_aliasing={{0}: (6, {}), {1}: (7, {}), {2}: (8, {})} | custom-call | tf_op jit(solution)/shard_map/grads/pallas_call | solution.py:309
  (85 shorter events, 51.0 us)
Async XLA Ops:
  2.0 11.7 %collective-permute-start.3 = (bf16[2,32,1024]{2,1,0:T(8,128)(2,1)S(1)}, bf16[2,32,1024]{2,1,0:T(8,128)(2,1)S(1)}, u32[]{:S(2)}, u32[]{:S(2)}) collective-permute-start(bf16[2,32,1024]{2,1,0:T(8,128)(2,1)S(1)} %pad_maximum_fusion.refs_0_), channel_id=1, source_target_pairs={{0,6},{1,7},{2,4},{3,5},{4,2},{5,3},{6,0},{7,1},{8,14},{9,15},{10,... | collective-permute-start | bytes 393224 | tf_op jit(solution)/shard_map/ppermute | solution.py:69
  6.7 11.7 %collective-permute-start.2 = (bf16[2,32,1024]{2,1,0:T(8,128)(2,1)S(1)}, bf16[2,32,1024]{2,1,0:T(8,128)(2,1)S(1)}, u32[]{:S(2)}, u32[]{:S(2)}) collective-permute-start(bf16[2,32,1024]{2,1,0:T(8,128)(2,1)S(1)} %pad_maximum_fusion.refs_0_), channel_id=1, source_target_pairs={{0,4},{1,5},{2,6},{3,7},{4,0},{5,1},{6,2},{7,3},{8,12},{9,13},{10,... | collective-permute-start | bytes 393224 | tf_op jit(solution)/shard_map/ppermute | solution.py:69
  6.7 11.7 %collective-permute-start.1 = (bf16[2,32,1024]{2,1,0:T(8,128)(2,1)S(1)}, bf16[2,32,1024]{2,1,0:T(8,128)(2,1)S(1)}, u32[]{:S(2)}, u32[]{:S(2)}) collective-permute-start(bf16[2,32,1024]{2,1,0:T(8,128)(2,1)S(1)} %pad_maximum_fusion.refs_0_), channel_id=1, source_target_pairs={{0,2},{1,3},{2,0},{3,1},{4,6},{5,7},{6,4},{7,5},{8,10},{9,11},{10,... | collective-permute-start | bytes 393224 | tf_op jit(solution)/shard_map/ppermute | solution.py:69
  25.3 10.0 %collective-permute-start.9 = (bf16[2,48,1536]{2,1,0:T(8,128)(2,1)S(1)}, bf16[2,48,1536]{2,1,0:T(8,128)(2,1)S(1)}, u32[]{:S(2)}, u32[]{:S(2)}) collective-permute-start(bf16[2,48,1536]{2,1,0:T(8,128)(2,1)S(1)} %get-tuple-element.86), channel_id=1, source_target_pairs={{0,16},{8,24},{16,0},{24,8},{1,17},{9,25},{17,1},{25,9},{2,18},{10... | collective-permute-start | bytes 884744 | tf_op jit(solution)/shard_map/ppermute | solution.py:65
  30.8 10.8 %collective-permute-start.7 = (bf16[2,48,1536]{2,1,0:T(8,128)(2,1)S(1)}, bf16[2,48,1536]{2,1,0:T(8,128)(2,1)S(1)}, u32[]{:S(2)}, u32[]{:S(2)}) collective-permute-start(bf16[2,48,1536]{2,1,0:T(8,128)(2,1)S(1)} %get-tuple-element.82), channel_id=1, source_target_pairs={{0,16},{8,24},{16,0},{24,8},{1,17},{9,25},{17,1},{25,9},{2,18},{10... | collective-permute-start | bytes 884744 | tf_op jit(solution)/shard_map/ppermute | solution.py:65
  31.8 9.9 %collective-permute-start.8 = (bf16[2,48,1536]{2,1,0:T(8,128)(2,1)S(1)}, bf16[2,48,1536]{2,1,0:T(8,128)(2,1)S(1)}, u32[]{:S(2)}, u32[]{:S(2)}) collective-permute-start(bf16[2,48,1536]{2,1,0:T(8,128)(2,1)S(1)} %get-tuple-element.85), channel_id=1, source_target_pairs={{0,8},{8,0},{16,24},{24,16},{1,9},{9,1},{17,25},{25,17},{2,10},{10... | collective-permute-start | bytes 884744 | tf_op jit(solution)/shard_map/ppermute | solution.py:65
  35.8 14.3 %collective-permute-start.14 = (bf16[2,64,1536]{2,1,0:T(8,128)(2,1)S(1)}, bf16[2,64,1536]{2,1,0:T(8,128)(2,1)S(1)}, u32[]{:S(2)}, u32[]{:S(2)}) collective-permute-start(bf16[2,64,1536]{2,1,0:T(8,128)(2,1)S(1)} %get-tuple-element.92.refs_2_), channel_id=1, source_target_pairs={{0,16},{8,24},{16,0},{24,8},{1,17},{9,25},{17,1},{25,9},{2,18},{10... | collective-permute-start | bytes 1179656 | tf_op jit(solution)/shard_map/ppermute | solution.py:65
  37.5 12.6 %collective-permute-start.13 = (bf16[2,64,1536]{2,1,0:T(8,128)(2,1)S(1)}, bf16[2,64,1536]{2,1,0:T(8,128)(2,1)S(1)}, u32[]{:S(2)}, u32[]{:S(2)}) collective-permute-start(bf16[2,64,1536]{2,1,0:T(8,128)(2,1)S(1)} %get-tuple-element.89.refs_8_.refs_0_), channel_id=1, source_target_pairs={{0,8},{8,0},{16,24},{24,16},{1,9},{9,1},{17,25},{25,17},{2,10},{10... | collective-permute-start | bytes 1179656 | tf_op jit(solution)/shard_map/ppermute | solution.py:65
  42.2 16.3 %collective-permute-start.12 = (bf16[2,64,1536]{2,1,0:T(8,128)(2,1)S(1)}, bf16[2,64,1536]{2,1,0:T(8,128)(2,1)S(1)}, u32[]{:S(2)}, u32[]{:S(2)}) collective-permute-start(bf16[2,64,1536]{2,1,0:T(8,128)(2,1)S(1)} %get-tuple-element.91.refs_2_), channel_id=1, source_target_pairs={{0,16},{8,24},{16,0},{24,8},{1,17},{9,25},{17,1},{25,9},{2,18},{10... | collective-permute-start | bytes 1179656 | tf_op jit(solution)/shard_map/ppermute | solution.py:65
  43.8 14.7 %collective-permute-start.11 = (bf16[2,64,1536]{2,1,0:T(8,128)(2,1)S(1)}, bf16[2,64,1536]{2,1,0:T(8,128)(2,1)S(1)}, u32[]{:S(2)}, u32[]{:S(2)}) collective-permute-start(bf16[2,64,1536]{2,1,0:T(8,128)(2,1)S(1)} %get-tuple-element.90.refs_5_.refs_0_), channel_id=1, source_target_pairs={{0,8},{8,0},{16,24},{24,16},{1,9},{9,1},{17,25},{25,17},{2,10},{10... | collective-permute-start | bytes 1179656 | tf_op jit(solution)/shard_map/ppermute | solution.py:65
  51.2 16.2 %collective-permute-start.20 = (bf16[2,64,1536]{2,1,0:T(8,128)(2,1)S(1)}, bf16[2,64,1536]{2,1,0:T(8,128)(2,1)S(1)}, u32[]{:S(2)}, u32[]{:S(2)}) collective-permute-start(bf16[2,64,1536]{2,1,0:T(8,128)(2,1)S(1)} %get-tuple-element.100.refs_4_), channel_id=1, source_target_pairs={{0,8},{8,0},{16,24},{24,16},{1,9},{9,1},{17,25},{25,17},{2,10},{10... | collective-permute-start | bytes 1179656 | tf_op jit(solution)/shard_map/ppermute | solution.py:65
  52.7 15.8 %collective-permute-start.19 = (bf16[2,64,1536]{2,1,0:T(8,128)(2,1)S(1)}, bf16[2,64,1536]{2,1,0:T(8,128)(2,1)S(1)}, u32[]{:S(2)}, u32[]{:S(2)}) collective-permute-start(bf16[2,64,1536]{2,1,0:T(8,128)(2,1)S(1)} %get-tuple-element.93.refs_5_.refs_2_), channel_id=1, source_target_pairs={{0,16},{8,24},{16,0},{24,8},{1,17},{9,25},{17,1},{25,9},{2,18},{10... | collective-permute-start | bytes 1179656 | tf_op jit(solution)/shard_map/ppermute | solution.py:65
  59.6 17.9 %collective-permute-start.18 = (bf16[2,64,1536]{2,1,0:T(8,128)(2,1)S(1)}, bf16[2,64,1536]{2,1,0:T(8,128)(2,1)S(1)}, u32[]{:S(2)}, u32[]{:S(2)}) collective-permute-start(bf16[2,64,1536]{2,1,0:T(8,128)(2,1)S(1)} %get-tuple-element.99.refs_4_), channel_id=1, source_target_pairs={{0,8},{8,0},{16,24},{24,16},{1,9},{9,1},{17,25},{25,17},{2,10},{10... | collective-permute-start | bytes 1179656 | tf_op jit(solution)/shard_map/ppermute | solution.py:65
  61.2 17.4 %collective-permute-start.17 = (bf16[2,64,1536]{2,1,0:T(8,128)(2,1)S(1)}, bf16[2,64,1536]{2,1,0:T(8,128)(2,1)S(1)}, u32[]{:S(2)}, u32[]{:S(2)}) collective-permute-start(bf16[2,64,1536]{2,1,0:T(8,128)(2,1)S(1)} %get-tuple-element.94.refs_6_.refs_2_), channel_id=1, source_target_pairs={{0,16},{8,24},{16,0},{24,8},{1,17},{9,25},{17,1},{25,9},{2,18},{10... | collective-permute-start | bytes 1179656 | tf_op jit(solution)/shard_map/ppermute | solution.py:65
  66.4 17.3 %collective-permute-start.15 = (bf16[2,64,1536]{2,1,0:T(8,128)(2,1)S(1)}, bf16[2,64,1536]{2,1,0:T(8,128)(2,1)S(1)}, u32[]{:S(2)}, u32[]{:S(2)}) collective-permute-start(bf16[2,64,1536]{2,1,0:T(8,128)(2,1)S(1)} %get-tuple-element.96), channel_id=1, source_target_pairs={{0,16},{8,24},{16,0},{24,8},{1,17},{9,25},{17,1},{25,9},{2,18},{10... | collective-permute-start | bytes 1179656 | tf_op jit(solution)/shard_map/ppermute | solution.py:65
  67.3 16.5 %collective-permute-start.16 = (bf16[2,64,1536]{2,1,0:T(8,128)(2,1)S(1)}, bf16[2,64,1536]{2,1,0:T(8,128)(2,1)S(1)}, u32[]{:S(2)}, u32[]{:S(2)}) collective-permute-start(bf16[2,64,1536]{2,1,0:T(8,128)(2,1)S(1)} %get-tuple-element.98), channel_id=1, source_target_pairs={{0,8},{8,0},{16,24},{24,16},{1,9},{9,1},{17,25},{25,17},{2,10},{10... | collective-permute-start | bytes 1179656 | tf_op jit(solution)/shard_map/ppermute | solution.py:65
  76.3 15.8 %collective-permute-start.23 = (bf16[2,64,1536]{2,1,0:T(8,128)(2,1)S(1)}, bf16[2,64,1536]{2,1,0:T(8,128)(2,1)S(1)}, u32[]{:S(2)}, u32[]{:S(2)}) collective-permute-start(bf16[2,64,1536]{2,1,0:T(8,128)(2,1)S(1)} %get-tuple-element.108), channel_id=1, source_target_pairs={{0,16},{8,24},{16,0},{24,8},{1,17},{9,25},{17,1},{25,9},{2,18},{10... | collective-permute-start | bytes 1179656 | tf_op jit(solution)/shard_map/ppermute | solution.py:65
  77.5 14.8 %collective-permute-start.24 = (bf16[2,64,1536]{2,1,0:T(8,128)(2,1)S(1)}, bf16[2,64,1536]{2,1,0:T(8,128)(2,1)S(1)}, u32[]{:S(2)}, u32[]{:S(2)}) collective-permute-start(bf16[2,64,1536]{2,1,0:T(8,128)(2,1)S(1)} %get-tuple-element.110), channel_id=1, source_target_pairs={{0,8},{8,0},{16,24},{24,16},{1,9},{9,1},{17,25},{25,17},{2,10},{10... | collective-permute-start | bytes 1179656 | tf_op jit(solution)/shard_map/ppermute | solution.py:65
  84.3 16.3 %collective-permute-start.22 = (bf16[2,64,1536]{2,1,0:T(8,128)(2,1)S(1)}, bf16[2,64,1536]{2,1,0:T(8,128)(2,1)S(1)}, u32[]{:S(2)}, u32[]{:S(2)}) collective-permute-start(bf16[2,64,1536]{2,1,0:T(8,128)(2,1)S(1)} %get-tuple-element.107.refs_2_), channel_id=1, source_target_pairs={{0,16},{8,24},{16,0},{24,8},{1,17},{9,25},{17,1},{25,9},{2,18},{10... | collective-permute-start | bytes 1179656 | tf_op jit(solution)/shard_map/ppermute | solution.py:65
  85.9 14.8 %collective-permute-start.21 = (bf16[2,64,1536]{2,1,0:T(8,128)(2,1)S(1)}, bf16[2,64,1536]{2,1,0:T(8,128)(2,1)S(1)}, u32[]{:S(2)}, u32[]{:S(2)}) collective-permute-start(bf16[2,64,1536]{2,1,0:T(8,128)(2,1)S(1)} %get-tuple-element.106.refs_4_.refs_0_), channel_id=1, source_target_pairs={{0,8},{8,0},{16,24},{24,16},{1,9},{9,1},{17,25},{25,17},{2,10},{10... | collective-permute-start | bytes 1179656 | tf_op jit(solution)/shard_map/ppermute | solution.py:65
  92.7 16.3 %collective-permute-start.28 = (bf16[2,64,1536]{2,1,0:T(8,128)(2,1)S(1)}, bf16[2,64,1536]{2,1,0:T(8,128)(2,1)S(1)}, u32[]{:S(2)}, u32[]{:S(2)}) collective-permute-start(bf16[2,64,1536]{2,1,0:T(8,128)(2,1)S(1)} %get-tuple-element.116.refs_2_), channel_id=1, source_target_pairs={{0,16},{8,24},{16,0},{24,8},{1,17},{9,25},{17,1},{25,9},{2,18},{10... | collective-permute-start | bytes 1179656 | tf_op jit(solution)/shard_map/ppermute | solution.py:65
  94.4 14.8 %collective-permute-start.27 = (bf16[2,64,1536]{2,1,0:T(8,128)(2,1)S(1)}, bf16[2,64,1536]{2,1,0:T(8,128)(2,1)S(1)}, u32[]{:S(2)}, u32[]{:S(2)}) collective-permute-start(bf16[2,64,1536]{2,1,0:T(8,128)(2,1)S(1)} %get-tuple-element.111.refs_5_.refs_0_), channel_id=1, source_target_pairs={{0,8},{8,0},{16,24},{24,16},{1,9},{9,1},{17,25},{25,17},{2,10},{10... | collective-permute-start | bytes 1179656 | tf_op jit(solution)/shard_map/ppermute | solution.py:65
  101.7 15.8 %collective-permute-start.26 = (bf16[2,64,1536]{2,1,0:T(8,128)(2,1)S(1)}, bf16[2,64,1536]{2,1,0:T(8,128)(2,1)S(1)}, u32[]{:S(2)}, u32[]{:S(2)}) collective-permute-start(bf16[2,64,1536]{2,1,0:T(8,128)(2,1)S(1)} %get-tuple-element.113.refs_4_), channel_id=1, source_target_pairs={{0,8},{8,0},{16,24},{24,16},{1,9},{9,1},{17,25},{25,17},{2,10},{10... | collective-permute-start | bytes 1179656 | tf_op jit(solution)/shard_map/ppermute | solution.py:65
  103.3 15.8 %collective-permute-start.25 = (bf16[2,64,1536]{2,1,0:T(8,128)(2,1)S(1)}, bf16[2,64,1536]{2,1,0:T(8,128)(2,1)S(1)}, u32[]{:S(2)}, u32[]{:S(2)}) collective-permute-start(bf16[2,64,1536]{2,1,0:T(8,128)(2,1)S(1)} %get-tuple-element.112.refs_5_.refs_2_), channel_id=1, source_target_pairs={{0,16},{8,24},{16,0},{24,8},{1,17},{9,25},{17,1},{25,9},{2,18},{10... | collective-permute-start | bytes 1179656 | tf_op jit(solution)/shard_map/ppermute | solution.py:65
  110.3 17.2 %collective-permute-start.34 = (bf16[2,64,1536]{2,1,0:T(8,128)(2,1)S(1)}, bf16[2,64,1536]{2,1,0:T(8,128)(2,1)S(1)}, u32[]{:S(2)}, u32[]{:S(2)}) collective-permute-start(bf16[2,64,1536]{2,1,0:T(8,128)(2,1)S(1)} %get-tuple-element.127.refs_4_), channel_id=1, source_target_pairs={{0,8},{8,0},{16,24},{24,16},{1,9},{9,1},{17,25},{25,17},{2,10},{10... | collective-permute-start | bytes 1179656 | tf_op jit(solution)/shard_map/ppermute | solution.py:65
  111.9 16.6 %collective-permute-start.33 = (bf16[2,64,1536]{2,1,0:T(8,128)(2,1)S(1)}, bf16[2,64,1536]{2,1,0:T(8,128)(2,1)S(1)}, u32[]{:S(2)}, u32[]{:S(2)}) collective-permute-start(bf16[2,64,1536]{2,1,0:T(8,128)(2,1)S(1)} %get-tuple-element.117.refs_6_.refs_2_), channel_id=1, source_target_pairs={{0,16},{8,24},{16,0},{24,8},{1,17},{9,25},{17,1},{25,9},{2,18},{10... | collective-permute-start | bytes 1179656 | tf_op jit(solution)/shard_map/ppermute | solution.py:65
  116.6 15.7 %collective-permute-start.31 = (bf16[2,64,1024]{2,1,0:T(8,128)(2,1)S(1)}, bf16[2,64,1024]{2,1,0:T(8,128)(2,1)S(1)}, u32[]{:S(2)}, u32[]{:S(2)}) collective-permute-start(bf16[2,64,1024]{2,1,0:T(8,128)(2,1)S(1)} %get-tuple-element.124), channel_id=1, source_target_pairs={{0,16},{8,24},{16,0},{24,8},{1,17},{9,25},{17,1},{25,9},{2,18},{10... | collective-permute-start | bytes 786440 | tf_op jit(solution)/shard_map/ppermute | solution.py:65
  117.6 14.7 %collective-permute-start.32 = (bf16[2,64,1024]{2,1,0:T(8,128)(2,1)S(1)}, bf16[2,64,1024]{2,1,0:T(8,128)(2,1)S(1)}, u32[]{:S(2)}, u32[]{:S(2)}) collective-permute-start(bf16[2,64,1024]{2,1,0:T(8,128)(2,1)S(1)} %get-tuple-element.126), channel_id=1, source_target_pairs={{0,8},{8,0},{16,24},{24,16},{1,9},{9,1},{17,25},{25,17},{2,10},{10... | collective-permute-start | bytes 786440 | tf_op jit(solution)/shard_map/ppermute | solution.py:65
  126.3 10.8 %collective-permute-start.29 = (bf16[2,64,1024]{2,1,0:T(8,128)(2,1)S(1)}, bf16[2,64,1024]{2,1,0:T(8,128)(2,1)S(1)}, u32[]{:S(2)}, u32[]{:S(2)}) collective-permute-start(bf16[2,64,1024]{2,1,0:T(8,128)(2,1)S(1)} %get-tuple-element.121), channel_id=1, source_target_pairs={{0,16},{8,24},{16,0},{24,8},{1,17},{9,25},{17,1},{25,9},{2,18},{10... | collective-permute-start | bytes 786440 | tf_op jit(solution)/shard_map/ppermute | solution.py:65
  132.4 10.3 %collective-permute-start.38 = (bf16[2,64,1024]{2,1,0:T(8,128)(2,1)S(1)}, bf16[2,64,1024]{2,1,0:T(8,128)(2,1)S(1)}, u32[]{:S(2)}, u32[]{:S(2)}) collective-permute-start(bf16[2,64,1024]{2,1,0:T(8,128)(2,1)S(1)} %get-tuple-element.134.refs_2_), channel_id=1, source_target_pairs={{0,16},{8,24},{16,0},{24,8},{1,17},{9,25},{17,1},{25,9},{2,18},{10... | collective-permute-start | bytes 786440 | tf_op jit(solution)/shard_map/ppermute | solution.py:65
  137.3 11.0 %collective-permute-start.36 = (bf16[2,64,1024]{2,1,0:T(8,128)(2,1)S(1)}, bf16[2,64,1024]{2,1,0:T(8,128)(2,1)S(1)}, u32[]{:S(2)}, u32[]{:S(2)}) collective-permute-start(bf16[2,64,1024]{2,1,0:T(8,128)(2,1)S(1)} %get-tuple-element.133.refs_2_), channel_id=1, source_target_pairs={{0,16},{8,24},{16,0},{24,8},{1,17},{9,25},{17,1},{25,9},{2,18},{10... | collective-permute-start | bytes 786440 | tf_op jit(solution)/shard_map/ppermute | solution.py:65
  143.4 10.7 %collective-permute-start.42 = (bf16[2,64,1024]{2,1,0:T(8,128)(2,1)S(1)}, bf16[2,64,1024]{2,1,0:T(8,128)(2,1)S(1)}, u32[]{:S(2)}, u32[]{:S(2)}) collective-permute-start(bf16[2,64,1024]{2,1,0:T(8,128)(2,1)S(1)} %get-tuple-element.138.refs_4_), channel_id=1, source_target_pairs={{0,8},{8,0},{16,24},{24,16},{1,9},{9,1},{17,25},{25,17},{2,10},{10... | collective-permute-start | bytes 786440 | tf_op jit(solution)/shard_map/ppermute | solution.py:65
  (12 other events, 112.7 us)

commit v4 on v3

--- a/solution.py
+++ b/solution.py
@@ -127,12 +127,13 @@
     for q, weight in enumerate((enc_ref, dec_ref)):
         part = jnp.dot(tokens_ref[q], weight[...], preferred_element_type=F32)
         for i, out in enumerate(outs):
-            out[q] = part[i * rows : (i + 1) * rows].astype(BF16)
+            out[q] = part[i * rows : (i + 1) * rows].astype(out.dtype)
 
 
 def partials(plan, groups, raws, enc_weight, dec_weight, first, width, after):
     tokens = sum(groups) * plan.rows
     outs = 4 if plan.blocks > 1 else 2
+    kinds = (F32, BF16, F32, BF16) if plan.blocks > 1 else (BF16, BF16)
     block = divisor(math.gcd(first, width), 1024)
     base = first // block
     weight = pl.BlockSpec((plan.stack, block), lambda i: (0, base + i))
@@ -143,7 +144,7 @@
         grid=(width // block,),
         in_specs=inputs + [weight] * 2 + waiting(after),
         out_specs=[out] * outs,
-        out_shape=[jax.ShapeDtypeStruct((2, tokens // outs, width), BF16)] * outs,
+        out_shape=[jax.ShapeDtypeStruct((2, tokens // outs, width), kind) for kind in kinds],
         scratch_shapes=[pltpu.VMEM((2, tokens, plan.stack), BF16)],
         compiler_params=params(),
         name="partials",

time: 162 us -> 162 us (level)
  transfers between devices with their start and end apart: 43 -> 43, of which waited for: 27 -> 25; matrix products, arithmetic and copies ran while one was open for 0% -> 0% of each run, Pallas kernels for 34% -> 34%
where the time goes in v4:
time: 162 us; the launch traced here: 161 us
  Pallas kernels  57.6 us (36%)
  starting transfers between devices  52.5 us (32%)
  waiting for transfers between devices  49 us (30%)
    ppermute x38, starting transfers between devices, swap(): return lax.ppermute(array, 'layer', pairs)  46.6 us
    ppermute x38, waiting for transfers between devices, swap(): return lax.ppermute(array, 'layer', pairs)  44.4 us
    pallas_call x7, Pallas kernels, partials(): pl.pallas_call(functools.partial(partial_kernel, plan, groups, len(raws),...  29.1 us
    pallas_call x6, Pallas kernels, grads(): pl.pallas_call(functools.partial(grads_kernel, [rows for _, rows, _ in he...  20.8 us
    ppermute x5, starting transfers between devices, peer(): return lax.ppermute(array, 'feat', pairs)  5.91 us
    pallas_call x6, Pallas kernels, gate(): pl.pallas_call(functools.partial(gate_kernel, len(after)), grid=(width //...  5.36 us
    ppermute x5, waiting for transfers between devices, peer(): return lax.ppermute(array, 'feat', pairs)  4.68 us
  transfers between devices with their start and end apart: 43, of which 25 were waited for; matrix products, arithmetic and copies ran while one was open for 0% of the time, Pallas kernels for 34%

profile of v4, /device:TPU:0, one launch (start us, length us, event | category | flops | bytes accessed | tf_op | source)
XLA Modules:
  0.0 161.4 jit_solution(4721301584664821873)
XLA Ops:
  2.0 4.7 %collective-permute-start.3 = (bf16[2,32,1024]{2,1,0:T(8,128)(2,1)S(1)}, bf16[2,32,1024]{2,1,0:T(8,128)(2,1)S(1)}, u32[]{:S(2)}, u32[]{:S(2)}) collective-permute-start(bf16[2,32,1024]{2,1,0:T(8,128)(2,1)S(1)} %pad_maximum_fusion.refs_0_), channel_id=1, source_target_pairs={{0,6},{1,7},{2,4},{3,5},{4,2},{5,3},{6,0},{7,1},{8,14},{9,15},{10,... | collective-permute-start | bytes 393224 | tf_op jit(solution)/shard_map/ppermute | solution.py:69
  7.4 6.4 %partials.7 = (f32[2,16,3072]{2,1,0:T(8,128)S(1)}, bf16[2,16,3072]{2,1,0:T(8,128)(2,1)S(1)}, f32[2,16,3072]{2,1,0:T(8,128)S(1)}, bf16[2,16,3072]{2,1,0:T(8,128)(2,1)S(1)}) custom-call(bf16[2,32,1024]{2,1,0:T(8,128)(2,1)S(1)} %pad_maximum_fusion.refs_0_, bf16[2,32,1024]{2,1,0:T(8,128)(2,1)S(1)} %collective-permute-done.refs_1_, bf16[1024,8192]{1,0:T(8,128)(2,1)} %refs_4_.7, ...), custom_call_target="tpu_custom_call" | custom-call | tf_op jit(solution)/shard_map/partials/pallas_call | solution.py:142
  13.7 4.7 %collective-permute-done.2.refs_1_ = bf16[2,32,1024]{2,1,0:T(8,128)(2,1)S(1)} collective-permute-done((bf16[2,32,1024]{2,1,0:T(8,128)(2,1)S(1)}, bf16[2,32,1024]{2,1,0:T(8,128)(2,1)S(1)}, u32[]{:S(2)}, u32[]{:S(2)}) %collective-permute-start.2) | collective-permute-done | bytes 131104 | tf_op jit(solution)/shard_map/ppermute | solution.py:69
  18.5 1.6 collective-permute-start.5
  21.6 3.7 %partials.8 = (f32[2,48,1536]{2,1,0:T(8,128)S(1)}, bf16[2,48,1536]{2,1,0:T(8,128)(2,1)S(1)}, f32[2,48,1536]{2,1,0:T(8,128)S(1)}, bf16[2,48,1536]{2,1,0:T(8,128)(2,1)S(1)}) custom-call(bf16[2,96,1024]{2,1,0:T(8,128)(2,1)S(1)} %collect.1.refs_0_.refs_2_, bf16[2,96,1024]{2,1,0:T(8,128)(2,1)S(1)} %collective-permute-done.4.refs_1_.refs_3_, ...), custom_call_target="tpu_custom_call" | custom-call | tf_op jit(solution)/shard_map/partials/pallas_call | solution.py:142
  27.1 3.7 %partials.9 = (f32[2,48,1536]{2,1,0:T(8,128)S(1)}, bf16[2,48,1536]{2,1,0:T(8,128)(2,1)S(1)}, f32[2,48,1536]{2,1,0:T(8,128)S(1)}, bf16[2,48,1536]{2,1,0:T(8,128)(2,1)S(1)}) custom-call(bf16[2,96,1024]{2,1,0:T(8,128)(2,1)S(1)} %collect.1.refs_0_.refs_2_, bf16[2,96,1024]{2,1,0:T(8,128)(2,1)S(1)} %collective-permute-done.4.refs_1_.refs_3_, ...), custom_call_target="tpu_custom_call" | custom-call | tf_op jit(solution)/shard_map/partials/pallas_call | solution.py:142
  33.7 1.6 collective-permute-done.9.refs_3_
  35.8 1.8 %collective-permute-start.14 = (bf16[2,64,1536]{2,1,0:T(8,128)(2,1)S(1)}, bf16[2,64,1536]{2,1,0:T(8,128)(2,1)S(1)}, u32[]{:S(2)}, u32[]{:S(2)}) collective-permute-start(bf16[2,64,1536]{2,1,0:T(8,128)(2,1)S(1)} %get-tuple-element.92.refs_2_), channel_id=1, source_target_pairs={{0,16},{8,24},{16,0},{24,8},{1,17},{9,25},{17,1},{25,9},{2,18},{10... | collective-permute-start | bytes 1179656 | tf_op jit(solution)/shard_map/ppermute | solution.py:65
  37.5 4.1 %collective-permute-done.7.refs_3_ = bf16[2,48,1536]{2,1,0:T(8,128)(2,1)S(1)} collective-permute-done((bf16[2,48,1536]{2,1,0:T(8,128)(2,1)S(1)}, bf16[2,48,1536]{2,1,0:T(8,128)(2,1)S(1)}, u32[]{:S(2)}, u32[]{:S(2)}) %collective-permute-start.7) | collective-permute-done | bytes 294944 | tf_op jit(solution)/shard_map/ppermute | solution.py:65
  42.2 1.6 %collective-permute-start.12 = (bf16[2,64,1536]{2,1,0:T(8,128)(2,1)S(1)}, bf16[2,64,1536]{2,1,0:T(8,128)(2,1)S(1)}, u32[]{:S(2)}, u32[]{:S(2)}) collective-permute-start(bf16[2,64,1536]{2,1,0:T(8,128)(2,1)S(1)} %get-tuple-element.91.refs_2_), channel_id=1, source_target_pairs={{0,16},{8,24},{16,0},{24,8},{1,17},{9,25},{17,1},{25,9},{2,18},{10... | collective-permute-start | bytes 1179656 | tf_op jit(solution)/shard_map/ppermute | solution.py:65
  44.9 5.2 %collective-permute-done.14.refs_3_ = bf16[2,64,1536]{2,1,0:T(8,128)(2,1)S(1)} collective-permute-done((bf16[2,64,1536]{2,1,0:T(8,128)(2,1)S(1)}, bf16[2,64,1536]{2,1,0:T(8,128)(2,1)S(1)}, u32[]{:S(2)}, u32[]{:S(2)}) %collective-permute-start.14) | collective-permute-done | bytes 393248 | tf_op jit(solution)/shard_map/ppermute | solution.py:65
  53.9 4.6 %collective-permute-done.12.refs_3_ = bf16[2,64,1536]{2,1,0:T(8,128)(2,1)S(1)} collective-permute-done((bf16[2,64,1536]{2,1,0:T(8,128)(2,1)S(1)}, bf16[2,64,1536]{2,1,0:T(8,128)(2,1)S(1)}, u32[]{:S(2)}, u32[]{:S(2)}) %collective-permute-start.12) | collective-permute-done | bytes 393248 | tf_op jit(solution)/shard_map/ppermute | solution.py:65
  62.3 4.1 %partials.10 = (f32[2,64,1536]{2,1,0:T(8,128)S(1)}, bf16[2,64,1536]{2,1,0:T(8,128)(2,1)S(1)}, f32[2,64,1536]{2,1,0:T(8,128)S(1)}, bf16[2,64,1536]{2,1,0:T(8,128)(2,1)S(1)}) custom-call(bf16[2,32,1024]{2,1,0:T(8,128)(2,1)S(1)} %pad_maximum_fusion.refs_0_, bf16[2,32,1024]{2,1,0:T(8,128)(2,1)S(1)} %collective-permute-done.refs_1_, ...), custom_call_target="tpu_custom_call" | custom-call | tf_op jit(solution)/shard_map/partials/pallas_call | solution.py:142
  68.5 3.7 %grads.6 = (bf16[1024,8192]{1,0:T(8,128)(2,1)}, bf16[1024,8192]{1,0:T(8,128)(2,1)}, f32[1,8192]{1,0:T(1,128)S(1)}) custom-call(bf16[1024,256]{1,0:T(8,128)(2,1)S(1)} %get-tuple-element.80.refs_8_.refs_0_, bf16[1024,256]{1,0:T(8,128)(2,1)S(1)} %get-tuple-element.81.refs_1_, bf16[2,64,1536]{2,1,0:T(8,128)(2,1)S(1)} %get-tuple-element.93.refs_5_.refs_2_, ...), custom_call_target="tpu_custom_call" | custom-call | tf_op jit(solution)/shard_map/grads/pallas_call | solution.py:310
  72.2 4.1 %partials.11 = (f32[2,64,1536]{2,1,0:T(8,128)S(1)}, bf16[2,64,1536]{2,1,0:T(8,128)(2,1)S(1)}, f32[2,64,1536]{2,1,0:T(8,128)S(1)}, bf16[2,64,1536]{2,1,0:T(8,128)(2,1)S(1)}) custom-call(bf16[2,32,1024]{2,1,0:T(8,128)(2,1)S(1)} %pad_maximum_fusion.refs_0_, bf16[2,32,1024]{2,1,0:T(8,128)(2,1)S(1)} %collective-permute-done.refs_1_, ...), custom_call_target="tpu_custom_call" | custom-call | tf_op jit(solution)/shard_map/partials/pallas_call | solution.py:142
  78.6 3.7 %grads.7 = (bf16[1024,8192]{1,0:T(8,128)(2,1)}, bf16[1024,8192]{1,0:T(8,128)(2,1)}, f32[1,8192]{1,0:T(1,128)S(1)}) custom-call(bf16[1024,256]{1,0:T(8,128)(2,1)S(1)} %get-tuple-element.80.refs_8_.refs_0_, bf16[1024,256]{1,0:T(8,128)(2,1)S(1)} %get-tuple-element.81.refs_1_, ...), custom_call_target="tpu_custom_call", output_to_operand_aliasing={{0}: (6, {}), {1}: (7, {}), {2}: (8, {})} | custom-call | tf_op jit(solution)/shard_map/grads/pallas_call | solution.py:310
  84.3 1.6 %collective-permute-start.22 = (bf16[2,64,1536]{2,1,0:T(8,128)(2,1)S(1)}, bf16[2,64,1536]{2,1,0:T(8,128)(2,1)S(1)}, u32[]{:S(2)}, u32[]{:S(2)}) collective-permute-start(bf16[2,64,1536]{2,1,0:T(8,128)(2,1)S(1)} %get-tuple-element.107.refs_2_), channel_id=1, source_target_pairs={{0,16},{8,24},{16,0},{24,8},{1,17},{9,25},{17,1},{25,9},{2,18},{10... | collective-permute-start | bytes 1179656 | tf_op jit(solution)/shard_map/ppermute | solution.py:65
  87.0 5.2 %collective-permute-done.23.refs_1_ = bf16[2,64,1536]{2,1,0:T(8,128)(2,1)S(1)} collective-permute-done((bf16[2,64,1536]{2,1,0:T(8,128)(2,1)S(1)}, bf16[2,64,1536]{2,1,0:T(8,128)(2,1)S(1)}, u32[]{:S(2)}, u32[]{:S(2)}) %collective-permute-start.23) | collective-permute-done | bytes 393248 | tf_op jit(solution)/shard_map/ppermute | solution.py:65
  92.7 1.6 %collective-permute-start.28 = (bf16[2,64,1536]{2,1,0:T(8,128)(2,1)S(1)}, bf16[2,64,1536]{2,1,0:T(8,128)(2,1)S(1)}, u32[]{:S(2)}, u32[]{:S(2)}) collective-permute-start(bf16[2,64,1536]{2,1,0:T(8,128)(2,1)S(1)} %get-tuple-element.116.refs_2_), channel_id=1, source_target_pairs={{0,16},{8,24},{16,0},{24,8},{1,17},{9,25},{17,1},{25,9},{2,18},{10... | collective-permute-start | bytes 1179656 | tf_op jit(solution)/shard_map/ppermute | solution.py:65
  95.4 5.2 %collective-permute-done.22.refs_3_ = bf16[2,64,1536]{2,1,0:T(8,128)(2,1)S(1)} collective-permute-done((bf16[2,64,1536]{2,1,0:T(8,128)(2,1)S(1)}, bf16[2,64,1536]{2,1,0:T(8,128)(2,1)S(1)}, u32[]{:S(2)}, u32[]{:S(2)}) %collective-permute-start.22) | collective-permute-done | bytes 393248 | tf_op jit(solution)/shard_map/ppermute | solution.py:65
  104.4 4.6 %collective-permute-done.28.refs_3_ = bf16[2,64,1536]{2,1,0:T(8,128)(2,1)S(1)} collective-permute-done((bf16[2,64,1536]{2,1,0:T(8,128)(2,1)S(1)}, bf16[2,64,1536]{2,1,0:T(8,128)(2,1)S(1)}, u32[]{:S(2)}, u32[]{:S(2)}) %collective-permute-start.28) | collective-permute-done | bytes 393248 | tf_op jit(solution)/shard_map/ppermute | solution.py:65
  113.0 3.5 %partials.12 = (f32[2,64,1024]{2,1,0:T(8,128)S(1)}, bf16[2,64,1024]{2,1,0:T(8,128)(2,1)S(1)}, f32[2,64,1024]{2,1,0:T(8,128)S(1)}, bf16[2,64,1024]{2,1,0:T(8,128)(2,1)S(1)}) custom-call(bf16[2,32,1024]{2,1,0:T(8,128)(2,1)S(1)} %pad_maximum_fusion.refs_0_, bf16[2,32,1024]{2,1,0:T(8,128)(2,1)S(1)} %collective-permute-done.refs_1_, ...), custom_call_target="tpu_custom_call" | custom-call | tf_op jit(solution)/shard_map/partials/pallas_call | solution.py:142
  119.1 3.7 %grads.8 = (bf16[1024,8192]{1,0:T(8,128)(2,1)}, bf16[1024,8192]{1,0:T(8,128)(2,1)}, f32[1,8192]{1,0:T(1,128)S(1)}) custom-call(bf16[1024,256]{1,0:T(8,128)(2,1)S(1)} %get-tuple-element.80.refs_8_.refs_0_, bf16[1024,256]{1,0:T(8,128)(2,1)S(1)} %get-tuple-element.81.refs_1_, ...), custom_call_target="tpu_custom_call", output_to_operand_aliasing={{0}: (6, {}), {1}: (7, {}), {2}: (8, {})} | custom-call | tf_op jit(solution)/shard_map/grads/pallas_call | solution.py:310
  122.8 3.5 %partials.13 = (f32[2,64,1024]{2,1,0:T(8,128)S(1)}, bf16[2,64,1024]{2,1,0:T(8,128)(2,1)S(1)}, f32[2,64,1024]{2,1,0:T(8,128)S(1)}, bf16[2,64,1024]{2,1,0:T(8,128)(2,1)S(1)}) custom-call(bf16[2,32,1024]{2,1,0:T(8,128)(2,1)S(1)} %pad_maximum_fusion.refs_0_, bf16[2,32,1024]{2,1,0:T(8,128)(2,1)S(1)} %collective-permute-done.refs_1_, ...), custom_call_target="tpu_custom_call" | custom-call | tf_op jit(solution)/shard_map/partials/pallas_call | solution.py:142
  128.5 3.7 %grads.9 = (bf16[1024,8192]{1,0:T(8,128)(2,1)}, bf16[1024,8192]{1,0:T(8,128)(2,1)}, f32[1,8192]{1,0:T(1,128)S(1)}) custom-call(bf16[1024,256]{1,0:T(8,128)(2,1)S(1)} %get-tuple-element.80.refs_8_.refs_0_, bf16[1024,256]{1,0:T(8,128)(2,1)S(1)} %get-tuple-element.81.refs_1_, ...), custom_call_target="tpu_custom_call", output_to_operand_aliasing={{0}: (6, {}), {1}: (7, {}), {2}: (8, {})} | custom-call | tf_op jit(solution)/shard_map/grads/pallas_call | solution.py:310
  134.4 2.7 %collective-permute-done.29.refs_1_ = bf16[2,64,1024]{2,1,0:T(8,128)(2,1)S(1)} collective-permute-done((bf16[2,64,1024]{2,1,0:T(8,128)(2,1)S(1)}, bf16[2,64,1024]{2,1,0:T(8,128)(2,1)S(1)}, u32[]{:S(2)}, u32[]{:S(2)}) %collective-permute-start.29) | collective-permute-done | bytes 262176 | tf_op jit(solution)/shard_map/ppermute | solution.py:65
  137.3 1.6 %collective-permute-start.36 = (bf16[2,64,1024]{2,1,0:T(8,128)(2,1)S(1)}, bf16[2,64,1024]{2,1,0:T(8,128)(2,1)S(1)}, u32[]{:S(2)}, u32[]{:S(2)}) collective-permute-start(bf16[2,64,1024]{2,1,0:T(8,128)(2,1)S(1)} %get-tuple-element.133.refs_2_), channel_id=1, source_target_pairs={{0,16},{8,24},{16,0},{24,8},{1,17},{9,25},{17,1},{25,9},{2,18},{10... | collective-permute-start | bytes 786440 | tf_op jit(solution)/shard_map/ppermute | solution.py:65
  140.0 2.7 %collective-permute-done.38.refs_3_ = bf16[2,64,1024]{2,1,0:T(8,128)(2,1)S(1)} collective-permute-done((bf16[2,64,1024]{2,1,0:T(8,128)(2,1)S(1)}, bf16[2,64,1024]{2,1,0:T(8,128)(2,1)S(1)}, u32[]{:S(2)}, u32[]{:S(2)}) %collective-permute-start.38) | collective-permute-done | bytes 262176 | tf_op jit(solution)/shard_map/ppermute | solution.py:65
  146.1 2.3 %collective-permute-done.36.refs_3_ = bf16[2,64,1024]{2,1,0:T(8,128)(2,1)S(1)} collective-permute-done((bf16[2,64,1024]{2,1,0:T(8,128)(2,1)S(1)}, bf16[2,64,1024]{2,1,0:T(8,128)(2,1)S(1)}, u32[]{:S(2)}, u32[]{:S(2)}) %collective-permute-start.36) | collective-permute-done | bytes 262176 | tf_op jit(solution)/shard_map/ppermute | solution.py:65
  151.7 2.4 %collective-permute-done.42.refs_5_ = bf16[2,64,1024]{2,1,0:T(8,128)(2,1)S(1)} collective-permute-done((bf16[2,64,1024]{2,1,0:T(8,128)(2,1)S(1)}, bf16[2,64,1024]{2,1,0:T(8,128)(2,1)S(1)}, u32[]{:S(2)}, u32[]{:S(2)}) %collective-permute-start.42) | collective-permute-done | bytes 262176 | tf_op jit(solution)/shard_map/ppermute | solution.py:65
  154.2 3.2 %grads.10 = (bf16[1024,8192]{1,0:T(8,128)(2,1)}, bf16[1024,8192]{1,0:T(8,128)(2,1)}, f32[1,8192]{1,0:T(1,128)S(1)}) custom-call(bf16[1024,256]{1,0:T(8,128)(2,1)S(1)} %get-tuple-element.80.refs_8_.refs_0_, bf16[1024,256]{1,0:T(8,128)(2,1)S(1)} %get-tuple-element.81.refs_1_, ...), custom_call_target="tpu_custom_call", output_to_operand_aliasing={{0}: (6, {}), {1}: (7, {}), {2}: (8, {})} | custom-call | tf_op jit(solution)/shard_map/grads/pallas_call | solution.py:310
  158.7 2.7 %grads.11 = (bf16[1024,8192]{1,0:T(8,128)(2,1)}, bf16[1024,8192]{1,0:T(8,128)(2,1)}, f32[1,8192]{1,0:T(1,128)}) custom-call(bf16[1024,256]{1,0:T(8,128)(2,1)S(1)} %get-tuple-element.80.refs_8_.refs_0_, bf16[1024,256]{1,0:T(8,128)(2,1)S(1)} %get-tuple-element.81.refs_1_, ...), custom_call_target="tpu_custom_call", output_to_operand_aliasing={{0}: (6, {}), {1}: (7, {}), {2}: (8, {})} | custom-call | tf_op jit(solution)/shard_map/grads/pallas_call | solution.py:310
  (85 shorter events, 50.9 us)
Async XLA Ops:
  2.0 11.7 %collective-permute-start.3 = (bf16[2,32,1024]{2,1,0:T(8,128)(2,1)S(1)}, bf16[2,32,1024]{2,1,0:T(8,128)(2,1)S(1)}, u32[]{:S(2)}, u32[]{:S(2)}) collective-permute-start(bf16[2,32,1024]{2,1,0:T(8,128)(2,1)S(1)} %pad_maximum_fusion.refs_0_), channel_id=1, source_target_pairs={{0,6},{1,7},{2,4},{3,5},{4,2},{5,3},{6,0},{7,1},{8,14},{9,15},{10,... | collective-permute-start | bytes 393224 | tf_op jit(solution)/shard_map/ppermute | solution.py:69
  6.7 11.7 %collective-permute-start.2 = (bf16[2,32,1024]{2,1,0:T(8,128)(2,1)S(1)}, bf16[2,32,1024]{2,1,0:T(8,128)(2,1)S(1)}, u32[]{:S(2)}, u32[]{:S(2)}) collective-permute-start(bf16[2,32,1024]{2,1,0:T(8,128)(2,1)S(1)} %pad_maximum_fusion.refs_0_), channel_id=1, source_target_pairs={{0,4},{1,5},{2,6},{3,7},{4,0},{5,1},{6,2},{7,3},{8,12},{9,13},{10,... | collective-permute-start | bytes 393224 | tf_op jit(solution)/shard_map/ppermute | solution.py:69
  6.7 11.7 %collective-permute-start.1 = (bf16[2,32,1024]{2,1,0:T(8,128)(2,1)S(1)}, bf16[2,32,1024]{2,1,0:T(8,128)(2,1)S(1)}, u32[]{:S(2)}, u32[]{:S(2)}) collective-permute-start(bf16[2,32,1024]{2,1,0:T(8,128)(2,1)S(1)} %pad_maximum_fusion.refs_0_), channel_id=1, source_target_pairs={{0,2},{1,3},{2,0},{3,1},{4,6},{5,7},{6,4},{7,5},{8,10},{9,11},{10,... | collective-permute-start | bytes 393224 | tf_op jit(solution)/shard_map/ppermute | solution.py:69
  25.3 10.0 %collective-permute-start.9 = (bf16[2,48,1536]{2,1,0:T(8,128)(2,1)S(1)}, bf16[2,48,1536]{2,1,0:T(8,128)(2,1)S(1)}, u32[]{:S(2)}, u32[]{:S(2)}) collective-permute-start(bf16[2,48,1536]{2,1,0:T(8,128)(2,1)S(1)} %get-tuple-element.86), channel_id=1, source_target_pairs={{0,16},{8,24},{16,0},{24,8},{1,17},{9,25},{17,1},{25,9},{2,18},{10... | collective-permute-start | bytes 884744 | tf_op jit(solution)/shard_map/ppermute | solution.py:65
  30.8 10.8 %collective-permute-start.7 = (bf16[2,48,1536]{2,1,0:T(8,128)(2,1)S(1)}, bf16[2,48,1536]{2,1,0:T(8,128)(2,1)S(1)}, u32[]{:S(2)}, u32[]{:S(2)}) collective-permute-start(bf16[2,48,1536]{2,1,0:T(8,128)(2,1)S(1)} %get-tuple-element.82), channel_id=1, source_target_pairs={{0,16},{8,24},{16,0},{24,8},{1,17},{9,25},{17,1},{25,9},{2,18},{10... | collective-permute-start | bytes 884744 | tf_op jit(solution)/shard_map/ppermute | solution.py:65
  31.8 9.9 %collective-permute-start.8 = (bf16[2,48,1536]{2,1,0:T(8,128)(2,1)S(1)}, bf16[2,48,1536]{2,1,0:T(8,128)(2,1)S(1)}, u32[]{:S(2)}, u32[]{:S(2)}) collective-permute-start(bf16[2,48,1536]{2,1,0:T(8,128)(2,1)S(1)} %get-tuple-element.85), channel_id=1, source_target_pairs={{0,8},{8,0},{16,24},{24,16},{1,9},{9,1},{17,25},{25,17},{2,10},{10... | collective-permute-start | bytes 884744 | tf_op jit(solution)/shard_map/ppermute | solution.py:65
  35.8 14.3 %collective-permute-start.14 = (bf16[2,64,1536]{2,1,0:T(8,128)(2,1)S(1)}, bf16[2,64,1536]{2,1,0:T(8,128)(2,1)S(1)}, u32[]{:S(2)}, u32[]{:S(2)}) collective-permute-start(bf16[2,64,1536]{2,1,0:T(8,128)(2,1)S(1)} %get-tuple-element.92.refs_2_), channel_id=1, source_target_pairs={{0,16},{8,24},{16,0},{24,8},{1,17},{9,25},{17,1},{25,9},{2,18},{10... | collective-permute-start | bytes 1179656 | tf_op jit(solution)/shard_map/ppermute | solution.py:65
  37.5 12.7 %collective-permute-start.13 = (bf16[2,64,1536]{2,1,0:T(8,128)(2,1)S(1)}, bf16[2,64,1536]{2,1,0:T(8,128)(2,1)S(1)}, u32[]{:S(2)}, u32[]{:S(2)}) collective-permute-start(bf16[2,64,1536]{2,1,0:T(8,128)(2,1)S(1)} %get-tuple-element.89.refs_8_.refs_0_), channel_id=1, source_target_pairs={{0,8},{8,0},{16,24},{24,16},{1,9},{9,1},{17,25},{25,17},{2,10},{10... | collective-permute-start | bytes 1179656 | tf_op jit(solution)/shard_map/ppermute | solution.py:65
  42.2 16.3 %collective-permute-start.12 = (bf16[2,64,1536]{2,1,0:T(8,128)(2,1)S(1)}, bf16[2,64,1536]{2,1,0:T(8,128)(2,1)S(1)}, u32[]{:S(2)}, u32[]{:S(2)}) collective-permute-start(bf16[2,64,1536]{2,1,0:T(8,128)(2,1)S(1)} %get-tuple-element.91.refs_2_), channel_id=1, source_target_pairs={{0,16},{8,24},{16,0},{24,8},{1,17},{9,25},{17,1},{25,9},{2,18},{10... | collective-permute-start | bytes 1179656 | tf_op jit(solution)/shard_map/ppermute | solution.py:65
  43.8 14.8 %collective-permute-start.11 = (bf16[2,64,1536]{2,1,0:T(8,128)(2,1)S(1)}, bf16[2,64,1536]{2,1,0:T(8,128)(2,1)S(1)}, u32[]{:S(2)}, u32[]{:S(2)}) collective-permute-start(bf16[2,64,1536]{2,1,0:T(8,128)(2,1)S(1)} %get-tuple-element.90.refs_5_.refs_0_), channel_id=1, source_target_pairs={{0,8},{8,0},{16,24},{24,16},{1,9},{9,1},{17,25},{25,17},{2,10},{10... | collective-permute-start | bytes 1179656 | tf_op jit(solution)/shard_map/ppermute | solution.py:65
  51.2 16.2 %collective-permute-start.20 = (bf16[2,64,1536]{2,1,0:T(8,128)(2,1)S(1)}, bf16[2,64,1536]{2,1,0:T(8,128)(2,1)S(1)}, u32[]{:S(2)}, u32[]{:S(2)}) collective-permute-start(bf16[2,64,1536]{2,1,0:T(8,128)(2,1)S(1)} %get-tuple-element.100.refs_4_), channel_id=1, source_target_pairs={{0,8},{8,0},{16,24},{24,16},{1,9},{9,1},{17,25},{25,17},{2,10},{10... | collective-permute-start | bytes 1179656 | tf_op jit(solution)/shard_map/ppermute | solution.py:65
  52.8 15.8 %collective-permute-start.19 = (bf16[2,64,1536]{2,1,0:T(8,128)(2,1)S(1)}, bf16[2,64,1536]{2,1,0:T(8,128)(2,1)S(1)}, u32[]{:S(2)}, u32[]{:S(2)}) collective-permute-start(bf16[2,64,1536]{2,1,0:T(8,128)(2,1)S(1)} %get-tuple-element.93.refs_5_.refs_2_), channel_id=1, source_target_pairs={{0,16},{8,24},{16,0},{24,8},{1,17},{9,25},{17,1},{25,9},{2,18},{10... | collective-permute-start | bytes 1179656 | tf_op jit(solution)/shard_map/ppermute | solution.py:65
  59.6 17.9 %collective-permute-start.18 = (bf16[2,64,1536]{2,1,0:T(8,128)(2,1)S(1)}, bf16[2,64,1536]{2,1,0:T(8,128)(2,1)S(1)}, u32[]{:S(2)}, u32[]{:S(2)}) collective-permute-start(bf16[2,64,1536]{2,1,0:T(8,128)(2,1)S(1)} %get-tuple-element.99.refs_4_), channel_id=1, source_target_pairs={{0,8},{8,0},{16,24},{24,16},{1,9},{9,1},{17,25},{25,17},{2,10},{10... | collective-permute-start | bytes 1179656 | tf_op jit(solution)/shard_map/ppermute | solution.py:65
  61.2 17.4 %collective-permute-start.17 = (bf16[2,64,1536]{2,1,0:T(8,128)(2,1)S(1)}, bf16[2,64,1536]{2,1,0:T(8,128)(2,1)S(1)}, u32[]{:S(2)}, u32[]{:S(2)}) collective-permute-start(bf16[2,64,1536]{2,1,0:T(8,128)(2,1)S(1)} %get-tuple-element.94.refs_6_.refs_2_), channel_id=1, source_target_pairs={{0,16},{8,24},{16,0},{24,8},{1,17},{9,25},{17,1},{25,9},{2,18},{10... | collective-permute-start | bytes 1179656 | tf_op jit(solution)/shard_map/ppermute | solution.py:65
  66.4 17.3 %collective-permute-start.15 = (bf16[2,64,1536]{2,1,0:T(8,128)(2,1)S(1)}, bf16[2,64,1536]{2,1,0:T(8,128)(2,1)S(1)}, u32[]{:S(2)}, u32[]{:S(2)}) collective-permute-start(bf16[2,64,1536]{2,1,0:T(8,128)(2,1)S(1)} %get-tuple-element.96), channel_id=1, source_target_pairs={{0,16},{8,24},{16,0},{24,8},{1,17},{9,25},{17,1},{25,9},{2,18},{10... | collective-permute-start | bytes 1179656 | tf_op jit(solution)/shard_map/ppermute | solution.py:65
  67.4 16.5 %collective-permute-start.16 = (bf16[2,64,1536]{2,1,0:T(8,128)(2,1)S(1)}, bf16[2,64,1536]{2,1,0:T(8,128)(2,1)S(1)}, u32[]{:S(2)}, u32[]{:S(2)}) collective-permute-start(bf16[2,64,1536]{2,1,0:T(8,128)(2,1)S(1)} %get-tuple-element.98), channel_id=1, source_target_pairs={{0,8},{8,0},{16,24},{24,16},{1,9},{9,1},{17,25},{25,17},{2,10},{10... | collective-permute-start | bytes 1179656 | tf_op jit(solution)/shard_map/ppermute | solution.py:65
  76.4 15.8 %collective-permute-start.23 = (bf16[2,64,1536]{2,1,0:T(8,128)(2,1)S(1)}, bf16[2,64,1536]{2,1,0:T(8,128)(2,1)S(1)}, u32[]{:S(2)}, u32[]{:S(2)}) collective-permute-start(bf16[2,64,1536]{2,1,0:T(8,128)(2,1)S(1)} %get-tuple-element.108), channel_id=1, source_target_pairs={{0,16},{8,24},{16,0},{24,8},{1,17},{9,25},{17,1},{25,9},{2,18},{10... | collective-permute-start | bytes 1179656 | tf_op jit(solution)/shard_map/ppermute | solution.py:65
  77.6 14.7 %collective-permute-start.24 = (bf16[2,64,1536]{2,1,0:T(8,128)(2,1)S(1)}, bf16[2,64,1536]{2,1,0:T(8,128)(2,1)S(1)}, u32[]{:S(2)}, u32[]{:S(2)}) collective-permute-start(bf16[2,64,1536]{2,1,0:T(8,128)(2,1)S(1)} %get-tuple-element.110), channel_id=1, source_target_pairs={{0,8},{8,0},{16,24},{24,16},{1,9},{9,1},{17,25},{25,17},{2,10},{10... | collective-permute-start | bytes 1179656 | tf_op jit(solution)/shard_map/ppermute | solution.py:65
  84.3 16.3 %collective-permute-start.22 = (bf16[2,64,1536]{2,1,0:T(8,128)(2,1)S(1)}, bf16[2,64,1536]{2,1,0:T(8,128)(2,1)S(1)}, u32[]{:S(2)}, u32[]{:S(2)}) collective-permute-start(bf16[2,64,1536]{2,1,0:T(8,128)(2,1)S(1)} %get-tuple-element.107.refs_2_), channel_id=1, source_target_pairs={{0,16},{8,24},{16,0},{24,8},{1,17},{9,25},{17,1},{25,9},{2,18},{10... | collective-permute-start | bytes 1179656 | tf_op jit(solution)/shard_map/ppermute | solution.py:65
  85.9 14.8 %collective-permute-start.21 = (bf16[2,64,1536]{2,1,0:T(8,128)(2,1)S(1)}, bf16[2,64,1536]{2,1,0:T(8,128)(2,1)S(1)}, u32[]{:S(2)}, u32[]{:S(2)}) collective-permute-start(bf16[2,64,1536]{2,1,0:T(8,128)(2,1)S(1)} %get-tuple-element.106.refs_4_.refs_0_), channel_id=1, source_target_pairs={{0,8},{8,0},{16,24},{24,16},{1,9},{9,1},{17,25},{25,17},{2,10},{10... | collective-permute-start | bytes 1179656 | tf_op jit(solution)/shard_map/ppermute | solution.py:65
  92.7 16.3 %collective-permute-start.28 = (bf16[2,64,1536]{2,1,0:T(8,128)(2,1)S(1)}, bf16[2,64,1536]{2,1,0:T(8,128)(2,1)S(1)}, u32[]{:S(2)}, u32[]{:S(2)}) collective-permute-start(bf16[2,64,1536]{2,1,0:T(8,128)(2,1)S(1)} %get-tuple-element.116.refs_2_), channel_id=1, source_target_pairs={{0,16},{8,24},{16,0},{24,8},{1,17},{9,25},{17,1},{25,9},{2,18},{10... | collective-permute-start | bytes 1179656 | tf_op jit(solution)/shard_map/ppermute | solution.py:65
  94.4 14.8 %collective-permute-start.27 = (bf16[2,64,1536]{2,1,0:T(8,128)(2,1)S(1)}, bf16[2,64,1536]{2,1,0:T(8,128)(2,1)S(1)}, u32[]{:S(2)}, u32[]{:S(2)}) collective-permute-start(bf16[2,64,1536]{2,1,0:T(8,128)(2,1)S(1)} %get-tuple-element.111.refs_5_.refs_0_), channel_id=1, source_target_pairs={{0,8},{8,0},{16,24},{24,16},{1,9},{9,1},{17,25},{25,17},{2,10},{10... | collective-permute-start | bytes 1179656 | tf_op jit(solution)/shard_map/ppermute | solution.py:65
  101.8 15.8 %collective-permute-start.26 = (bf16[2,64,1536]{2,1,0:T(8,128)(2,1)S(1)}, bf16[2,64,1536]{2,1,0:T(8,128)(2,1)S(1)}, u32[]{:S(2)}, u32[]{:S(2)}) collective-permute-start(bf16[2,64,1536]{2,1,0:T(8,128)(2,1)S(1)} %get-tuple-element.113.refs_4_), channel_id=1, source_target_pairs={{0,8},{8,0},{16,24},{24,16},{1,9},{9,1},{17,25},{25,17},{2,10},{10... | collective-permute-start | bytes 1179656 | tf_op jit(solution)/shard_map/ppermute | solution.py:65
  103.3 15.8 %collective-permute-start.25 = (bf16[2,64,1536]{2,1,0:T(8,128)(2,1)S(1)}, bf16[2,64,1536]{2,1,0:T(8,128)(2,1)S(1)}, u32[]{:S(2)}, u32[]{:S(2)}) collective-permute-start(bf16[2,64,1536]{2,1,0:T(8,128)(2,1)S(1)} %get-tuple-element.112.refs_5_.refs_2_), channel_id=1, source_target_pairs={{0,16},{8,24},{16,0},{24,8},{1,17},{9,25},{17,1},{25,9},{2,18},{10... | collective-permute-start | bytes 1179656 | tf_op jit(solution)/shard_map/ppermute | solution.py:65
  110.4 17.1 %collective-permute-start.34 = (bf16[2,64,1536]{2,1,0:T(8,128)(2,1)S(1)}, bf16[2,64,1536]{2,1,0:T(8,128)(2,1)S(1)}, u32[]{:S(2)}, u32[]{:S(2)}) collective-permute-start(bf16[2,64,1536]{2,1,0:T(8,128)(2,1)S(1)} %get-tuple-element.127.refs_4_), channel_id=1, source_target_pairs={{0,8},{8,0},{16,24},{24,16},{1,9},{9,1},{17,25},{25,17},{2,10},{10... | collective-permute-start | bytes 1179656 | tf_op jit(solution)/shard_map/ppermute | solution.py:65
  111.9 16.6 %collective-permute-start.33 = (bf16[2,64,1536]{2,1,0:T(8,128)(2,1)S(1)}, bf16[2,64,1536]{2,1,0:T(8,128)(2,1)S(1)}, u32[]{:S(2)}, u32[]{:S(2)}) collective-permute-start(bf16[2,64,1536]{2,1,0:T(8,128)(2,1)S(1)} %get-tuple-element.117.refs_6_.refs_2_), channel_id=1, source_target_pairs={{0,16},{8,24},{16,0},{24,8},{1,17},{9,25},{17,1},{25,9},{2,18},{10... | collective-permute-start | bytes 1179656 | tf_op jit(solution)/shard_map/ppermute | solution.py:65
  116.6 15.7 %collective-permute-start.31 = (bf16[2,64,1024]{2,1,0:T(8,128)(2,1)S(1)}, bf16[2,64,1024]{2,1,0:T(8,128)(2,1)S(1)}, u32[]{:S(2)}, u32[]{:S(2)}) collective-permute-start(bf16[2,64,1024]{2,1,0:T(8,128)(2,1)S(1)} %get-tuple-element.124), channel_id=1, source_target_pairs={{0,16},{8,24},{16,0},{24,8},{1,17},{9,25},{17,1},{25,9},{2,18},{10... | collective-permute-start | bytes 786440 | tf_op jit(solution)/shard_map/ppermute | solution.py:65
  117.6 14.7 %collective-permute-start.32 = (bf16[2,64,1024]{2,1,0:T(8,128)(2,1)S(1)}, bf16[2,64,1024]{2,1,0:T(8,128)(2,1)S(1)}, u32[]{:S(2)}, u32[]{:S(2)}) collective-permute-start(bf16[2,64,1024]{2,1,0:T(8,128)(2,1)S(1)} %get-tuple-element.126), channel_id=1, source_target_pairs={{0,8},{8,0},{16,24},{24,16},{1,9},{9,1},{17,25},{25,17},{2,10},{10... | collective-permute-start | bytes 786440 | tf_op jit(solution)/shard_map/ppermute | solution.py:65
  126.3 10.8 %collective-permute-start.29 = (bf16[2,64,1024]{2,1,0:T(8,128)(2,1)S(1)}, bf16[2,64,1024]{2,1,0:T(8,128)(2,1)S(1)}, u32[]{:S(2)}, u32[]{:S(2)}) collective-permute-start(bf16[2,64,1024]{2,1,0:T(8,128)(2,1)S(1)} %get-tuple-element.121), channel_id=1, source_target_pairs={{0,16},{8,24},{16,0},{24,8},{1,17},{9,25},{17,1},{25,9},{2,18},{10... | collective-permute-start | bytes 786440 | tf_op jit(solution)/shard_map/ppermute | solution.py:65
  132.4 10.4 %collective-permute-start.38 = (bf16[2,64,1024]{2,1,0:T(8,128)(2,1)S(1)}, bf16[2,64,1024]{2,1,0:T(8,128)(2,1)S(1)}, u32[]{:S(2)}, u32[]{:S(2)}) collective-permute-start(bf16[2,64,1024]{2,1,0:T(8,128)(2,1)S(1)} %get-tuple-element.134.refs_2_), channel_id=1, source_target_pairs={{0,16},{8,24},{16,0},{24,8},{1,17},{9,25},{17,1},{25,9},{2,18},{10... | collective-permute-start | bytes 786440 | tf_op jit(solution)/shard_map/ppermute | solution.py:65
  137.3 11.0 %collective-permute-start.36 = (bf16[2,64,1024]{2,1,0:T(8,128)(2,1)S(1)}, bf16[2,64,1024]{2,1,0:T(8,128)(2,1)S(1)}, u32[]{:S(2)}, u32[]{:S(2)}) collective-permute-start(bf16[2,64,1024]{2,1,0:T(8,128)(2,1)S(1)} %get-tuple-element.133.refs_2_), channel_id=1, source_target_pairs={{0,16},{8,24},{16,0},{24,8},{1,17},{9,25},{17,1},{25,9},{2,18},{10... | collective-permute-start | bytes 786440 | tf_op jit(solution)/shard_map/ppermute | solution.py:65
  143.4 10.7 %collective-permute-start.42 = (bf16[2,64,1024]{2,1,0:T(8,128)(2,1)S(1)}, bf16[2,64,1024]{2,1,0:T(8,128)(2,1)S(1)}, u32[]{:S(2)}, u32[]{:S(2)}) collective-permute-start(bf16[2,64,1024]{2,1,0:T(8,128)(2,1)S(1)} %get-tuple-element.138.refs_4_), channel_id=1, source_target_pairs={{0,8},{8,0},{16,24},{24,16},{1,9},{9,1},{17,25},{25,17},{2,10},{10... | collective-permute-start | bytes 786440 | tf_op jit(solution)/shard_map/ppermute | solution.py:65
  (12 other events, 112.8 us)
